TPU v7x, 32 devices: a whole 2x2x4 slice. The times are simulated.
32 devices in a mesh: groups: 1, lat: 16 (over z, y, x), ckpt: 2 (over core).
Axes of the slice: x: 2, y: 2, z: 4, core: 2. Of those that a mesh axis runs over, the one named last changes fastest.
Arguments:
- inputs: bfloat16 [2, 512, 4096], P('ckpt', ('groups', 'lat')), may hold values from -6 to 6
- enc_weight: bfloat16 [2, 4096, 32768], P('ckpt', None, 'lat'), may hold values from -0.0625 to 0.0625
- enc_bias: float32 [32768], P('lat'), may hold values from -3 to 3
- dec_weight: bfloat16 [2, 4096, 32768], P('ckpt', 'lat'), may hold values from -0.375 to 0.375
- dec_bias: float32 [2, 4096], P('ckpt', 'lat'), may hold values from -3 to 3
- block_ids: int32 [4, 16], P('groups'), may hold values from 0 to 31
- live: int32 [4, 16], P('groups'), may hold values 0 or 1
Outputs:
- recon: bfloat16 [2, 4096, 512], P('ckpt', 'lat', 'groups')
Inputs may be any that keep to these rules, and one draw needn't show every extreme that they name: block_ids numbers a block among the 32 blocks of its owner; it matters only where live is 1. live is the count of active blocks of an owner in a tile.
All inputs are finite; a program needn't handle non-finite values.
Results may differ from a plain program's by a relative error of at most 0.0047.
Values may be sent and summed in bfloat16 or wider, within the bound.
No kernel may reach another device: no remote copies, remote signals or barrier semaphores. Data moves between devices by JAX's collectives and lax.ppermute only.
A program may use at most 128 MiB of HBM per device.

v0:
```python
import jax
import jax.numpy as jnp
from jax import lax
from jax.sharding import PartitionSpec as P

BLOCK = 64
TILE = 128


def body(inputs, enc_weight, enc_bias, dec_weight, dec_bias, block_ids, live):
    lat_count = lax.axis_size("lat")
    lat_index = lax.axis_index("lat")
    lat_dev = enc_weight.shape[2]
    own_blocks = lat_dev // BLOCK
    local_ckpts = dec_weight.shape[0]
    features = dec_weight.shape[1]
    preact = jnp.einsum(
        "cdl,crd->lr",
        enc_weight,
        lax.all_gather(inputs, "lat", axis=1, tiled=True),
        preferred_element_type=jnp.float32,
    )
    token_count = preact.shape[1]
    tiles = token_count // TILE
    own_ids = lax.dynamic_slice_in_dim(block_ids, lat_index, 1, 1)[:, 0]
    own_live = lax.dynamic_slice_in_dim(live, lat_index, 1, 1)[:, 0]
    choose = (
        (own_ids[:, None] == jnp.arange(own_blocks, dtype=jnp.int32)[None, :])
        & (own_live[:, None] == 1)
    ).astype(jnp.float32)
    choose_cols = jnp.transpose(choose)
    summed = lax.psum(preact, "ckpt")
    shifted = jnp.maximum(summed.reshape(lat_dev, tiles, TILE) + enc_bias[:, None, None], 0.0)
    grouped_vals = shifted.reshape(own_blocks, BLOCK, tiles, TILE)
    picked = jnp.sum(grouped_vals * choose_cols[:, None, :, None], axis=0)
    acts = jnp.transpose(picked, (1, 0, 2)).astype(jnp.bfloat16)
    onehot = (
        (block_ids[:, :, None] == jnp.arange(own_blocks, dtype=jnp.int32)[None, None, :])
        & (live[:, :, None] == 1)
    ).astype(jnp.bfloat16)
    grouped = dec_weight.reshape(local_ckpts, features, lat_count, own_blocks, BLOCK)
    selected = jnp.einsum(
        "tnp,cdnpe->cdtne", onehot, grouped, preferred_element_type=jnp.float32
    ).astype(jnp.bfloat16)
    total = jnp.einsum(
        "ntes,cdtne->cdts",
        lax.all_gather(acts[None], "lat", axis=0, tiled=True),
        selected,
        preferred_element_type=jnp.float32,
    )
    recon = total.reshape(local_ckpts, features, token_count)
    return (recon + dec_bias[:, :, None]).astype(jnp.bfloat16)


def solution(mesh):
    placed = (
        P("ckpt", ("groups", "lat"), None),
        P("ckpt", None, "lat"),
        P("lat"),
        P("ckpt", "lat", None),
        P("ckpt", "lat"),
        P("groups", None),
        P("groups", None),
    )
    return jax.shard_map(
        body, mesh=mesh, in_specs=placed, out_specs=P("ckpt", "lat", "groups"), check_vma=False
    )
```

profile of v0, /device:TPU:0, one launch (start us, length us, event | category | flops | bytes accessed | tf_op | source)
XLA Modules:
  0.0 207.5 jit_solution(4583635202906915458)
XLA Ops:
  6.5 0.0 all-gather.4.cloned.1.call-start
  6.5 0.7 all-gather.4.cloned.1.call-update
  7.3 0.0 all-reduce.2.cloned.1.call-start
  7.3 81.6 %all-gather.4.cloned.1.call-done = bf16[1,512,4096]{2,1,0:T(8,128)(2,1)} async-done(((bf16[1,32,4096]{2,1,0:T(8,128)(2,1)}), bf16[1,512,4096]{2,1,0:T(8,128)(2,1)}) %all-gather.4.cloned.1.call-update) | async-done | bytes 4194320 | tf_op jit(solution)/shard_map/all_gather | solution.py:20
  88.9 15.0 %fusion = f32[2048,512]{1,0:T(8,128)} fusion(bf16[1,4096,2048]{2,1,0:T(8,128)(2,1)} %param.8, bf16[1,512,4096]{2,1,0:T(8,128)(2,1)} %all-gather.4.cloned.1.call-done), kind=kOutput, calls=%fused_computation | convolution fusion | flops 8589934592 | bytes 25165824 | tf_op jit(solution)/shard_map/cdl,crd->lr/dot_general | solution.py:17
  103.9 5.2 %reshape.111 = f32[32,64,4,128]{3,2,1,0:T(4,128)} reshape(f32[2048,512]{1,0:T(8,128)} %fusion) | data formatting | bytes 8388608 | tf_op jit(solution)/shard_map/reshape | solution.py:33
  109.1 0.0 copy-start
  109.1 0.0 copy-start.1
  109.1 0.0 copy-start.2
  109.2 0.0 all-reduce.2.cloned.1.call-update
  109.2 0.2 all-gather.6.cloned.1.call-start
  109.4 0.4 copy-done
  109.8 0.1 add.33
  109.9 0.0 copy-done.1
  109.9 0.2 dynamic-slice_reduce_fusion
  110.1 0.0 copy-done.2
  110.1 0.2 fusion.17
  110.3 26.1 %all-reduce.2.cloned.1.call-done = f32[32,64,4,128]{3,2,1,0:T(4,128)} async-done(((f32[32,64,4,128]{3,2,1,0:T(4,128)}), f32[32,64,4,128]{3,2,1,0:T(4,128)}) %all-reduce.2.cloned.1.call-update) | async-done | bytes 4194320 | tf_op jit(solution)/shard_map/psum | solution.py:32
  136.4 4.4 %multiply_reduce_fusion = bf16[64,4,128]{2,1,0:T(4,128)(2,1)S(1)} fusion(f32[32,64,4,128]{3,2,1,0:T(4,128)} %all-reduce.2.cloned.1.call-done, f32[32,4]{1,0:T(8,128)S(1)} %fusion.15, f32[32,64]{1,0:T(8,128)S(1)} %add.33), kind=kLoop, calls=%fused_computation.5 | loop fusion | flops 4161536 | bytes 4268544 | tf_op jit(solution)/shard_map/reduce_sum | solution.py:35
  140.8 0.6 copy.24
  141.5 0.0 all-gather.6.cloned.1.call-update
  141.5 0.1 copy.20
  141.6 22.4 %copy.22 = bf16[1,256,32768]{1,2,0:T(8,128)(2,1)} copy(bf16[1,256,32768]{2,1,0:T(8,128)(2,1)} %param.10) | data formatting | bytes 33554432 | tf_op args[3]
  164.0 0.1 copy.21
  164.1 15.3 %convert_bitcast_fusion = bf16[256,4,16,64]{0,1,3,2:T(4,128)(2,1)S(1)} fusion(bf16[256,16,32,64]{0,3,2,1:T(8,128)(2,1)} %bitcast.32, s32[4,16]{0,1:T(8,128)S(1)} %copy.20, pred[4,16]{0,1:T(8,128)(4,1)S(1)} %copy.21), kind=kOutput, calls=%fused_computation.8 | convolution fusion | flops 68161536 | bytes 18874688 | tf_op jit(solution)/shard_map/tnp,cdnpe->cdtne/dot_general | solution.py:42
  179.4 0.0 copy-start.3
  179.4 18.7 %all-gather.6.cloned.1.call-done = bf16[64,64,128]{2,1,0:T(8,128)(2,1)} async-done(((bf16[4,64,128]{2,1,0:T(8,128)(2,1)}), bf16[64,64,128]{2,1,0:T(8,128)(2,1)}) %all-gather.6.cloned.1.call-update) | async-done | bytes 1048592 | tf_op jit(solution)/shard_map/all_gather | solution.py:47
  198.1 1.8 fusion.5
  199.9 0.2 copy.27
  200.1 0.0 copy-done.3
  200.1 0.8 add_convert_fusion
  (2 shorter events, 0.0 us)
Async XLA Ops:
  6.5 82.4 %all-gather.4.cloned.1.call-start = ((), (), s32[]{:S(2)}) async-start(), calls=%async_computation | async-start | bytes 4456448 | tf_op jit(solution)/shard_map/all_gather | solution.py:20
  7.3 129.1 %all-reduce.2.cloned.1.call-start = ((), (), s32[]{:S(2)}) async-start(), calls=%async_computation.1 | async-start | bytes 8388608 | tf_op jit(solution)/shard_map/psum | solution.py:32
  109.1 0.7 copy-start
  109.1 0.8 copy-start.1
  109.1 1.0 copy-start.2
  109.2 88.9 %all-gather.6.cloned.1.call-start = ((), (), s32[]{:S(2)}) async-start(), calls=%async_computation.2 | async-start | bytes 1114112 | tf_op jit(solution)/shard_map/all_gather | solution.py:47
  179.4 20.7 %copy-start.3 = (f32[1,256]{1,0:T(1,128)S(1)}, f32[1,256]{1,0:T(1,128)}, u32[]{:S(2)}) copy-start(f32[1,256]{1,0:T(1,128)} %param.11) | copy-start | bytes 3076
Sparse Core Ops, SparseCore 0:
  10.1 78.7 all-gather.3
  109.3 27.0 all-reduce.1
  141.6 56.4 all-gather.5
where the time goes:
time: 208 us; the launch traced here: 207 us
  waiting for transfers between devices  127 us (61%)
  matrix products  32.1 us (15%)
  local copies, waits for them, and re-layouts  29.3 us (14%)
  between operations  13.2 us (6%)
  other arithmetic  5.46 us (3%)
    all_gather x1, waiting for transfers between devices, body(): lax.all_gather(inputs, 'lat', axis=1, tiled=True)  81.6 us
    psum x1, waiting for transfers between devices, body(): summed = lax.psum(preact, 'ckpt')  26.1 us
    unnamed x10, local copies, waits for them, and re-layouts  22.9 us
    all_gather x1, waiting for transfers between devices, body(): lax.all_gather(acts[None], 'lat', axis=0, tiled=True)  18.7 us
    dot_general x1, matrix products, body(): jnp.einsum('tnp,cdnpe->cdtne', onehot, grouped, preferred_element_type=jn...  15.3 us
    dot_general x1, matrix products, body(): jnp.einsum('cdl,crd->lr', enc_weight, lax.all_gather(inputs, 'lat', axis=...  15 us
    reshape x1, local copies, waits for them, and re-layouts, body(): summed.reshape(lat_dev, tiles, TILE) + enc_bias[:, None, None]  5.24 us
    reduce_sum x1, other arithmetic, body(): picked = jnp.sum(grouped_vals * choose_cols[:, None, :, None], axis=0)  4.45 us
  transfers between devices with their start and end apart: 3, of which 3 were waited for; matrix products, arithmetic and copies ran while one was open for 18% of the time, Pallas kernels for 0%

commit v1 on v0

v1 whole, which is shorter than its diff:
```python
import functools

import jax
import jax.numpy as jnp
from jax import lax
from jax.experimental import pallas as pl
from jax.experimental.pallas import tpu as pltpu
from jax.sharding import PartitionSpec as P

BLOCK = 64
TILE = 128
PAIR = 2 * BLOCK
F32 = jnp.float32
BF16 = jnp.bfloat16
VMEM_BYTES = 24 * 1024 * 1024
VMEM_WEIGHTS = 52 * 1024 * 1024


def body_any(inputs, enc_weight, enc_bias, dec_weight, dec_bias, block_ids, live):
    lat_count = lax.axis_size("lat")
    lat_index = lax.axis_index("lat")
    lat_dev = enc_weight.shape[2]
    own_blocks = lat_dev // BLOCK
    local_ckpts = dec_weight.shape[0]
    features = dec_weight.shape[1]
    preact = jnp.einsum(
        "cdl,crd->lr",
        enc_weight,
        lax.all_gather(inputs, "lat", axis=1, tiled=True),
        preferred_element_type=F32,
    )
    token_count = preact.shape[1]
    tiles = token_count // TILE
    own_ids = lax.dynamic_slice_in_dim(block_ids, lat_index, 1, 1)[:, 0]
    own_live = lax.dynamic_slice_in_dim(live, lat_index, 1, 1)[:, 0]
    choose = (own_ids[:, None] == jnp.arange(own_blocks, dtype=jnp.int32)[None, :]) & (own_live[:, None] == 1)
    choose_cols = jnp.transpose(choose.astype(F32))
    grouped_vals = preact.reshape(own_blocks, BLOCK, tiles, TILE)
    picked = jnp.sum(grouped_vals * choose_cols[:, None, :, None], axis=0)
    picked_bias = jnp.einsum("pe,pt->et", enc_bias.reshape(own_blocks, BLOCK), choose_cols, precision=lax.Precision.HIGHEST)
    summed = lax.psum(picked, "ckpt") + picked_bias[:, :, None]
    acts = jnp.transpose(jnp.maximum(summed, 0.0), (1, 0, 2)).astype(BF16)
    onehot = (
        (block_ids[:, :, None] == jnp.arange(own_blocks, dtype=jnp.int32)[None, None, :]) & (live[:, :, None] == 1)
    ).astype(BF16)
    grouped = dec_weight.reshape(local_ckpts, features, lat_count, own_blocks, BLOCK)
    selected = jnp.einsum("tnp,cdnpe->cdtne", onehot, grouped, preferred_element_type=F32).astype(BF16)
    total = jnp.einsum(
        "ntes,cdtne->cdts",
        lax.all_gather(acts[None], "lat", axis=0, tiled=True),
        selected,
        preferred_element_type=F32,
    )
    recon = total.reshape(local_ckpts, features, token_count)
    return (recon + dec_bias[:, :, None]).astype(BF16)


def block_at(ids_ref, tile, owner, owners):
    return ids_ref[tile * owners + owner]


def swap_halves(values):
    return pltpu.roll(values.astype(F32), BLOCK, 1).astype(BF16)


def send_columns_kernel(ids_ref, at_ref, first_ref, second_ref, out_ref, *, owners):
    lat = at_ref[0]
    plane = lat // 4
    lane = lax.broadcasted_iota(jnp.int32, (first_ref.shape[0], PAIR), 1)
    odd_first = block_at(ids_ref, plane ^ 1, lat, owners) % 2
    odd_second = block_at(ids_ref, plane ^ 3, lat, owners) % 2
    first = first_ref[...].astype(F32)
    second = second_ref[...].astype(F32)
    first = jnp.where(odd_first == 1, pltpu.roll(first, BLOCK, 1), first)
    second = jnp.where(odd_second == 0, pltpu.roll(second, BLOCK, 1), second)
    out_ref[...] = jnp.where(lane < BLOCK, first, second).astype(BF16)


def send_columns(ids, at, enc_weight, owners):
    depth = enc_weight.shape[0]
    step = 1024

    def pick(mask):
        def index(i, ids_ref, at_ref):
            lat = at_ref[0]
            return i, block_at(ids_ref, (lat // 4) ^ mask, lat, owners) // 2

        return index

    return pl.pallas_call(
        functools.partial(send_columns_kernel, owners=owners),
        out_shape=jax.ShapeDtypeStruct((depth, PAIR), BF16),
        grid_spec=pltpu.PrefetchScalarGridSpec(
            num_scalar_prefetch=2,
            grid=(depth // step,),
            in_specs=[pl.BlockSpec((step, PAIR), pick(1)), pl.BlockSpec((step, PAIR), pick(3))],
            out_specs=pl.BlockSpec((step, PAIR), lambda i, ids_ref, at_ref: (i, 0)),
        ),
        compiler_params=pltpu.CompilerParams(vmem_limit_bytes=VMEM_WEIGHTS),
        cost_estimate=pl.CostEstimate(flops=0, bytes_accessed=3 * depth * PAIR * 2, transcendentals=0),
        name="send_columns",
    )(ids, at, enc_weight, enc_weight)


def encode_kernel(ids_ref, live_ref, at_ref, *refs, owners):
    near = refs[0:4]
    far = refs[4:8]
    near_w, far_w, partner_w, bias_ref, out_ref, acc_ref, turn_ref = refs[8:]
    step = pl.program_id(0)

    @pl.when(step == 0)
    def _():
        acc_ref[...] = jnp.zeros_like(acc_ref)

    for index, (tokens, own_w) in enumerate(((near, near_w), (far, far_w))):
        rows = jnp.concatenate([ref[...] for ref in tokens], axis=0)
        columns = jnp.concatenate([own_w[...], partner_w[...]], axis=1)
        acc_ref[index] += jnp.dot(rows, columns, preferred_element_type=F32)

    @pl.when(step == pl.num_programs(0) - 1)
    def _():
        lat = at_ref[0]
        plane, place = lat // 4, lat % 4
        shard = TILE // 4
        for index in range(2):
            tile = plane ^ (2 * index)
            for turn in range(4):
                turn_ref[pl.ds(pl.multiple_of((place ^ turn) * shard, shard), shard), :] = acc_ref[
                    index, turn * shard : (turn + 1) * shard, :
                ]
            acc_ref[index, :PAIR, :PAIR] = jnp.transpose(turn_ref[:, :PAIR])
            acc_ref[index, :PAIR, PAIR:] = jnp.transpose(turn_ref[:, PAIR:])
            odd = block_at(ids_ref, tile, lat, owners) % 2
            own = acc_ref[index, pl.ds(pl.multiple_of(odd * BLOCK, BLOCK), BLOCK), :PAIR]
            other = acc_ref[index, index * BLOCK : (index + 1) * BLOCK, PAIR:]
            own_live = live_ref[tile * owners + lat] == 1
            other_live = live_ref[tile * owners + (lat ^ 4)] == 1
            out_ref[index] = jnp.where(own_live, own + bias_ref[index], 0.0)
            out_ref[2 + index] = jnp.where(other_live, other + bias_ref[2 + index], 0.0)


def encode(ids, live, at, near, far, enc_weight, partner, bias, owners):
    depth = enc_weight.shape[0]
    step = 1024
    shard = near[0].shape[0]

    def pick(mask):
        def index(i, ids_ref, live_ref, at_ref):
            lat = at_ref[0]
            return i, block_at(ids_ref, (lat // 4) ^ mask, lat, owners) // 2

        return index

    tokens = pl.BlockSpec((shard, step), lambda i, *_: (0, i))
    whole = pl.BlockSpec((4, BLOCK, TILE), lambda i, *_: (0, 0, 0))
    return pl.pallas_call(
        functools.partial(encode_kernel, owners=owners),
        out_shape=jax.ShapeDtypeStruct((4, BLOCK, TILE), F32),
        grid_spec=pltpu.PrefetchScalarGridSpec(
            num_scalar_prefetch=3,
            grid=(depth // step,),
            in_specs=[tokens] * 8
            + [
                pl.BlockSpec((step, PAIR), pick(0)),
                pl.BlockSpec((step, PAIR), pick(2)),
                pl.BlockSpec((step, PAIR), lambda i, *_: (i, 0)),
                whole,
            ],
            out_specs=whole,
            scratch_shapes=[pltpu.VMEM((2, TILE, 2 * PAIR), F32), pltpu.VMEM((TILE, 2 * PAIR), F32)],
        ),
        compiler_params=pltpu.CompilerParams(vmem_limit_bytes=VMEM_WEIGHTS),
        cost_estimate=pl.CostEstimate(flops=4 * TILE * depth * 2 * PAIR, bytes_accessed=5 * 2**20, transcendentals=0),
        name="encode",
    )(ids, live, at, *near, *far, enc_weight, enc_weight, partner, bias)


def stage_decoder_kernel(ids_ref, *refs):
    for owner, ref in enumerate(refs[:-1]):
        refs[-1][0, :, owner * PAIR : (owner + 1) * PAIR] = ref[...]


def stage_decoder(ids, dec_weight, owners, tiles):
    features = dec_weight.shape[0]
    per_owner = dec_weight.shape[1] // owners // PAIR

    def pick(owner):
        return lambda t, ids_ref: (0, owner * per_owner + block_at(ids_ref, t, owner, owners) // 2)

    return pl.pallas_call(
        stage_decoder_kernel,
        out_shape=jax.ShapeDtypeStruct((tiles, features, owners * PAIR), BF16),
        grid_spec=pltpu.PrefetchScalarGridSpec(
            num_scalar_prefetch=1,
            grid=(tiles,),
            in_specs=[pl.BlockSpec((features, PAIR), pick(owner)) for owner in range(owners)],
            out_specs=pl.BlockSpec((1, features, owners * PAIR), lambda t, ids_ref: (t, 0, 0)),
        ),
        compiler_params=pltpu.CompilerParams(vmem_limit_bytes=VMEM_WEIGHTS),
        cost_estimate=pl.CostEstimate(
            flops=0, bytes_accessed=2 * tiles * features * owners * PAIR * 2, transcendentals=0
        ),
        name="stage_decoder",
    )(ids, *([dec_weight] * owners))


def decode_kernel(ids_ref, at_ref, *refs, owners):
    mine = refs[0:4]
    theirs = refs[4:8]
    columns_ref, bias_ref, out_ref, acts_ref = refs[8:]
    tile_now = pl.program_id(0)

    @pl.when(tile_now == 0)
    def _():
        lat, core = at_ref[0], at_ref[1]
        for place in range(4):
            for ref, holder in ((mine[place], core), (theirs[place], 1 - core)):
                slots = ((0, holder), (4 + 8 * holder, 0), (4 + 8 * holder, 1), (8, holder))
                for slot, (mask, which) in enumerate(slots):
                    source = lat ^ place ^ mask
                    owner = source ^ (4 * which)
                    for index in range(2):
                        tile = (source // 4) ^ (2 * index)
                        odd = block_at(ids_ref, tile, owner, owners) % 2
                        values = ref[slot, index]
                        zeros = jnp.zeros_like(values)
                        row = pl.multiple_of((tile * owners + owner) * PAIR, PAIR)
                        acts_ref[pl.ds(row, PAIR), :] = jnp.concatenate(
                            [jnp.where(odd == 0, values, zeros), jnp.where(odd == 1, values, zeros)], axis=0
                        )

    rows = owners * PAIR
    acts = acts_ref[pl.ds(pl.multiple_of(tile_now * rows, rows), rows), :]
    total = jnp.dot(columns_ref[0], acts, preferred_element_type=F32)
    out_ref[...] = (total + bias_ref[...]).astype(BF16)


def decode(ids, at, mine, theirs, columns, dec_bias, owners):
    tiles, features, depth = columns.shape
    payload = pl.BlockSpec(mine[0].shape, lambda t, *_: (0, 0, 0, 0))
    return pl.pallas_call(
        functools.partial(decode_kernel, owners=owners),
        out_shape=jax.ShapeDtypeStruct((features, tiles * TILE), BF16),
        grid_spec=pltpu.PrefetchScalarGridSpec(
            num_scalar_prefetch=2,
            grid=(tiles,),
            in_specs=[payload] * 8
            + [
                pl.BlockSpec((1, features, depth), lambda t, *_: (t, 0, 0)),
                pl.BlockSpec((features, 1), lambda t, *_: (0, 0)),
            ],
            out_specs=pl.BlockSpec((features, TILE), lambda t, *_: (0, t)),
            scratch_shapes=[pltpu.VMEM((tiles * depth, TILE), BF16)],
        ),
        compiler_params=pltpu.CompilerParams(vmem_limit_bytes=VMEM_BYTES),
        cost_estimate=pl.CostEstimate(
            flops=2 * tiles * features * depth * TILE, bytes_accessed=6 * 2**20, transcendentals=0
        ),
        name="decode",
    )(ids, at, *mine, *theirs, columns, dec_bias)


def body_planes(inputs, enc_weight, enc_bias, dec_weight, dec_bias, block_ids, live):
    owners = lax.axis_size("lat")
    lat = lax.axis_index("lat")
    core = lax.axis_index("ckpt")
    tiles = block_ids.shape[0]
    own_blocks = enc_weight.shape[2] // BLOCK
    at = jnp.stack([lat, core]).astype(jnp.int32)
    ids = block_ids.reshape(-1)
    alive = live.reshape(-1)

    def swap(values, mask):
        return lax.ppermute(values, "lat", [(i, i ^ mask) for i in range(owners)])

    def across(values):
        return lax.ppermute(values, "ckpt", [(0, 1), (1, 0)])

    near_own = inputs[0]
    far_own = swap(near_own, 8)
    near = [near_own] + [swap(near_own, place) for place in range(1, 4)]
    partner_bias = swap(enc_bias, 4)
    partner = swap(send_columns(ids, at, enc_weight[0], owners), 4)
    far = [far_own] + [swap(far_own, place) for place in range(1, 4)]

    plane = lat // 4
    rows = []
    for whose, values in ((lat, enc_bias), (lat ^ 4, partner_bias)):
        for index in range(2):
            block = lax.dynamic_slice(block_ids, (plane ^ (2 * index), whose), (1, 1))[0, 0]
            rows.append(lax.dynamic_slice(values, (block * BLOCK,), (BLOCK,)))
    bias = jnp.where(core == 0, jnp.stack(rows), 0.0)
    bias = jnp.broadcast_to(bias[:, :, None], (4, BLOCK, TILE))

    columns = stage_decoder(ids, dec_weight[0], owners, tiles)
    ids_encode, columns = lax.optimization_barrier((ids, columns))
    partial = encode(ids_encode, alive, at, near, far, enc_weight[0], partner, bias, owners)
    acts = jnp.maximum(partial + across(partial), 0.0).astype(BF16).reshape(2, 2, BLOCK, TILE)

    ends = [(2 * i, 2 * (i ^ 4)) for i in range(owners)] + [(2 * i + 1, 2 * (i ^ 12) + 1) for i in range(owners)]
    along = lax.ppermute(acts, ("lat", "ckpt"), ends)
    middle = swap(acts, 8)

    def half(values):
        return lax.dynamic_slice_in_dim(values, core, 1, 0)

    payload = jnp.concatenate([half(acts), along, half(middle)], axis=0)
    mine = [payload] + [swap(payload, place) for place in range(1, 4)]
    theirs = [across(values) for values in mine]
    recon = decode(ids, at, mine, theirs, columns, dec_bias.reshape(-1, 1), owners)
    return recon[None]


def body(inputs, enc_weight, enc_bias, dec_weight, dec_bias, block_ids, live):
    tiles, owners = block_ids.shape
    cores = lax.axis_size("ckpt")
    if owners == 16 and cores == 2 and tiles == 4 and inputs.shape[:2] == (1, tiles * TILE // owners):
        return body_planes(inputs, enc_weight, enc_bias, dec_weight, dec_bias, block_ids, live)
    return body_any(inputs, enc_weight, enc_bias, dec_weight, dec_bias, block_ids, live)


def solution(mesh):
    placed = (
        P("ckpt", ("groups", "lat"), None),
        P("ckpt", None, "lat"),
        P("lat"),
        P("ckpt", "lat", None),
        P("ckpt", "lat"),
        P("groups", None),
        P("groups", None),
    )
    return jax.shard_map(
        body, mesh=mesh, in_specs=placed, out_specs=P("ckpt", "lat", "groups"), check_vma=False
    )
```

time: 208 us -> 88.5 us (0.43)
  waiting for transfers between devices: 127 us -> 38.6 us
  matrix products: 32.1 us -> 0 us
  local copies, waits for them, and re-layouts: 29.3 us -> 4.7 us
  starting transfers between devices: 0.26 us -> 23.5 us
  Pallas kernels: 0 us -> 18.4 us
  between operations: 13.2 us -> 2.71 us
  other arithmetic: 5.46 us -> 0.12 us
    all_gather x2 -> x0, waiting for transfers between devices: 100 us -> none  [the longest x1 81.6 us: body(): lax.all_gather(inputs, 'lat', axis=1, tiled=True)]
    ppermute x0 -> x19, waiting for transfers between devices: none -> 38.6 us  [the longest x13 36.3 us: swap(): return lax.ppermute(values, 'lat', [(i, i ^ mask) for i in range(owners)])]
    dot_general x3 -> x0, matrix products: 32.1 us -> none  [the longest x1 15.3 us: body(): jnp.einsum('tnp,cdnpe->cdtne', onehot, grouped, preferred_element_type=jn...]
    psum x1 -> x0, waiting for transfers between devices: 26.1 us -> none  [body(): summed = lax.psum(preact, 'ckpt')]
    ppermute x0 -> x19, starting transfers between devices: none -> 23.5 us  [the longest x13 21.2 us: swap(): return lax.ppermute(values, 'lat', [(i, i ^ mask) for i in range(owners)])]
    unnamed x10 -> x16, local copies, waits for them, and re-layouts: 22.9 us -> 2.81 us
    pallas_call x0 -> x4, Pallas kernels: none -> 18.4 us  [the longest x1 6.15 us: stage_decoder(): pl.pallas_call(stage_decoder_kernel, out_shape=jax.ShapeDtypeStruct((tile...]
    reshape x2 -> x3, local copies, waits for them, and re-layouts: 5.43 us -> 0.98 us  [the longest x1 0.76 us: body_planes(): ids = block_ids.reshape(-1)]
  transfers between devices with their start and end apart: 3 -> 19, of which waited for: 3 -> 9; matrix products, arithmetic and copies ran while one was open for 18% -> 1% of each run, Pallas kernels for 0% -> 7%
where the time goes in v1:
time: 88.5 us; the launch traced here: 87.9 us
  waiting for transfers between devices  38.6 us (44%)
  starting transfers between devices  23.5 us (27%)
  Pallas kernels  18.4 us (21%)
  local copies, waits for them, and re-layouts  4.7 us (5%)
  between operations  2.71 us (3%)
    ppermute x13, waiting for transfers between devices, swap(): return lax.ppermute(values, 'lat', [(i, i ^ mask) for i in range(owners)])  36.3 us
    ppermute x13, starting transfers between devices, swap(): return lax.ppermute(values, 'lat', [(i, i ^ mask) for i in range(owners)])  21.2 us
    pallas_call x1, Pallas kernels, stage_decoder(): pl.pallas_call(stage_decoder_kernel, out_shape=jax.ShapeDtypeStruct((tile...  6.15 us
    pallas_call x1, Pallas kernels, encode(): pl.pallas_call(functools.partial(encode_kernel, owners=owners), out_shape...  4.54 us
    pallas_call x1, Pallas kernels, decode(): pl.pallas_call(functools.partial(decode_kernel, owners=owners), out_shape...  4.04 us
    pallas_call x1, Pallas kernels, send_columns(): pl.pallas_call(functools.partial(send_columns_kernel, owners=owners), out...  3.63 us
    unnamed x16, local copies, waits for them, and re-layouts  2.81 us
    ppermute x5, waiting for transfers between devices, across(): return lax.ppermute(values, 'ckpt', [(0, 1), (1, 0)])  2.2 us
  transfers between devices with their start and end apart: 19, of which 9 were waited for; matrix products, arithmetic and copies ran while one was open for 1% of the time, Pallas kernels for 7%

profile of v1, /device:TPU:0, one launch (start us, length us, event | category | flops | bytes accessed | tf_op | source)
XLA Modules:
  0.0 87.9 jit_solution(12822863566839840199)
XLA Ops:
  0.0 0.8 reshape.53.ids_ref
  0.8 3.6 %send_columns.1 = bf16[4096,128]{1,0:T(8,128)(2,1)S(1)} custom-call(s32[64]{0:T(128)S(1)} %reshape.53.ids_ref, s32[2]{0:T(128)S(1)} %pad_add_fusion.at_ref, bf16[4096,2048]{1,0:T(8,128)(2,1)} %bitcast.41, bf16[4096,2048]{1,0:T(8,128)(2,1)} %bitcast.42), custom_call_target="tpu_custom_call" | custom-call | bytes 3145728 | tf_op jit(solution)/shard_map/send_columns/pallas_call | solution.py:90
  4.5 3.1 %collective-permute-start.7 = (bf16[4096,128]{1,0:T(8,128)(2,1)S(1)}, bf16[4096,128]{1,0:T(8,128)(2,1)}, u32[]{:S(2)}, u32[]{:S(2)}) collective-permute-start(bf16[4096,128]{1,0:T(8,128)(2,1)S(1)} %send_columns.1), channel_id=1, source_target_pairs={{0,8},{2,10},{4,12},{6,14},{8,0},{10,2},{12,4},{14,6},{16,24},{18,... | collective-permute-start | bytes 3145736 | tf_op jit(solution)/shard_map/ppermute | solution.py:274
  7.6 2.6 %collective-permute-start.3 = (bf16[32,4096]{1,0:T(8,128)(2,1)S(1)}, bf16[32,4096]{1,0:T(8,128)(2,1)S(1)}, u32[]{:S(2)}, u32[]{:S(2)}) collective-permute-start(bf16[32,4096]{1,0:T(8,128)(2,1)S(1)} %bitcast.20), channel_id=1, source_target_pairs={{0,16},{2,18},{4,20},{6,22},{8,24},{10,26},{12,28},{14,30},{16,0},... | collective-permute-start | bytes 786440 | tf_op jit(solution)/shard_map/ppermute | solution.py:274
  10.2 1.5 %collective-permute-start = (bf16[32,4096]{1,0:T(8,128)(2,1)S(1)}, bf16[32,4096]{1,0:T(8,128)(2,1)S(1)}, u32[]{:S(2)}, u32[]{:S(2)}) collective-permute-start(bf16[32,4096]{1,0:T(8,128)(2,1)S(1)} %bitcast.21), channel_id=1, source_target_pairs={{0,2},{2,0},{4,6},{6,4},{8,10},{10,8},{12,14},{14,12},{16,18},{18,... | collective-permute-start | bytes 786440 | tf_op jit(solution)/shard_map/ppermute | solution.py:274
  11.7 1.5 %collective-permute-start.1 = (bf16[32,4096]{1,0:T(8,128)(2,1)S(1)}, bf16[32,4096]{1,0:T(8,128)(2,1)S(1)}, u32[]{:S(2)}, u32[]{:S(2)}) collective-permute-start(bf16[32,4096]{1,0:T(8,128)(2,1)S(1)} %bitcast.22), channel_id=1, source_target_pairs={{0,4},{2,6},{4,0},{6,2},{8,12},{10,14},{12,8},{14,10},{16,20},{18,... | collective-permute-start | bytes 786440 | tf_op jit(solution)/shard_map/ppermute | solution.py:274
  13.2 0.4 collective-permute-start.8
  13.6 0.7 fusion
  15.6 20.9 %collective-permute-done.8 = f32[2048]{0:T(1024)S(1)} collective-permute-done((f32[2048]{0:T(1024)S(1)}, f32[2048]{0:T(1024)S(1)}, u32[]{:S(2)}, u32[]{:S(2)}) %collective-permute-start.8) | collective-permute-done | bytes 8224 | tf_op jit(solution)/shard_map/ppermute | solution.py:274
  36.5 2.6 %collective-permute-start.2 = (bf16[32,4096]{1,0:T(8,128)(2,1)S(1)}, bf16[32,4096]{1,0:T(8,128)(2,1)S(1)}, u32[]{:S(2)}, u32[]{:S(2)}) collective-permute-start(bf16[32,4096]{1,0:T(8,128)(2,1)S(1)} %bitcast.23), channel_id=1, source_target_pairs={{0,6},{2,4},{4,2},{6,0},{8,14},{10,12},{12,10},{14,8},{16,22},{18,... | collective-permute-start | bytes 786440 | tf_op jit(solution)/shard_map/ppermute | solution.py:274
  39.2 0.5 collective-permute-start.4
  39.7 0.3 collective-permute-start.5
  40.0 2.6 %collective-permute-start.6 = (bf16[32,4096]{1,0:T(8,128)(2,1)S(1)}, bf16[32,4096]{1,0:T(8,128)(2,1)S(1)}, u32[]{:S(2)}, u32[]{:S(2)}) collective-permute-start(bf16[32,4096]{1,0:T(8,128)(2,1)S(1)} %collective-permute-done.3.refs_4_), channel_id=1, source_target_pairs={{0,6},{2,4},{4,2},{6,0},{8,14},{10,12},{12,10},{14,8},{16,22},{18,... | collective-permute-start | bytes 786440 | tf_op jit(solution)/shard_map/ppermute | solution.py:274
  44.0 6.2 %stage_decoder.1.refs_8_ = bf16[4,256,2048]{2,1,0:T(8,128)(2,1)} custom-call(s32[64]{0:T(128)S(1)} %reshape.53.ids_ref, bf16[256,32768]{1,0:T(8,128)(2,1)} %bitcast.25, bf16[256,32768]{1,0:T(8,128)(2,1)} %bitcast.26, bf16[256,32768]{1,0:T(8,128)(2,1)} %bitcast.27, bf16[256,32768]{1,0:T(8,128)(2,1)} %bitcast.28, bf16[256,32768]{1,0:T(8,128)(2,1)} %bitcast.29, ...), custom_call_target="tpu_custom_call" | custom-call | bytes 8388608 | tf_op jit(solution)/shard_map/stage_decoder/pallas_call | solution.py:190
  50.3 2.2 %collective-permute-done.4.refs_5_ = bf16[32,4096]{1,0:T(8,128)(2,1)S(1)} collective-permute-done((bf16[32,4096]{1,0:T(8,128)(2,1)S(1)}, bf16[32,4096]{1,0:T(8,128)(2,1)S(1)}, u32[]{:S(2)}, u32[]{:S(2)}) %collective-permute-start.4) | collective-permute-done | bytes 262176 | tf_op jit(solution)/shard_map/ppermute | solution.py:274
  52.6 3.7 %collective-permute-done.6.refs_7_ = bf16[32,4096]{1,0:T(8,128)(2,1)S(1)} collective-permute-done((bf16[32,4096]{1,0:T(8,128)(2,1)S(1)}, bf16[32,4096]{1,0:T(8,128)(2,1)S(1)}, u32[]{:S(2)}, u32[]{:S(2)}) %collective-permute-start.6) | collective-permute-done | bytes 262176 | tf_op jit(solution)/shard_map/ppermute | solution.py:274
  56.4 0.6 copy-done.3
  57.0 4.5 %encode.1 = f32[4,64,128]{2,1,0:T(8,128)S(1)} custom-call(s32[64]{0:T(128)S(1)} %reshape.53.ids_ref, s32[64]{0:T(128)S(1)} %reshape.54.live_ref, s32[2]{0:T(128)S(1)} %pad_add_fusion.at_ref, bf16[32,4096]{1,0:T(8,128)(2,1)S(1)} %bitcast.24, bf16[32,4096]{1,0:T(8,128)(2,1)S(1)} %collective-permute-done.refs_1_, ...), custom_call_target="tpu_custom_call" | custom-call | flops 536870912 | bytes 5242880 | tf_op jit(solution)/shard_map/encode/pallas_call | solution.py:156
  61.6 1.3 %collective-permute-done.9 = f32[4,64,128]{2,1,0:T(8,128)S(1)} collective-permute-done((f32[4,64,128]{2,1,0:T(8,128)S(1)}, f32[4,64,128]{2,1,0:T(8,128)S(1)}, u32[]{:S(2)}, u32[]{:S(2)}) %collective-permute-start.9) | collective-permute-done | bytes 131104 | tf_op jit(solution)/shard_map/ppermute | solution.py:277
  63.0 2.4 %collective-permute-start.11 = (bf16[2,2,64,128]{3,2,1,0:T(8,128)(2,1)S(1)}, bf16[2,2,64,128]{3,2,1,0:T(8,128)(2,1)S(1)}, u32[]{:S(2)}, u32[]{:S(2)}) collective-permute-start(bf16[2,2,64,128]{3,2,1,0:T(8,128)(2,1)S(1)} %bitcast.45), channel_id=1, source_target_pairs={{0,16},{2,18},{4,20},{6,22},{8,24},{10,26},{12,28},{14,30},{16,0},... | collective-permute-start | bytes 196616 | tf_op jit(solution)/shard_map/ppermute | solution.py:274
  65.4 1.7 %collective-permute-start.10 = (bf16[2,2,64,128]{3,2,1,0:T(8,128)(2,1)S(1)}, bf16[2,2,64,128]{3,2,1,0:T(8,128)(2,1)S(1)}, u32[]{:S(2)}, u32[]{:S(2)}) collective-permute-start(bf16[2,2,64,128]{3,2,1,0:T(8,128)(2,1)S(1)} %bitcast.46), channel_id=1, source_target_pairs={{0,8},{2,10},{4,12},{6,14},{8,0},{10,2},{12,4},{14,6},{16,24},{18,... | collective-permute-start | bytes 196616 | tf_op jit(solution)/shard_map/ppermute | solution.py:301
  67.1 3.8 %collective-permute-done.11 = bf16[2,2,64,128]{3,2,1,0:T(8,128)(2,1)S(1)} collective-permute-done((bf16[2,2,64,128]{3,2,1,0:T(8,128)(2,1)S(1)}, bf16[2,2,64,128]{3,2,1,0:T(8,128)(2,1)S(1)}, u32[]{:S(2)}, u32[]{:S(2)}) %collective-permute-start.11) | collective-permute-done | bytes 65568 | tf_op jit(solution)/shard_map/ppermute | solution.py:274
  71.0 1.4 %collective-permute-start.12 = (bf16[4,2,64,128]{3,2,1,0:T(8,128)(2,1)S(1)}, bf16[4,2,64,128]{3,2,1,0:T(8,128)(2,1)S(1)}, u32[]{:S(2)}, u32[]{:S(2)}) collective-permute-start(bf16[4,2,64,128]{3,2,1,0:T(8,128)(2,1)S(1)} %pad_maximum_fusion.refs_0_), channel_id=1, source_target_pairs={{0,2},{2,0},{4,6},{6,4},{8,10},{10,8},{12,14},{14,12},{16,18},{18,... | collective-permute-start | bytes 393224 | tf_op jit(solution)/shard_map/ppermute | solution.py:274
  72.4 1.5 %collective-permute-start.13 = (bf16[4,2,64,128]{3,2,1,0:T(8,128)(2,1)S(1)}, bf16[4,2,64,128]{3,2,1,0:T(8,128)(2,1)S(1)}, u32[]{:S(2)}, u32[]{:S(2)}) collective-permute-start(bf16[4,2,64,128]{3,2,1,0:T(8,128)(2,1)S(1)} %pad_maximum_fusion.refs_0_), channel_id=1, source_target_pairs={{0,4},{2,6},{4,0},{6,2},{8,12},{10,14},{12,8},{14,10},{16,20},{18,... | collective-permute-start | bytes 393224 | tf_op jit(solution)/shard_map/ppermute | solution.py:274
  73.9 0.6 collective-permute-start.14
  74.5 2.1 %collective-permute-done.12.refs_1_ = bf16[4,2,64,128]{3,2,1,0:T(8,128)(2,1)S(1)} collective-permute-done((bf16[4,2,64,128]{3,2,1,0:T(8,128)(2,1)S(1)}, bf16[4,2,64,128]{3,2,1,0:T(8,128)(2,1)S(1)}, u32[]{:S(2)}, u32[]{:S(2)}) %collective-permute-start.12) | collective-permute-done | bytes 131104 | tf_op jit(solution)/shard_map/ppermute | solution.py:274
  76.6 3.5 %collective-permute-done.13.refs_2_ = bf16[4,2,64,128]{3,2,1,0:T(8,128)(2,1)S(1)} collective-permute-done((bf16[4,2,64,128]{3,2,1,0:T(8,128)(2,1)S(1)}, bf16[4,2,64,128]{3,2,1,0:T(8,128)(2,1)S(1)}, u32[]{:S(2)}, u32[]{:S(2)}) %collective-permute-start.13) | collective-permute-done | bytes 131104 | tf_op jit(solution)/shard_map/ppermute | solution.py:274
  80.2 0.5 collective-permute-start.18
  80.8 0.7 collective-permute-done.17.refs_6_
  81.5 0.2 collective-permute-done.18.refs_7_
  81.7 2.2 %copy-done = bf16[4,256,2048]{2,1,0:T(8,128)(2,1)S(1)} copy-done((bf16[4,256,2048]{2,1,0:T(8,128)(2,1)S(1)}, bf16[4,256,2048]{2,1,0:T(8,128)(2,1)}, u32[]{:S(2)}) %copy-start) | copy-done | bytes 4194328
  83.9 4.0 %decode.1 = bf16[256,512]{1,0:T(8,128)(2,1)} custom-call(s32[64]{0:T(128)S(1)} %reshape.53.ids_ref, s32[2]{0:T(128)S(1)} %pad_add_fusion.at_ref, bf16[4,2,64,128]{3,2,1,0:T(8,128)(2,1)S(1)} %pad_maximum_fusion.refs_0_, bf16[4,2,64,128]{3,2,1,0:T(8,128)(2,1)S(1)} %collective-permute-done.12.refs_1_, ...), custom_call_target="tpu_custom_call" | custom-call | flops 536870912 | bytes 6291456 | tf_op jit(solution)/shard_map/decode/pallas_call | solution.py:241
  (39 shorter events, 0.7 us)
Async XLA Ops:
  0.8 6.7 %copy-start.1 = (bf16[1,32,4096]{2,1,0:T(8,128)(2,1)S(1)}, bf16[1,32,4096]{2,1,0:T(8,128)(2,1)}, u32[]{:S(2)}) copy-start(bf16[1,32,4096]{2,1,0:T(8,128)(2,1)} %param.7) | copy-start | bytes 786436
  0.8 12.3 %copy-start.7 = (f32[2048]{0:T(1024)S(1)}, f32[2048]{0:T(1024)}, u32[]{:S(2)}) copy-start(f32[2048]{0:T(1024)} %param.9) | copy-start | bytes 24580
  0.8 12.8 %copy-start.4 = (s32[4,16]{1,0:T(4,128)S(1)}, s32[4,16]{1,0:T(4,128)}, u32[]{:S(2)}) copy-start(s32[4,16]{1,0:T(4,128)} %param.12) | copy-start | bytes 772
  4.5 51.8 %collective-permute-start.7 = (bf16[4096,128]{1,0:T(8,128)(2,1)S(1)}, bf16[4096,128]{1,0:T(8,128)(2,1)}, u32[]{:S(2)}, u32[]{:S(2)}) collective-permute-start(bf16[4096,128]{1,0:T(8,128)(2,1)S(1)} %send_columns.1), channel_id=1, source_target_pairs={{0,8},{2,10},{4,12},{6,14},{8,0},{10,2},{12,4},{14,6},{16,24},{18,... | collective-permute-start | bytes 3145736 | tf_op jit(solution)/shard_map/ppermute | solution.py:274
  7.6 31.6 %collective-permute-start.3 = (bf16[32,4096]{1,0:T(8,128)(2,1)S(1)}, bf16[32,4096]{1,0:T(8,128)(2,1)S(1)}, u32[]{:S(2)}, u32[]{:S(2)}) collective-permute-start(bf16[32,4096]{1,0:T(8,128)(2,1)S(1)} %bitcast.20), channel_id=1, source_target_pairs={{0,16},{2,18},{4,20},{6,22},{8,24},{10,26},{12,28},{14,30},{16,0},... | collective-permute-start | bytes 786440 | tf_op jit(solution)/shard_map/ppermute | solution.py:274
  10.2 29.5 %collective-permute-start = (bf16[32,4096]{1,0:T(8,128)(2,1)S(1)}, bf16[32,4096]{1,0:T(8,128)(2,1)S(1)}, u32[]{:S(2)}, u32[]{:S(2)}) collective-permute-start(bf16[32,4096]{1,0:T(8,128)(2,1)S(1)} %bitcast.21), channel_id=1, source_target_pairs={{0,2},{2,0},{4,6},{6,4},{8,10},{10,8},{12,14},{14,12},{16,18},{18,... | collective-permute-start | bytes 786440 | tf_op jit(solution)/shard_map/ppermute | solution.py:274
  11.7 28.4 %collective-permute-start.1 = (bf16[32,4096]{1,0:T(8,128)(2,1)S(1)}, bf16[32,4096]{1,0:T(8,128)(2,1)S(1)}, u32[]{:S(2)}, u32[]{:S(2)}) collective-permute-start(bf16[32,4096]{1,0:T(8,128)(2,1)S(1)} %bitcast.22), channel_id=1, source_target_pairs={{0,4},{2,6},{4,0},{6,2},{8,12},{10,14},{12,8},{14,10},{16,20},{18,... | collective-permute-start | bytes 786440 | tf_op jit(solution)/shard_map/ppermute | solution.py:274
  13.2 23.4 %collective-permute-start.8 = (f32[2048]{0:T(1024)S(1)}, f32[2048]{0:T(1024)S(1)}, u32[]{:S(2)}, u32[]{:S(2)}) collective-permute-start(f32[2048]{0:T(1024)S(1)} %copy-done.7), channel_id=1, source_target_pairs={{0,8},{2,10},{4,12},{6,14},{8,0},{10,2},{12,4},{14,6},{16,24},{18,... | collective-permute-start | bytes 24584 | tf_op jit(solution)/shard_map/ppermute | solution.py:274
  36.5 13.8 %collective-permute-start.2 = (bf16[32,4096]{1,0:T(8,128)(2,1)S(1)}, bf16[32,4096]{1,0:T(8,128)(2,1)S(1)}, u32[]{:S(2)}, u32[]{:S(2)}) collective-permute-start(bf16[32,4096]{1,0:T(8,128)(2,1)S(1)} %bitcast.23), channel_id=1, source_target_pairs={{0,6},{2,4},{4,2},{6,0},{8,14},{10,12},{12,10},{14,8},{16,22},{18,... | collective-permute-start | bytes 786440 | tf_op jit(solution)/shard_map/ppermute | solution.py:274
  39.2 13.4 %collective-permute-start.4 = (bf16[32,4096]{1,0:T(8,128)(2,1)S(1)}, bf16[32,4096]{1,0:T(8,128)(2,1)S(1)}, u32[]{:S(2)}, u32[]{:S(2)}) collective-permute-start(bf16[32,4096]{1,0:T(8,128)(2,1)S(1)} %collective-permute-done.3.refs_4_), channel_id=1, source_target_pairs={{0,2},{2,0},{4,6},{6,4},{8,10},{10,8},{12,14},{14,12},{16,18},{18,... | collective-permute-start | bytes 786440 | tf_op jit(solution)/shard_map/ppermute | solution.py:274
  39.7 12.9 %collective-permute-start.5 = (bf16[32,4096]{1,0:T(8,128)(2,1)S(1)}, bf16[32,4096]{1,0:T(8,128)(2,1)S(1)}, u32[]{:S(2)}, u32[]{:S(2)}) collective-permute-start(bf16[32,4096]{1,0:T(8,128)(2,1)S(1)} %collective-permute-done.3.refs_4_), channel_id=1, source_target_pairs={{0,4},{2,6},{4,0},{6,2},{8,12},{10,14},{12,8},{14,10},{16,20},{18,... | collective-permute-start | bytes 786440 | tf_op jit(solution)/shard_map/ppermute | solution.py:274
  40.0 16.3 %collective-permute-start.6 = (bf16[32,4096]{1,0:T(8,128)(2,1)S(1)}, bf16[32,4096]{1,0:T(8,128)(2,1)S(1)}, u32[]{:S(2)}, u32[]{:S(2)}) collective-permute-start(bf16[32,4096]{1,0:T(8,128)(2,1)S(1)} %collective-permute-done.3.refs_4_), channel_id=1, source_target_pairs={{0,6},{2,4},{4,2},{6,0},{8,14},{10,12},{12,10},{14,8},{16,22},{18,... | collective-permute-start | bytes 786440 | tf_op jit(solution)/shard_map/ppermute | solution.py:274
  44.0 6.2 %copy-start.5 = (s32[4,16]{1,0:T(4,128)S(1)}, s32[4,16]{1,0:T(4,128)}, u32[]{:S(2)}) copy-start(s32[4,16]{1,0:T(4,128)} %param.13) | copy-start | bytes 772
  52.6 3.8 %copy-start.2 = (bf16[32,4096]{1,0:T(8,128)(2,1)}, bf16[32,4096]{1,0:T(8,128)(2,1)S(1)}, u32[]{:S(2)}) copy-start(bf16[32,4096]{1,0:T(8,128)(2,1)S(1)} %collective-permute-done.5.refs_6_) | copy-start | bytes 786436
  56.3 0.7 copy-start.3
  57.0 23.7 %copy-start.6 = (f32[1,256]{1,0:T(1,128)S(1)}, f32[1,256]{1,0:T(1,128)}, u32[]{:S(2)}) copy-start(f32[1,256]{1,0:T(1,128)} %param.11) | copy-start | bytes 3076
  61.6 1.4 %collective-permute-start.9 = (f32[4,64,128]{2,1,0:T(8,128)S(1)}, f32[4,64,128]{2,1,0:T(8,128)S(1)}, u32[]{:S(2)}, u32[]{:S(2)}) collective-permute-start(f32[4,64,128]{2,1,0:T(8,128)S(1)} %encode.1), channel_id=1, source_target_pairs={{0,1},{1,0},{2,3},{3,2},{4,5},{5,4},{6,7},{7,6},{8,9},{9,8},{10,11... | collective-permute-start | bytes 393224 | tf_op jit(solution)/shard_map/ppermute | solution.py:277
  63.0 7.9 %collective-permute-start.11 = (bf16[2,2,64,128]{3,2,1,0:T(8,128)(2,1)S(1)}, bf16[2,2,64,128]{3,2,1,0:T(8,128)(2,1)S(1)}, u32[]{:S(2)}, u32[]{:S(2)}) collective-permute-start(bf16[2,2,64,128]{3,2,1,0:T(8,128)(2,1)S(1)} %bitcast.45), channel_id=1, source_target_pairs={{0,16},{2,18},{4,20},{6,22},{8,24},{10,26},{12,28},{14,30},{16,0},... | collective-permute-start | bytes 196616 | tf_op jit(solution)/shard_map/ppermute | solution.py:274
  65.4 5.6 %collective-permute-start.10 = (bf16[2,2,64,128]{3,2,1,0:T(8,128)(2,1)S(1)}, bf16[2,2,64,128]{3,2,1,0:T(8,128)(2,1)S(1)}, u32[]{:S(2)}, u32[]{:S(2)}) collective-permute-start(bf16[2,2,64,128]{3,2,1,0:T(8,128)(2,1)S(1)} %bitcast.46), channel_id=1, source_target_pairs={{0,8},{2,10},{4,12},{6,14},{8,0},{10,2},{12,4},{14,6},{16,24},{18,... | collective-permute-start | bytes 196616 | tf_op jit(solution)/shard_map/ppermute | solution.py:301
  71.0 5.6 %collective-permute-start.12 = (bf16[4,2,64,128]{3,2,1,0:T(8,128)(2,1)S(1)}, bf16[4,2,64,128]{3,2,1,0:T(8,128)(2,1)S(1)}, u32[]{:S(2)}, u32[]{:S(2)}) collective-permute-start(bf16[4,2,64,128]{3,2,1,0:T(8,128)(2,1)S(1)} %pad_maximum_fusion.refs_0_), channel_id=1, source_target_pairs={{0,2},{2,0},{4,6},{6,4},{8,10},{10,8},{12,14},{14,12},{16,18},{18,... | collective-permute-start | bytes 393224 | tf_op jit(solution)/shard_map/ppermute | solution.py:274
  72.4 7.8 %collective-permute-start.13 = (bf16[4,2,64,128]{3,2,1,0:T(8,128)(2,1)S(1)}, bf16[4,2,64,128]{3,2,1,0:T(8,128)(2,1)S(1)}, u32[]{:S(2)}, u32[]{:S(2)}) collective-permute-start(bf16[4,2,64,128]{3,2,1,0:T(8,128)(2,1)S(1)} %pad_maximum_fusion.refs_0_), channel_id=1, source_target_pairs={{0,4},{2,6},{4,0},{6,2},{8,12},{10,14},{12,8},{14,10},{16,20},{18,... | collective-permute-start | bytes 393224 | tf_op jit(solution)/shard_map/ppermute | solution.py:274
  73.9 6.3 %collective-permute-start.14 = (bf16[4,2,64,128]{3,2,1,0:T(8,128)(2,1)S(1)}, bf16[4,2,64,128]{3,2,1,0:T(8,128)(2,1)S(1)}, u32[]{:S(2)}, u32[]{:S(2)}) collective-permute-start(bf16[4,2,64,128]{3,2,1,0:T(8,128)(2,1)S(1)} %pad_maximum_fusion.refs_0_), channel_id=1, source_target_pairs={{0,6},{2,4},{4,2},{6,0},{8,14},{10,12},{12,10},{14,8},{16,22},{18,... | collective-permute-start | bytes 393224 | tf_op jit(solution)/shard_map/ppermute | solution.py:274
  74.5 6.3 %collective-permute-start.15 = (bf16[4,2,64,128]{3,2,1,0:T(8,128)(2,1)S(1)}, bf16[4,2,64,128]{3,2,1,0:T(8,128)(2,1)S(1)}, u32[]{:S(2)}, u32[]{:S(2)}) collective-permute-start(bf16[4,2,64,128]{3,2,1,0:T(8,128)(2,1)S(1)} %pad_maximum_fusion.refs_0_), channel_id=1, source_target_pairs={{0,1},{1,0},{2,3},{3,2},{4,5},{5,4},{6,7},{7,6},{8,9},{9,8},{10,11... | collective-permute-start | bytes 393224 | tf_op jit(solution)/shard_map/ppermute | solution.py:277
  76.6 4.2 %collective-permute-start.16 = (bf16[4,2,64,128]{3,2,1,0:T(8,128)(2,1)S(1)}, bf16[4,2,64,128]{3,2,1,0:T(8,128)(2,1)S(1)}, u32[]{:S(2)}, u32[]{:S(2)}) collective-permute-start(bf16[4,2,64,128]{3,2,1,0:T(8,128)(2,1)S(1)} %collective-permute-done.12.refs_1_), channel_id=1, source_target_pairs={{0,1},{1,0},{2,3},{3,2},{4,5},{5,4},{6,7},{7,6},{8,9},{9,8},{10,11... | collective-permute-start | bytes 393224 | tf_op jit(solution)/shard_map/ppermute | solution.py:277
  80.2 1.3 %collective-permute-start.17 = (bf16[4,2,64,128]{3,2,1,0:T(8,128)(2,1)S(1)}, bf16[4,2,64,128]{3,2,1,0:T(8,128)(2,1)S(1)}, u32[]{:S(2)}, u32[]{:S(2)}) collective-permute-start(bf16[4,2,64,128]{3,2,1,0:T(8,128)(2,1)S(1)} %collective-permute-done.13.refs_2_), channel_id=1, source_target_pairs={{0,1},{1,0},{2,3},{3,2},{4,5},{5,4},{6,7},{7,6},{8,9},{9,8},{10,11... | collective-permute-start | bytes 393224 | tf_op jit(solution)/shard_map/ppermute | solution.py:277
  80.2 1.5 %collective-permute-start.18 = (bf16[4,2,64,128]{3,2,1,0:T(8,128)(2,1)S(1)}, bf16[4,2,64,128]{3,2,1,0:T(8,128)(2,1)S(1)}, u32[]{:S(2)}, u32[]{:S(2)}) collective-permute-start(bf16[4,2,64,128]{3,2,1,0:T(8,128)(2,1)S(1)} %collective-permute-done.14.refs_3_), channel_id=1, source_target_pairs={{0,1},{1,0},{2,3},{3,2},{4,5},{5,4},{6,7},{7,6},{8,9},{9,8},{10,11... | collective-permute-start | bytes 393224 | tf_op jit(solution)/shard_map/ppermute | solution.py:277
  81.7 2.2 %copy-start = (bf16[4,256,2048]{2,1,0:T(8,128)(2,1)S(1)}, bf16[4,256,2048]{2,1,0:T(8,128)(2,1)}, u32[]{:S(2)}) copy-start(bf16[4,256,2048]{2,1,0:T(8,128)(2,1)} %stage_decoder.1.refs_8_) | copy-start | bytes 12582916

commit v2 on v0

v2 whole, which is shorter than its diff:
```python
import functools

import jax
import jax.numpy as jnp
from jax import lax
from jax.experimental import pallas as pl
from jax.experimental.pallas import tpu as pltpu
from jax.sharding import PartitionSpec as P

BLOCK = 64
TILE = 128
PAIR = 2 * BLOCK
EXTRA = 16
FIRST = 2048
F32 = jnp.float32
BF16 = jnp.bfloat16
VMEM_WEIGHTS = 50 * 1024 * 1024
VMEM_SMALL = 12 * 1024 * 1024


def body_any(inputs, enc_weight, enc_bias, dec_weight, dec_bias, block_ids, live):
    lat_count = lax.axis_size("lat")
    lat_index = lax.axis_index("lat")
    lat_dev = enc_weight.shape[2]
    own_blocks = lat_dev // BLOCK
    local_ckpts = dec_weight.shape[0]
    features = dec_weight.shape[1]
    preact = jnp.einsum(
        "cdl,crd->lr",
        enc_weight,
        lax.all_gather(inputs, "lat", axis=1, tiled=True),
        preferred_element_type=F32,
    )
    token_count = preact.shape[1]
    tiles = token_count // TILE
    own_ids = lax.dynamic_slice_in_dim(block_ids, lat_index, 1, 1)[:, 0]
    own_live = lax.dynamic_slice_in_dim(live, lat_index, 1, 1)[:, 0]
    choose = (own_ids[:, None] == jnp.arange(own_blocks, dtype=jnp.int32)[None, :]) & (own_live[:, None] == 1)
    choose_cols = jnp.transpose(choose.astype(F32))
    grouped_vals = preact.reshape(own_blocks, BLOCK, tiles, TILE)
    picked = jnp.sum(grouped_vals * choose_cols[:, None, :, None], axis=0)
    picked_bias = jnp.einsum("pe,pt->et", enc_bias.reshape(own_blocks, BLOCK), choose_cols, precision=lax.Precision.HIGHEST)
    summed = lax.psum(picked, "ckpt") + picked_bias[:, :, None]
    acts = jnp.transpose(jnp.maximum(summed, 0.0), (1, 0, 2)).astype(BF16)
    onehot = (
        (block_ids[:, :, None] == jnp.arange(own_blocks, dtype=jnp.int32)[None, None, :]) & (live[:, :, None] == 1)
    ).astype(BF16)
    grouped = dec_weight.reshape(local_ckpts, features, lat_count, own_blocks, BLOCK)
    selected = jnp.einsum("tnp,cdnpe->cdtne", onehot, grouped, preferred_element_type=F32).astype(BF16)
    total = jnp.einsum(
        "ntes,cdtne->cdts",
        lax.all_gather(acts[None], "lat", axis=0, tiled=True),
        selected,
        preferred_element_type=F32,
    )
    recon = total.reshape(local_ckpts, features, token_count)
    return (recon + dec_bias[:, :, None]).astype(BF16)


def swap_if(flag, values):
    return jnp.where(flag, pltpu.roll(values, BLOCK, 1), values)


def side_by_side(first, first_odd, second, second_odd):
    lane = lax.broadcasted_iota(jnp.int32, first.shape, 1)
    return jnp.where(lane < BLOCK, swap_if(first_odd == 1, first), swap_if(second_odd == 0, second))


def column_of(block):
    return pl.ds(pl.multiple_of((block // 2) * PAIR, PAIR), PAIR)


SMEM = pl.BlockSpec(memory_space=pltpu.SMEM)
VMEM = pl.BlockSpec(memory_space=pltpu.VMEM)
ANY = pl.BlockSpec(memory_space=pl.ANY)


def params(limit=VMEM_WEIGHTS):
    return pltpu.CompilerParams(vmem_limit_bytes=limit)


def cost(flops, moved):
    return pl.CostEstimate(flops=flops, bytes_accessed=moved, transcendentals=0)


def send_columns_kernel(ids_ref, weight_ref, bias_ref, out_ref, in_ref, sems, *, step, base):
    lat = lax.axis_index("lat")
    plane = lat // 4
    depth = in_ref.shape[1]
    chunks = depth // step
    extra = out_ref.shape[0] - depth
    blocks = [ids_ref[plane ^ mask, lat] for mask in (1, 3)]
    odds = [block % 2 for block in blocks]

    def fetch(chunk, which):
        source = weight_ref.at[pl.ds(base + chunk * step, step), column_of(blocks[which])]
        return pltpu.make_async_copy(source, in_ref.at[which, pl.ds(chunk * step, step)], sems.at[which, chunk])

    for chunk in range(chunks):
        for which in range(2):
            fetch(chunk, which).start()

    if extra:
        parts = [bias_ref[pl.ds(block // 2, 1), :] for block in blocks]
        bias = side_by_side(parts[0], odds[0], parts[1], odds[1])
        high = bias.astype(BF16)
        middle = (bias - high.astype(F32)).astype(BF16)
        low = (bias - high.astype(F32) - middle.astype(F32)).astype(BF16)
        row = lax.broadcasted_iota(jnp.int32, (extra, PAIR), 0)
        rows = jnp.zeros((extra, PAIR), F32)
        for index, part in enumerate((high, middle, low)):
            rows = jnp.where(row == index, jnp.broadcast_to(part.astype(F32), rows.shape), rows)
        out_ref[depth:, :] = rows.astype(BF16)

    for chunk in range(chunks):
        for which in range(2):
            fetch(chunk, which).wait()
        rows = slice(chunk * step, (chunk + 1) * step)
        both = side_by_side(in_ref[0, rows, :].astype(F32), odds[0], in_ref[1, rows, :].astype(F32), odds[1])
        out_ref[rows, :] = both.astype(BF16)


def send_columns(ids, enc_weight, bias, base, depth, extra, step):
    return pl.pallas_call(
        functools.partial(send_columns_kernel, step=step, base=base),
        out_shape=jax.ShapeDtypeStruct((depth + extra, PAIR), BF16),
        in_specs=[SMEM, ANY, VMEM],
        out_specs=VMEM,
        scratch_shapes=[pltpu.VMEM((2, depth, PAIR), BF16), pltpu.SemaphoreType.DMA((2, depth // step))],
        compiler_params=params(),
        cost_estimate=cost(0, 3 * depth * PAIR * 2),
        name="send_columns",
    )(ids, enc_weight, bias)


def own_columns_kernel(ids_ref, weight_ref, out_ref, sems, *, step):
    lat = lax.axis_index("lat")
    copies = []
    for index in range(2):
        lanes = column_of(ids_ref[(lat // 4) ^ (2 * index), lat])
        for chunk in range(out_ref.shape[1] // step):
            rows = pl.ds(chunk * step, step)
            copies.append(
                pltpu.make_async_copy(weight_ref.at[rows, lanes], out_ref.at[index, rows], sems.at[index, chunk])
            )
    for copy in copies:
        copy.start()
    for copy in copies:
        copy.wait()


def own_columns(ids, enc_weight):
    depth = enc_weight.shape[0]
    step = 1024
    return pl.pallas_call(
        functools.partial(own_columns_kernel, step=step),
        out_shape=jax.ShapeDtypeStruct((2, depth, PAIR), BF16),
        in_specs=[SMEM, ANY],
        out_specs=VMEM,
        scratch_shapes=[pltpu.SemaphoreType.DMA((2, depth // step))],
        compiler_params=params(),
        cost_estimate=cost(0, 4 * depth * PAIR * 2),
        name="own_columns",
    )(ids, enc_weight)


def encode_kernel(ids_ref, live_ref, *refs):
    near = refs[0:4]
    far = refs[4:8]
    own_ref, first_ref, rest_ref, bias_ref, out_ref, turn_ref, flip_ref = refs[8:]
    lat, core = lax.axis_index("lat"), lax.axis_index("ckpt")
    plane, place = lat // 4, lat % 4
    depth = own_ref.shape[1]
    shard = TILE // 4
    step = 1024
    parts = first_ref[FIRST:, :].astype(F32)
    other_bias = (parts[0:1] + parts[1:2]) + parts[2:3]
    for index, tokens in enumerate((near, far)):
        total = jnp.zeros((TILE, 2 * PAIR), F32)
        for start in range(0, depth, step):
            rows = jnp.concatenate([ref[:, start : start + step] for ref in tokens], axis=0)
            partner = first_ref[start : start + step, :] if start < FIRST else rest_ref[start - FIRST : start - FIRST + step, :]
            columns = jnp.concatenate([own_ref[index, start : start + step, :], partner], axis=1)
            total += jnp.dot(rows, columns, preferred_element_type=F32)
        tile = plane ^ (2 * index)
        block = ids_ref[tile, lat]
        bias = jnp.concatenate([bias_ref[pl.ds(block // 2, 1), :], other_bias], axis=1)
        total += jnp.where(core == 0, bias, 0.0)
        for turn in range(4):
            to = pl.ds(pl.multiple_of((place ^ turn) * shard, shard), shard)
            turn_ref[to, :] = total[turn * shard : (turn + 1) * shard, :]
        flip_ref[...] = jnp.transpose(turn_ref[:, :PAIR])
        own = flip_ref[pl.ds(pl.multiple_of((block % 2) * BLOCK, BLOCK), BLOCK), :]
        other = jnp.transpose(turn_ref[:, PAIR:])[index * BLOCK : (index + 1) * BLOCK, :]
        out_ref[index] = jnp.where(live_ref[tile, lat] == 1, own, 0.0)
        out_ref[2 + index] = jnp.where(live_ref[tile, lat ^ 4] == 1, other, 0.0)


def encode(ids, live, near, far, own, first, rest, bias):
    return pl.pallas_call(
        encode_kernel,
        out_shape=jax.ShapeDtypeStruct((4, BLOCK, TILE), F32),
        in_specs=[SMEM, SMEM] + [VMEM] * 12,
        out_specs=VMEM,
        scratch_shapes=[pltpu.VMEM((TILE, 2 * PAIR), F32), pltpu.VMEM((PAIR, TILE), F32)],
        compiler_params=params(VMEM_SMALL),
        cost_estimate=cost(4 * TILE * own.shape[1] * 2 * PAIR, 5 * 2**20),
        name="encode",
    )(ids, live, *near, *far, own, first, rest, bias)


def stage_decoder_kernel(ids_ref, weight_ref, out_ref, in_ref, sems):
    tiles, owners = ids_ref.shape
    span = weight_ref.shape[1] // owners

    def fetch(tile, owner):
        lanes = pl.ds(pl.multiple_of(owner * span + (ids_ref[tile, owner] // 2) * PAIR, PAIR), PAIR)
        return pltpu.make_async_copy(weight_ref.at[:, lanes], in_ref.at[tile, owner], sems.at[tile, owner])

    for tile in range(tiles):
        for owner in range(owners):
            fetch(tile, owner).start()
    for tile in range(tiles):
        for owner in range(0, owners, 2):
            fetch(tile, owner).wait()
            fetch(tile, owner + 1).wait()
            both = side_by_side(
                in_ref[tile, owner].astype(F32),
                ids_ref[tile, owner] % 2,
                in_ref[tile, owner + 1].astype(F32),
                ids_ref[tile, owner + 1] % 2,
            )
            out_ref[tile, :, owner * BLOCK : owner * BLOCK + PAIR] = both.astype(BF16)


def stage_decoder(ids, dec_weight):
    tiles, owners = ids.shape
    features = dec_weight.shape[0]
    return pl.pallas_call(
        stage_decoder_kernel,
        out_shape=jax.ShapeDtypeStruct((tiles, features, owners * BLOCK), BF16),
        in_specs=[SMEM, ANY],
        out_specs=VMEM,
        scratch_shapes=[
            pltpu.VMEM((tiles, owners, features, PAIR), BF16),
            pltpu.SemaphoreType.DMA((tiles, owners)),
        ],
        compiler_params=params(),
        cost_estimate=cost(0, 6 * tiles * features * owners * BLOCK),
        name="stage_decoder",
    )(ids, dec_weight)


def decode_kernel(*refs):
    mine = refs[0:4]
    theirs = refs[4:8]
    columns_ref, bias_ref, out_ref, acts_ref, back_ref, sems = refs[8:]
    lat, core = lax.axis_index("lat"), lax.axis_index("ckpt")
    tiles, _, depth = columns_ref.shape
    for place in range(4):
        for ref, holder in ((mine[place], core), (theirs[place], 1 - core)):
            slots = ((0, holder), (4 + 8 * holder, 0), (4 + 8 * holder, 1), (8, holder))
            for slot, (mask, which) in enumerate(slots):
                source = lat ^ place ^ mask
                owner = source ^ (4 * which)
                for index in range(2):
                    tile = (source // 4) ^ (2 * index)
                    row = pl.multiple_of(tile * depth + owner * BLOCK, BLOCK)
                    acts_ref[pl.ds(row, BLOCK), :] = ref[slot, index]

    def give(tile):
        lanes = pl.ds(tile * TILE, TILE)
        return pltpu.make_async_copy(back_ref.at[tile], out_ref.at[:, lanes], sems.at[tile])

    for tile in range(tiles):
        acts = acts_ref[tile * depth : (tile + 1) * depth, :]
        total = jnp.dot(columns_ref[tile], acts, preferred_element_type=F32)
        back_ref[tile] = (total + bias_ref[...]).astype(BF16)
        give(tile).start()
    for tile in range(tiles):
        give(tile).wait()


def decode(mine, theirs, columns, dec_bias):
    tiles, features, depth = columns.shape
    return pl.pallas_call(
        decode_kernel,
        out_shape=jax.ShapeDtypeStruct((features, tiles * TILE), BF16),
        in_specs=[VMEM] * 10,
        out_specs=ANY,
        scratch_shapes=[
            pltpu.VMEM((tiles * depth, TILE), BF16),
            pltpu.VMEM((tiles, features, TILE), BF16),
            pltpu.SemaphoreType.DMA((tiles,)),
        ],
        compiler_params=params(VMEM_SMALL),
        cost_estimate=cost(2 * tiles * features * depth * TILE, 4 * 2**20),
        name="decode",
    )(*mine, *theirs, columns, dec_bias)


def body_planes(inputs, enc_weight, enc_bias, dec_weight, dec_bias, block_ids, live):
    owners = lax.axis_size("lat")
    core = lax.axis_index("ckpt")

    def swap(values, mask):
        return lax.ppermute(values, "lat", [(i, i ^ mask) for i in range(owners)])

    def across(values):
        return lax.ppermute(values, "ckpt", [(0, 1), (1, 0)])

    near_own = inputs[0]
    far_own = swap(near_own, 8)
    near = [near_own] + [swap(near_own, place) for place in range(1, 4)]
    bias = enc_bias.reshape(-1, PAIR)
    first = swap(send_columns(block_ids, enc_weight[0], bias, 0, FIRST, EXTRA, 512), 4)
    depth = enc_weight.shape[1]
    rest = send_columns(block_ids, enc_weight[0], bias, FIRST, depth - FIRST, 0, 512)
    rest = swap(rest, 4)
    own = own_columns(block_ids, enc_weight[0])
    near[1], near[2], near[3], far_own, own = lax.optimization_barrier((near[1], near[2], near[3], far_own, own))
    columns = stage_decoder(block_ids, dec_weight[0])
    far = [far_own] + [swap(far_own, place) for place in range(1, 4)]

    partial = encode(block_ids, live, near, far, own, first, rest, bias)
    partial, columns = lax.optimization_barrier((partial, columns))
    acts = jnp.maximum(partial + across(partial), 0.0).astype(BF16).reshape(2, 2, BLOCK, TILE)

    ends = [(2 * i, 2 * (i ^ 4)) for i in range(owners)] + [(2 * i + 1, 2 * (i ^ 12) + 1) for i in range(owners)]
    along = lax.ppermute(acts, ("lat", "ckpt"), ends)
    middle = swap(acts, 8)

    def half(values):
        return lax.dynamic_slice_in_dim(values, core, 1, 0)

    payload = jnp.concatenate([half(acts), along, half(middle)], axis=0)
    mine = [payload] + [swap(payload, place) for place in range(1, 4)]
    theirs = [across(values) for values in mine]
    recon = decode(mine, theirs, columns, dec_bias.reshape(-1, 1))
    return recon[None]


def body(inputs, enc_weight, enc_bias, dec_weight, dec_bias, block_ids, live):
    tiles, owners = block_ids.shape
    cores = lax.axis_size("ckpt")
    if owners == 16 and cores == 2 and tiles == 4 and inputs.shape[:2] == (1, tiles * TILE // owners):
        return body_planes(inputs, enc_weight, enc_bias, dec_weight, dec_bias, block_ids, live)
    return body_any(inputs, enc_weight, enc_bias, dec_weight, dec_bias, block_ids, live)


def solution(mesh):
    placed = (
        P("ckpt", ("groups", "lat"), None),
        P("ckpt", None, "lat"),
        P("lat"),
        P("ckpt", "lat", None),
        P("ckpt", "lat"),
        P("groups", None),
        P("groups", None),
    )
    return jax.shard_map(
        body, mesh=mesh, in_specs=placed, out_specs=P("ckpt", "lat", "groups"), check_vma=False
    )
```

time: 208 us -> 60.7 us (0.29)
  waiting for transfers between devices: 127 us -> 24.1 us
  matrix products: 32.1 us -> 0 us
  local copies, waits for them, and re-layouts: 29.3 us -> 1.54 us
  starting transfers between devices: 0.26 us -> 19.3 us
  Pallas kernels: 0 us -> 15.3 us
  between operations: 13.2 us -> 0.13 us
  other arithmetic: 5.46 us -> 0.04 us
    all_gather x2 -> x0, waiting for transfers between devices: 100 us -> none  [the longest x1 81.6 us: body(): lax.all_gather(inputs, 'lat', axis=1, tiled=True)]
    dot_general x3 -> x0, matrix products: 32.1 us -> none  [the longest x1 15.3 us: body(): jnp.einsum('tnp,cdnpe->cdtne', onehot, grouped, preferred_element_type=jn...]
    psum x1 -> x0, waiting for transfers between devices: 26.1 us -> none  [body(): summed = lax.psum(preact, 'ckpt')]
    ppermute x0 -> x19, waiting for transfers between devices: none -> 24.1 us  [the longest x13 21.9 us: swap(): return lax.ppermute(values, 'lat', [(i, i ^ mask) for i in range(owners)])]
    unnamed x10 -> x14, local copies, waits for them, and re-layouts: 22.9 us -> 1.4 us
    ppermute x0 -> x19, starting transfers between devices: none -> 19.3 us  [the longest x13 17.3 us: swap(): return lax.ppermute(values, 'lat', [(i, i ^ mask) for i in range(owners)])]
    pallas_call x0 -> x6, Pallas kernels: none -> 15.3 us  [the longest x1 5.61 us: stage_decoder(): pl.pallas_call(stage_decoder_kernel, out_shape=jax.ShapeDtypeStruct((tile...]
    reshape x2 -> x1, local copies, waits for them, and re-layouts: 5.43 us -> 0.13 us  [body_planes(): recon = decode(mine, theirs, columns, dec_bias.reshape(-1, 1))]
  transfers between devices with their start and end apart: 3 -> 19, of which waited for: 3 -> 13; matrix products, arithmetic and copies ran while one was open for 18% -> 0% of each run, Pallas kernels for 0% -> 20%
where the time goes in v2:
time: 60.7 us; the launch traced here: 60.4 us
  waiting for transfers between devices  24.1 us (40%)
  starting transfers between devices  19.3 us (32%)
  Pallas kernels  15.3 us (25%)
  local copies, waits for them, and re-layouts  1.54 us (3%)
    ppermute x13, waiting for transfers between devices, swap(): return lax.ppermute(values, 'lat', [(i, i ^ mask) for i in range(owners)])  21.9 us
    ppermute x13, starting transfers between devices, swap(): return lax.ppermute(values, 'lat', [(i, i ^ mask) for i in range(owners)])  17.3 us
    pallas_call x1, Pallas kernels, stage_decoder(): pl.pallas_call(stage_decoder_kernel, out_shape=jax.ShapeDtypeStruct((tile...  5.61 us
    pallas_call x2, Pallas kernels, send_columns(): pl.pallas_call(functools.partial(send_columns_kernel, step=step, base=bas...  4.43 us
    pallas_call x1, Pallas kernels, own_columns(): pl.pallas_call(functools.partial(own_columns_kernel, step=step), out_shap...  2.22 us
    ppermute x5, waiting for transfers between devices, across(): return lax.ppermute(values, 'ckpt', [(0, 1), (1, 0)])  2.19 us
    pallas_call x1, Pallas kernels, decode(): pl.pallas_call(decode_kernel, out_shape=jax.ShapeDtypeStruct((features, t...  1.55 us
    pallas_call x1, Pallas kernels, encode(): pl.pallas_call(encode_kernel, out_shape=jax.ShapeDtypeStruct((4, BLOCK, T...  1.46 us
  transfers between devices with their start and end apart: 19, of which 13 were waited for; matrix products, arithmetic and copies ran while one was open for 0% of the time, Pallas kernels for 20%

profile of v2, /device:TPU:0, one launch (start us, length us, event | category | flops | bytes accessed | tf_op | source)
XLA Modules:
  0.0 60.4 jit_solution(17943660963388900508)
XLA Ops:
  0.0 4.0 %collective-permute-start.3 = (bf16[32,4096]{1,0:T(8,128)(2,1)}, bf16[32,4096]{1,0:T(8,128)(2,1)S(1)}, u32[]{:S(2)}, u32[]{:S(2)}) collective-permute-start(bf16[32,4096]{1,0:T(8,128)(2,1)} %bitcast.7), channel_id=1, source_target_pairs={{0,16},{2,18},{4,20},{6,22},{8,24},{10,26},{12,28},{14,30},{16,0},... | collective-permute-start | bytes 786440 | tf_op jit(solution)/shard_map/ppermute | solution.py:307
  4.0 0.7 %copy-done.1 = f32[2048]{0:T(1024)S(1)} copy-done((f32[2048]{0:T(1024)S(1)}, f32[2048]{0:T(1024)}, u32[]{:S(2)}) %copy-start.1) | copy-done | bytes 8216
  4.7 0.7 %copy-done.3 = s32[4,16]{1,0:T(4,128)S(1)} copy-done((s32[4,16]{1,0:T(4,128)S(1)}, s32[4,16]{1,0:T(4,128)}, u32[]{:S(2)}) %copy-start.3) | copy-done | bytes 280
  5.4 2.2 %send_columns.2 = bf16[2064,128]{1,0:T(8,128)(2,1)S(1)} custom-call(s32[4,16]{1,0:T(4,128)S(1)} %copy-done.3, bf16[4096,2048]{1,0:T(8,128)(2,1)} %bitcast.15, f32[16,128]{1,0:T(8,128)S(1)} %bitcast.12), custom_call_target="tpu_custom_call" | custom-call | bytes 1572864 | tf_op jit(solution)/shard_map/send_columns/pallas_call | solution.py:124
  7.6 1.6 %collective-permute-start.7 = (bf16[2064,128]{1,0:T(8,128)(2,1)S(1)}, bf16[2064,128]{1,0:T(8,128)(2,1)S(1)}, u32[]{:S(2)}, u32[]{:S(2)}) collective-permute-start(bf16[2064,128]{1,0:T(8,128)(2,1)S(1)} %send_columns.2), channel_id=1, source_target_pairs={{0,8},{2,10},{4,12},{6,14},{8,0},{10,2},{12,4},{14,6},{16,24},{18,... | collective-permute-start | bytes 1585160 | tf_op jit(solution)/shard_map/ppermute | solution.py:307
  9.3 2.4 %collective-permute-start.2 = (bf16[32,4096]{1,0:T(8,128)(2,1)S(1)}, bf16[32,4096]{1,0:T(8,128)(2,1)S(1)}, u32[]{:S(2)}, u32[]{:S(2)}) collective-permute-start(bf16[32,4096]{1,0:T(8,128)(2,1)S(1)} %bitcast.8), channel_id=1, source_target_pairs={{0,6},{2,4},{4,2},{6,0},{8,14},{10,12},{12,10},{14,8},{16,22},{18,... | collective-permute-start | bytes 786440 | tf_op jit(solution)/shard_map/ppermute | solution.py:307
  11.7 0.5 collective-permute-start.1
  12.2 0.5 collective-permute-start
  12.8 2.2 %send_columns.3 = bf16[2048,128]{1,0:T(8,128)(2,1)S(1)} custom-call(s32[4,16]{1,0:T(4,128)S(1)} %copy-done.4, bf16[4096,2048]{1,0:T(8,128)(2,1)} %bitcast.16, f32[16,128]{1,0:T(8,128)S(1)} %bitcast.13), custom_call_target="tpu_custom_call" | custom-call | bytes 1572864 | tf_op jit(solution)/shard_map/send_columns/pallas_call | solution.py:124
  15.0 1.3 %collective-permute-done.3.refs_4_ = bf16[32,4096]{1,0:T(8,128)(2,1)S(1)} collective-permute-done((bf16[32,4096]{1,0:T(8,128)(2,1)}, bf16[32,4096]{1,0:T(8,128)(2,1)S(1)}, u32[]{:S(2)}, u32[]{:S(2)}) %collective-permute-start.3) | collective-permute-done | bytes 262176 | tf_op jit(solution)/shard_map/ppermute | solution.py:307
  16.3 0.7 %collective-permute-start.8 = (bf16[2048,128]{1,0:T(8,128)(2,1)S(1)}, bf16[2048,128]{1,0:T(8,128)(2,1)S(1)}, u32[]{:S(2)}, u32[]{:S(2)}) collective-permute-start(bf16[2048,128]{1,0:T(8,128)(2,1)S(1)} %send_columns.3), channel_id=1, source_target_pairs={{0,8},{2,10},{4,12},{6,14},{8,0},{10,2},{12,4},{14,6},{16,24},{18,... | collective-permute-start | bytes 1572872 | tf_op jit(solution)/shard_map/ppermute | solution.py:307
  17.0 2.2 %own_columns.1.refs_8_ = bf16[2,4096,128]{2,1,0:T(8,128)(2,1)S(1)} custom-call(s32[4,16]{1,0:T(4,128)S(1)} %copy-done.4, bf16[4096,2048]{1,0:T(8,128)(2,1)} %bitcast.17), custom_call_target="tpu_custom_call" | custom-call | bytes 4194304 | tf_op jit(solution)/shard_map/own_columns/pallas_call | solution.py:155
  19.5 3.8 %collective-permute-done.1.refs_2_ = bf16[32,4096]{1,0:T(8,128)(2,1)S(1)} collective-permute-done((bf16[32,4096]{1,0:T(8,128)(2,1)S(1)}, bf16[32,4096]{1,0:T(8,128)(2,1)S(1)}, u32[]{:S(2)}, u32[]{:S(2)}) %collective-permute-start.1) | collective-permute-done | bytes 262176 | tf_op jit(solution)/shard_map/ppermute | solution.py:307
  23.4 1.6 %collective-permute-start.6 = (bf16[32,4096]{1,0:T(8,128)(2,1)S(1)}, bf16[32,4096]{1,0:T(8,128)(2,1)S(1)}, u32[]{:S(2)}, u32[]{:S(2)}) collective-permute-start(bf16[32,4096]{1,0:T(8,128)(2,1)S(1)} %collective-permute-done.3.refs_4_), channel_id=1, source_target_pairs={{0,6},{2,4},{4,2},{6,0},{8,14},{10,12},{12,10},{14,8},{16,22},{18,... | collective-permute-start | bytes 786440 | tf_op jit(solution)/shard_map/ppermute | solution.py:307
  25.0 1.3 %collective-permute-start.5 = (bf16[32,4096]{1,0:T(8,128)(2,1)S(1)}, bf16[32,4096]{1,0:T(8,128)(2,1)S(1)}, u32[]{:S(2)}, u32[]{:S(2)}) collective-permute-start(bf16[32,4096]{1,0:T(8,128)(2,1)S(1)} %collective-permute-done.3.refs_4_), channel_id=1, source_target_pairs={{0,4},{2,6},{4,0},{6,2},{8,12},{10,14},{12,8},{14,10},{16,20},{18,... | collective-permute-start | bytes 786440 | tf_op jit(solution)/shard_map/ppermute | solution.py:307
  26.3 0.5 collective-permute-start.4
  26.9 5.6 %stage_decoder.1.refs_8_ = bf16[4,256,1024]{2,1,0:T(8,128)(2,1)S(1)} custom-call(s32[4,16]{1,0:T(4,128)S(1)} %copy-done.4, bf16[256,32768]{1,0:T(8,128)(2,1)} %bitcast.18), custom_call_target="tpu_custom_call" | custom-call | bytes 6291456 | tf_op jit(solution)/shard_map/stage_decoder/pallas_call | solution.py:239
  32.5 4.4 %collective-permute-done.8.refs_10_ = bf16[2048,128]{1,0:T(8,128)(2,1)S(1)} collective-permute-done((bf16[2048,128]{1,0:T(8,128)(2,1)S(1)}, bf16[2048,128]{1,0:T(8,128)(2,1)S(1)}, u32[]{:S(2)}, u32[]{:S(2)}) %collective-permute-start.8) | collective-permute-done | bytes 524320 | tf_op jit(solution)/shard_map/ppermute | solution.py:307
  36.9 1.1 %collective-permute-done.5.refs_6_ = bf16[32,4096]{1,0:T(8,128)(2,1)S(1)} collective-permute-done((bf16[32,4096]{1,0:T(8,128)(2,1)S(1)}, bf16[32,4096]{1,0:T(8,128)(2,1)S(1)}, u32[]{:S(2)}, u32[]{:S(2)}) %collective-permute-start.5) | collective-permute-done | bytes 262176 | tf_op jit(solution)/shard_map/ppermute | solution.py:307
  38.1 1.5 %encode.1 = f32[4,64,128]{2,1,0:T(8,128)S(1)} custom-call(s32[4,16]{1,0:T(4,128)S(1)} %copy-done.4, s32[4,16]{1,0:T(4,128)S(1)} %copy-done.5, bf16[32,4096]{1,0:T(8,128)(2,1)S(1)} %bitcast.11, bf16[32,4096]{1,0:T(8,128)(2,1)S(1)} %collective-permute-done.refs_1_, bf16[32,4096]{1,0:T(8,128)(2,1)S(1)} %collective-permute-done.1.refs_2_, ...), custom_call_target="tpu_custom_call" | custom-call | flops 536870912 | bytes 5242880 | tf_op jit(solution)/shard_map/encode/pallas_call | solution.py:200
  39.7 1.3 %collective-permute-done.9 = f32[4,64,128]{2,1,0:T(8,128)S(1)} collective-permute-done((f32[4,64,128]{2,1,0:T(8,128)S(1)}, f32[4,64,128]{2,1,0:T(8,128)S(1)}, u32[]{:S(2)}, u32[]{:S(2)}) %collective-permute-start.9) | collective-permute-done | bytes 131104 | tf_op jit(solution)/shard_map/ppermute | solution.py:310
  41.1 0.4 collective-permute-start.11
  41.5 1.4 %collective-permute-start.10 = (bf16[2,2,64,128]{3,2,1,0:T(8,128)(2,1)S(1)}, bf16[2,2,64,128]{3,2,1,0:T(8,128)(2,1)S(1)}, u32[]{:S(2)}, u32[]{:S(2)}) collective-permute-start(bf16[2,2,64,128]{3,2,1,0:T(8,128)(2,1)S(1)} %bitcast.20), channel_id=1, source_target_pairs={{0,8},{2,10},{4,12},{6,14},{8,0},{10,2},{12,4},{14,6},{16,24},{18,... | collective-permute-start | bytes 196616 | tf_op jit(solution)/shard_map/ppermute | solution.py:330
  42.9 5.4 %collective-permute-done.11 = bf16[2,2,64,128]{3,2,1,0:T(8,128)(2,1)S(1)} collective-permute-done((bf16[2,2,64,128]{3,2,1,0:T(8,128)(2,1)S(1)}, bf16[2,2,64,128]{3,2,1,0:T(8,128)(2,1)S(1)}, u32[]{:S(2)}, u32[]{:S(2)}) %collective-permute-start.11) | collective-permute-done | bytes 65568 | tf_op jit(solution)/shard_map/ppermute | solution.py:307
  48.3 1.5 %collective-permute-start.14 = (bf16[4,2,64,128]{3,2,1,0:T(8,128)(2,1)S(1)}, bf16[4,2,64,128]{3,2,1,0:T(8,128)(2,1)S(1)}, u32[]{:S(2)}, u32[]{:S(2)}) collective-permute-start(bf16[4,2,64,128]{3,2,1,0:T(8,128)(2,1)S(1)} %pad_maximum_fusion.refs_0_), channel_id=1, source_target_pairs={{0,6},{2,4},{4,2},{6,0},{8,14},{10,12},{12,10},{14,8},{16,22},{18,... | collective-permute-start | bytes 393224 | tf_op jit(solution)/shard_map/ppermute | solution.py:307
  49.8 1.4 %collective-permute-start.13 = (bf16[4,2,64,128]{3,2,1,0:T(8,128)(2,1)S(1)}, bf16[4,2,64,128]{3,2,1,0:T(8,128)(2,1)S(1)}, u32[]{:S(2)}, u32[]{:S(2)}) collective-permute-start(bf16[4,2,64,128]{3,2,1,0:T(8,128)(2,1)S(1)} %pad_maximum_fusion.refs_0_), channel_id=1, source_target_pairs={{0,4},{2,6},{4,0},{6,2},{8,12},{10,14},{12,8},{14,10},{16,20},{18,... | collective-permute-start | bytes 393224 | tf_op jit(solution)/shard_map/ppermute | solution.py:307
  51.2 0.6 %collective-permute-start.12 = (bf16[4,2,64,128]{3,2,1,0:T(8,128)(2,1)S(1)}, bf16[4,2,64,128]{3,2,1,0:T(8,128)(2,1)S(1)}, u32[]{:S(2)}, u32[]{:S(2)}) collective-permute-start(bf16[4,2,64,128]{3,2,1,0:T(8,128)(2,1)S(1)} %pad_maximum_fusion.refs_0_), channel_id=1, source_target_pairs={{0,2},{2,0},{4,6},{6,4},{8,10},{10,8},{12,14},{14,12},{16,18},{18,... | collective-permute-start | bytes 393224 | tf_op jit(solution)/shard_map/ppermute | solution.py:307
  51.9 3.8 %collective-permute-done.14.refs_3_ = bf16[4,2,64,128]{3,2,1,0:T(8,128)(2,1)S(1)} collective-permute-done((bf16[4,2,64,128]{3,2,1,0:T(8,128)(2,1)S(1)}, bf16[4,2,64,128]{3,2,1,0:T(8,128)(2,1)S(1)}, u32[]{:S(2)}, u32[]{:S(2)}) %collective-permute-start.14) | collective-permute-done | bytes 131104 | tf_op jit(solution)/shard_map/ppermute | solution.py:307
  55.6 1.7 %collective-permute-done.13.refs_2_ = bf16[4,2,64,128]{3,2,1,0:T(8,128)(2,1)S(1)} collective-permute-done((bf16[4,2,64,128]{3,2,1,0:T(8,128)(2,1)S(1)}, bf16[4,2,64,128]{3,2,1,0:T(8,128)(2,1)S(1)}, u32[]{:S(2)}, u32[]{:S(2)}) %collective-permute-start.13) | collective-permute-done | bytes 131104 | tf_op jit(solution)/shard_map/ppermute | solution.py:307
  57.4 0.5 collective-permute-start.16
  58.0 0.7 %collective-permute-done.17.refs_6_ = bf16[4,2,64,128]{3,2,1,0:T(8,128)(2,1)S(1)} collective-permute-done((bf16[4,2,64,128]{3,2,1,0:T(8,128)(2,1)S(1)}, bf16[4,2,64,128]{3,2,1,0:T(8,128)(2,1)S(1)}, u32[]{:S(2)}, u32[]{:S(2)}) %collective-permute-start.17) | collective-permute-done | bytes 131104 | tf_op jit(solution)/shard_map/ppermute | solution.py:310
  58.9 1.5 %decode.1 = bf16[256,512]{1,0:T(8,128)(2,1)} custom-call(bf16[4,2,64,128]{3,2,1,0:T(8,128)(2,1)S(1)} %pad_maximum_fusion.refs_0_, bf16[4,2,64,128]{3,2,1,0:T(8,128)(2,1)S(1)} %collective-permute-done.12.refs_1_, bf16[4,2,64,128]{3,2,1,0:T(8,128)(2,1)S(1)} %collective-permute-done.13.refs_2_, bf16[4,2,64,128]{3,2,1,0:T(8,128)(2,1)S(1)} %collective-permute-done.14.refs_3_, ...), custom_call_target="tpu_custom_call" | custom-call | flops 268435456 | bytes 4194304 | tf_op jit(solution)/shard_map/decode/pallas_call | solution.py:286
  (31 shorter events, 0.9 us)
Async XLA Ops:
  0.0 9.3 %copy-start = (bf16[1,32,4096]{2,1,0:T(8,128)(2,1)S(1)}, bf16[1,32,4096]{2,1,0:T(8,128)(2,1)}, u32[]{:S(2)}) copy-start(bf16[1,32,4096]{2,1,0:T(8,128)(2,1)} %param.7) | copy-start | bytes 786436
  0.0 16.3 %collective-permute-start.3 = (bf16[32,4096]{1,0:T(8,128)(2,1)}, bf16[32,4096]{1,0:T(8,128)(2,1)S(1)}, u32[]{:S(2)}, u32[]{:S(2)}) collective-permute-start(bf16[32,4096]{1,0:T(8,128)(2,1)} %bitcast.7), channel_id=1, source_target_pairs={{0,16},{2,18},{4,20},{6,22},{8,24},{10,26},{12,28},{14,30},{16,0},... | collective-permute-start | bytes 786440 | tf_op jit(solution)/shard_map/ppermute | solution.py:307
  4.0 0.7 %copy-start.1 = (f32[2048]{0:T(1024)S(1)}, f32[2048]{0:T(1024)}, u32[]{:S(2)}) copy-start(f32[2048]{0:T(1024)} %param.9) | copy-start | bytes 24580
  4.7 0.7 %copy-start.3 = (s32[4,16]{1,0:T(4,128)S(1)}, s32[4,16]{1,0:T(4,128)}, u32[]{:S(2)}) copy-start(s32[4,16]{1,0:T(4,128)} %ids_ref.9) | copy-start | bytes 772
  5.4 7.4 %copy-start.2 = (f32[2048]{0:T(1024)S(1)}, f32[2048]{0:T(1024)}, u32[]{:S(2)}) copy-start(f32[2048]{0:T(1024)} %param.9) | copy-start | bytes 24580
  5.4 7.4 %copy-start.4 = (s32[4,16]{1,0:T(4,128)S(1)}, s32[4,16]{1,0:T(4,128)}, u32[]{:S(2)}) copy-start(s32[4,16]{1,0:T(4,128)} %ids_ref.9) | copy-start | bytes 772
  7.6 30.5 %collective-permute-start.7 = (bf16[2064,128]{1,0:T(8,128)(2,1)S(1)}, bf16[2064,128]{1,0:T(8,128)(2,1)S(1)}, u32[]{:S(2)}, u32[]{:S(2)}) collective-permute-start(bf16[2064,128]{1,0:T(8,128)(2,1)S(1)} %send_columns.2), channel_id=1, source_target_pairs={{0,8},{2,10},{4,12},{6,14},{8,0},{10,2},{12,4},{14,6},{16,24},{18,... | collective-permute-start | bytes 1585160 | tf_op jit(solution)/shard_map/ppermute | solution.py:307
  9.3 10.2 %collective-permute-start.2 = (bf16[32,4096]{1,0:T(8,128)(2,1)S(1)}, bf16[32,4096]{1,0:T(8,128)(2,1)S(1)}, u32[]{:S(2)}, u32[]{:S(2)}) collective-permute-start(bf16[32,4096]{1,0:T(8,128)(2,1)S(1)} %bitcast.8), channel_id=1, source_target_pairs={{0,6},{2,4},{4,2},{6,0},{8,14},{10,12},{12,10},{14,8},{16,22},{18,... | collective-permute-start | bytes 786440 | tf_op jit(solution)/shard_map/ppermute | solution.py:307
  11.7 11.6 %collective-permute-start.1 = (bf16[32,4096]{1,0:T(8,128)(2,1)S(1)}, bf16[32,4096]{1,0:T(8,128)(2,1)S(1)}, u32[]{:S(2)}, u32[]{:S(2)}) collective-permute-start(bf16[32,4096]{1,0:T(8,128)(2,1)S(1)} %bitcast.9), channel_id=1, source_target_pairs={{0,4},{2,6},{4,0},{6,2},{8,12},{10,14},{12,8},{14,10},{16,20},{18,... | collective-permute-start | bytes 786440 | tf_op jit(solution)/shard_map/ppermute | solution.py:307
  12.2 11.1 %collective-permute-start = (bf16[32,4096]{1,0:T(8,128)(2,1)S(1)}, bf16[32,4096]{1,0:T(8,128)(2,1)S(1)}, u32[]{:S(2)}, u32[]{:S(2)}) collective-permute-start(bf16[32,4096]{1,0:T(8,128)(2,1)S(1)} %bitcast.10), channel_id=1, source_target_pairs={{0,2},{2,0},{4,6},{6,4},{8,10},{10,8},{12,14},{14,12},{16,18},{18,... | collective-permute-start | bytes 786440 | tf_op jit(solution)/shard_map/ppermute | solution.py:307
  15.0 23.1 %copy-start.5 = (s32[4,16]{1,0:T(4,128)S(1)}, s32[4,16]{1,0:T(4,128)}, u32[]{:S(2)}) copy-start(s32[4,16]{1,0:T(4,128)} %live_ref.1) | copy-start | bytes 772
  16.3 20.6 %collective-permute-start.8 = (bf16[2048,128]{1,0:T(8,128)(2,1)S(1)}, bf16[2048,128]{1,0:T(8,128)(2,1)S(1)}, u32[]{:S(2)}, u32[]{:S(2)}) collective-permute-start(bf16[2048,128]{1,0:T(8,128)(2,1)S(1)} %send_columns.3), channel_id=1, source_target_pairs={{0,8},{2,10},{4,12},{6,14},{8,0},{10,2},{12,4},{14,6},{16,24},{18,... | collective-permute-start | bytes 1572872 | tf_op jit(solution)/shard_map/ppermute | solution.py:307
  19.3 38.6 %copy-start.6 = (f32[1,256]{1,0:T(1,128)S(1)}, f32[1,256]{1,0:T(1,128)}, u32[]{:S(2)}) copy-start(f32[1,256]{1,0:T(1,128)} %param.11) | copy-start | bytes 3076
  23.4 13.5 %collective-permute-start.6 = (bf16[32,4096]{1,0:T(8,128)(2,1)S(1)}, bf16[32,4096]{1,0:T(8,128)(2,1)S(1)}, u32[]{:S(2)}, u32[]{:S(2)}) collective-permute-start(bf16[32,4096]{1,0:T(8,128)(2,1)S(1)} %collective-permute-done.3.refs_4_), channel_id=1, source_target_pairs={{0,6},{2,4},{4,2},{6,0},{8,14},{10,12},{12,10},{14,8},{16,22},{18,... | collective-permute-start | bytes 786440 | tf_op jit(solution)/shard_map/ppermute | solution.py:307
  25.0 13.0 %collective-permute-start.5 = (bf16[32,4096]{1,0:T(8,128)(2,1)S(1)}, bf16[32,4096]{1,0:T(8,128)(2,1)S(1)}, u32[]{:S(2)}, u32[]{:S(2)}) collective-permute-start(bf16[32,4096]{1,0:T(8,128)(2,1)S(1)} %collective-permute-done.3.refs_4_), channel_id=1, source_target_pairs={{0,4},{2,6},{4,0},{6,2},{8,12},{10,14},{12,8},{14,10},{16,20},{18,... | collective-permute-start | bytes 786440 | tf_op jit(solution)/shard_map/ppermute | solution.py:307
  26.3 11.8 %collective-permute-start.4 = (bf16[32,4096]{1,0:T(8,128)(2,1)S(1)}, bf16[32,4096]{1,0:T(8,128)(2,1)S(1)}, u32[]{:S(2)}, u32[]{:S(2)}) collective-permute-start(bf16[32,4096]{1,0:T(8,128)(2,1)S(1)} %collective-permute-done.3.refs_4_), channel_id=1, source_target_pairs={{0,2},{2,0},{4,6},{6,4},{8,10},{10,8},{12,14},{14,12},{16,18},{18,... | collective-permute-start | bytes 786440 | tf_op jit(solution)/shard_map/ppermute | solution.py:307
  39.6 1.4 %collective-permute-start.9 = (f32[4,64,128]{2,1,0:T(8,128)S(1)}, f32[4,64,128]{2,1,0:T(8,128)S(1)}, u32[]{:S(2)}, u32[]{:S(2)}) collective-permute-start(f32[4,64,128]{2,1,0:T(8,128)S(1)} %encode.1), channel_id=1, source_target_pairs={{0,1},{1,0},{2,3},{3,2},{4,5},{5,4},{6,7},{7,6},{8,9},{9,8},{10,11... | collective-permute-start | bytes 393224 | tf_op jit(solution)/shard_map/ppermute | solution.py:310
  41.1 7.2 %collective-permute-start.11 = (bf16[2,2,64,128]{3,2,1,0:T(8,128)(2,1)S(1)}, bf16[2,2,64,128]{3,2,1,0:T(8,128)(2,1)S(1)}, u32[]{:S(2)}, u32[]{:S(2)}) collective-permute-start(bf16[2,2,64,128]{3,2,1,0:T(8,128)(2,1)S(1)} %bitcast.19), channel_id=1, source_target_pairs={{0,16},{2,18},{4,20},{6,22},{8,24},{10,26},{12,28},{14,30},{16,0},... | collective-permute-start | bytes 196616 | tf_op jit(solution)/shard_map/ppermute | solution.py:307
  41.5 6.8 %collective-permute-start.10 = (bf16[2,2,64,128]{3,2,1,0:T(8,128)(2,1)S(1)}, bf16[2,2,64,128]{3,2,1,0:T(8,128)(2,1)S(1)}, u32[]{:S(2)}, u32[]{:S(2)}) collective-permute-start(bf16[2,2,64,128]{3,2,1,0:T(8,128)(2,1)S(1)} %bitcast.20), channel_id=1, source_target_pairs={{0,8},{2,10},{4,12},{6,14},{8,0},{10,2},{12,4},{14,6},{16,24},{18,... | collective-permute-start | bytes 196616 | tf_op jit(solution)/shard_map/ppermute | solution.py:330
  48.3 7.3 %collective-permute-start.14 = (bf16[4,2,64,128]{3,2,1,0:T(8,128)(2,1)S(1)}, bf16[4,2,64,128]{3,2,1,0:T(8,128)(2,1)S(1)}, u32[]{:S(2)}, u32[]{:S(2)}) collective-permute-start(bf16[4,2,64,128]{3,2,1,0:T(8,128)(2,1)S(1)} %pad_maximum_fusion.refs_0_), channel_id=1, source_target_pairs={{0,6},{2,4},{4,2},{6,0},{8,14},{10,12},{12,10},{14,8},{16,22},{18,... | collective-permute-start | bytes 393224 | tf_op jit(solution)/shard_map/ppermute | solution.py:307
  49.8 7.6 %collective-permute-start.13 = (bf16[4,2,64,128]{3,2,1,0:T(8,128)(2,1)S(1)}, bf16[4,2,64,128]{3,2,1,0:T(8,128)(2,1)S(1)}, u32[]{:S(2)}, u32[]{:S(2)}) collective-permute-start(bf16[4,2,64,128]{3,2,1,0:T(8,128)(2,1)S(1)} %pad_maximum_fusion.refs_0_), channel_id=1, source_target_pairs={{0,4},{2,6},{4,0},{6,2},{8,12},{10,14},{12,8},{14,10},{16,20},{18,... | collective-permute-start | bytes 393224 | tf_op jit(solution)/shard_map/ppermute | solution.py:307
  51.2 6.1 %collective-permute-start.12 = (bf16[4,2,64,128]{3,2,1,0:T(8,128)(2,1)S(1)}, bf16[4,2,64,128]{3,2,1,0:T(8,128)(2,1)S(1)}, u32[]{:S(2)}, u32[]{:S(2)}) collective-permute-start(bf16[4,2,64,128]{3,2,1,0:T(8,128)(2,1)S(1)} %pad_maximum_fusion.refs_0_), channel_id=1, source_target_pairs={{0,2},{2,0},{4,6},{6,4},{8,10},{10,8},{12,14},{14,12},{16,18},{18,... | collective-permute-start | bytes 393224 | tf_op jit(solution)/shard_map/ppermute | solution.py:307
  51.9 6.2 %collective-permute-start.15 = (bf16[4,2,64,128]{3,2,1,0:T(8,128)(2,1)S(1)}, bf16[4,2,64,128]{3,2,1,0:T(8,128)(2,1)S(1)}, u32[]{:S(2)}, u32[]{:S(2)}) collective-permute-start(bf16[4,2,64,128]{3,2,1,0:T(8,128)(2,1)S(1)} %pad_maximum_fusion.refs_0_), channel_id=1, source_target_pairs={{0,1},{1,0},{2,3},{3,2},{4,5},{5,4},{6,7},{7,6},{8,9},{9,8},{10,11... | collective-permute-start | bytes 393224 | tf_op jit(solution)/shard_map/ppermute | solution.py:310
  55.6 2.4 %collective-permute-start.18 = (bf16[4,2,64,128]{3,2,1,0:T(8,128)(2,1)S(1)}, bf16[4,2,64,128]{3,2,1,0:T(8,128)(2,1)S(1)}, u32[]{:S(2)}, u32[]{:S(2)}) collective-permute-start(bf16[4,2,64,128]{3,2,1,0:T(8,128)(2,1)S(1)} %collective-permute-done.14.refs_3_), channel_id=1, source_target_pairs={{0,1},{1,0},{2,3},{3,2},{4,5},{5,4},{6,7},{7,6},{8,9},{9,8},{10,11... | collective-permute-start | bytes 393224 | tf_op jit(solution)/shard_map/ppermute | solution.py:310
  57.4 1.3 %collective-permute-start.17 = (bf16[4,2,64,128]{3,2,1,0:T(8,128)(2,1)S(1)}, bf16[4,2,64,128]{3,2,1,0:T(8,128)(2,1)S(1)}, u32[]{:S(2)}, u32[]{:S(2)}) collective-permute-start(bf16[4,2,64,128]{3,2,1,0:T(8,128)(2,1)S(1)} %collective-permute-done.13.refs_2_), channel_id=1, source_target_pairs={{0,1},{1,0},{2,3},{3,2},{4,5},{5,4},{6,7},{7,6},{8,9},{9,8},{10,11... | collective-permute-start | bytes 393224 | tf_op jit(solution)/shard_map/ppermute | solution.py:310
  57.4 1.5 %collective-permute-start.16 = (bf16[4,2,64,128]{3,2,1,0:T(8,128)(2,1)S(1)}, bf16[4,2,64,128]{3,2,1,0:T(8,128)(2,1)S(1)}, u32[]{:S(2)}, u32[]{:S(2)}) collective-permute-start(bf16[4,2,64,128]{3,2,1,0:T(8,128)(2,1)S(1)} %collective-permute-done.12.refs_1_), channel_id=1, source_target_pairs={{0,1},{1,0},{2,3},{3,2},{4,5},{5,4},{6,7},{7,6},{8,9},{9,8},{10,11... | collective-permute-start | bytes 393224 | tf_op jit(solution)/shard_map/ppermute | solution.py:310

commit v3 on v2

--- a/solution.py
+++ b/solution.py
@@ -11,7 +11,7 @@
 TILE = 128
 PAIR = 2 * BLOCK
 EXTRA = 16
-FIRST = 2048
+FIRST = 1024
 F32 = jnp.float32
 BF16 = jnp.bfloat16
 VMEM_WEIGHTS = 50 * 1024 * 1024
@@ -83,12 +83,13 @@
     return pl.CostEstimate(flops=flops, bytes_accessed=moved, transcendentals=0)
 
 
-def send_columns_kernel(ids_ref, weight_ref, bias_ref, out_ref, in_ref, sems, *, step, base):
+def send_columns_kernel(ids_ref, weight_ref, *refs, step, base):
+    *bias_refs, out_ref, in_ref, sems = refs
     lat = lax.axis_index("lat")
     plane = lat // 4
     depth = in_ref.shape[1]
     chunks = depth // step
-    extra = out_ref.shape[0] - depth
+    folded = out_ref.shape[1] > PAIR
     blocks = [ids_ref[plane ^ mask, lat] for mask in (1, 3)]
     odds = [block % 2 for block in blocks]
 
@@ -100,7 +101,9 @@
         for which in range(2):
             fetch(chunk, which).start()
 
-    if extra:
+    if bias_refs:
+        (bias_ref,) = bias_refs
+        extra = out_ref.shape[0] - depth
         parts = [bias_ref[pl.ds(block // 2, 1), :] for block in blocks]
         bias = side_by_side(parts[0], odds[0], parts[1], odds[1])
         high = bias.astype(BF16)
@@ -117,20 +120,27 @@
             fetch(chunk, which).wait()
         rows = slice(chunk * step, (chunk + 1) * step)
         both = side_by_side(in_ref[0, rows, :].astype(F32), odds[0], in_ref[1, rows, :].astype(F32), odds[1])
-        out_ref[rows, :] = both.astype(BF16)
-
-
-def send_columns(ids, enc_weight, bias, base, depth, extra, step):
+        both = both.astype(BF16)
+        if folded:
+            high = out_ref.shape[0]
+            for piece in range(step // high):
+                left = (chunk * (step // high) + piece) * PAIR
+                out_ref[:, left : left + PAIR] = both[piece * high : (piece + 1) * high, :]
+        else:
+            out_ref[rows, :] = both
+
+
+def send_columns(ids, enc_weight, bias, base, depth, shape, step):
     return pl.pallas_call(
         functools.partial(send_columns_kernel, step=step, base=base),
-        out_shape=jax.ShapeDtypeStruct((depth + extra, PAIR), BF16),
-        in_specs=[SMEM, ANY, VMEM],
+        out_shape=jax.ShapeDtypeStruct(shape, BF16),
+        in_specs=[SMEM, ANY] + [VMEM] * len(bias),
         out_specs=VMEM,
         scratch_shapes=[pltpu.VMEM((2, depth, PAIR), BF16), pltpu.SemaphoreType.DMA((2, depth // step))],
         compiler_params=params(),
         cost_estimate=cost(0, 3 * depth * PAIR * 2),
         name="send_columns",
-    )(ids, enc_weight, bias)
+    )(ids, enc_weight, *bias)
 
 
 def own_columns_kernel(ids_ref, weight_ref, out_ref, sems, *, step):
@@ -173,13 +183,17 @@
     depth = own_ref.shape[1]
     shard = TILE // 4
     step = 1024
-    parts = first_ref[FIRST:, :].astype(F32)
+    parts = rest_ref[depth - FIRST :, :].astype(F32)
     other_bias = (parts[0:1] + parts[1:2]) + parts[2:3]
     for index, tokens in enumerate((near, far)):
         total = jnp.zeros((TILE, 2 * PAIR), F32)
         for start in range(0, depth, step):
             rows = jnp.concatenate([ref[:, start : start + step] for ref in tokens], axis=0)
-            partner = first_ref[start : start + step, :] if start < FIRST else rest_ref[start - FIRST : start - FIRST + step, :]
+            if start < FIRST:
+                pieces = range(start // shard, (start + step) // shard)
+                partner = jnp.concatenate([first_ref[:, i * PAIR : (i + 1) * PAIR] for i in pieces], axis=0)
+            else:
+                partner = rest_ref[start - FIRST : start - FIRST + step, :]
             columns = jnp.concatenate([own_ref[index, start : start + step, :], partner], axis=1)
             total += jnp.dot(rows, columns, preferred_element_type=F32)
         tile = plane ^ (2 * index)
@@ -310,15 +324,26 @@
         return lax.ppermute(values, "ckpt", [(0, 1), (1, 0)])
 
     near_own = inputs[0]
-    far_own = swap(near_own, 8)
     near = [near_own] + [swap(near_own, place) for place in range(1, 4)]
     bias = enc_bias.reshape(-1, PAIR)
-    first = swap(send_columns(block_ids, enc_weight[0], bias, 0, FIRST, EXTRA, 512), 4)
     depth = enc_weight.shape[1]
-    rest = send_columns(block_ids, enc_weight[0], bias, FIRST, depth - FIRST, 0, 512)
+    first = send_columns(block_ids, enc_weight[0], [], 0, FIRST, near_own.shape, 256)
+    plane = lax.axis_index("lat") // 4
+    at_end = (plane == 0) | (plane == 3)
+
+    def rotate(values, end_mask, middle_mask):
+        pairs = [(i, i ^ (end_mask if i // 4 in (0, 3) else middle_mask)) for i in range(owners)]
+        return lax.ppermute(values, "lat", pairs)
+
+    one = rotate(jnp.where(at_end, first, near_own), 4, 8)
+    two = rotate(jnp.where(at_end, near_own, first), 8, 4)
+    rest = send_columns(block_ids, enc_weight[0], [bias], FIRST, depth - FIRST, (depth - FIRST + EXTRA, PAIR), 512)
+    rest, one = lax.optimization_barrier((rest, one))
     rest = swap(rest, 4)
+    far_own = jnp.where(at_end, one, two)
+    first = jnp.where(at_end, two, one)
     own = own_columns(block_ids, enc_weight[0])
-    near[1], near[2], near[3], far_own, own = lax.optimization_barrier((near[1], near[2], near[3], far_own, own))
+    far_own, own = lax.optimization_barrier((far_own, own))
     columns = stage_decoder(block_ids, dec_weight[0])
     far = [far_own] + [swap(far_own, place) for place in range(1, 4)]
 
@@ -328,12 +353,9 @@
 
     ends = [(2 * i, 2 * (i ^ 4)) for i in range(owners)] + [(2 * i + 1, 2 * (i ^ 12) + 1) for i in range(owners)]
     along = lax.ppermute(acts, ("lat", "ckpt"), ends)
-    middle = swap(acts, 8)
-
-    def half(values):
-        return lax.dynamic_slice_in_dim(values, core, 1, 0)
-
-    payload = jnp.concatenate([half(acts), along, half(middle)], axis=0)
+    mine_half = lax.dynamic_slice_in_dim(acts, core, 1, 0)
+    middle = swap(mine_half, 8)
+    payload = jnp.concatenate([mine_half, along, middle], axis=0)
     mine = [payload] + [swap(payload, place) for place in range(1, 4)]
     theirs = [across(values) for values in mine]
     recon = decode(mine, theirs, columns, dec_bias.reshape(-1, 1))

time: 60.7 us -> 58.5 us (0.964)
  waiting for transfers between devices: 24.1 us -> 18.5 us
  starting transfers between devices: 19.3 us -> 23.1 us
  local copies, waits for them, and re-layouts: 1.54 us -> 0.88 us
    ppermute x13 -> x11, waiting for transfers between devices: 21.9 us -> 16.3 us  [swap(): return lax.ppermute(values, 'lat', [(i, i ^ mask) for i in range(owners)])]
    ppermute x0 -> x2, starting transfers between devices: none -> 4.11 us  [rotate(): return lax.ppermute(values, 'lat', pairs)]
    unnamed x14 -> x10, local copies, waits for them, and re-layouts: 1.4 us -> 0.74 us
    ppermute x13 -> x11, starting transfers between devices: 17.3 us -> 17.6 us  [swap(): return lax.ppermute(values, 'lat', [(i, i ^ mask) for i in range(owners)])]
  transfers between devices with their start and end apart: 19 -> 19, of which waited for: 13 -> 9; matrix products, arithmetic and copies ran while one was open for 0% -> 0% of each run, Pallas kernels for 20% -> 18%
where the time goes in v3:
time: 58.5 us; the launch traced here: 58.2 us
  starting transfers between devices  23.1 us (39%)
  waiting for transfers between devices  18.5 us (32%)
  Pallas kernels  15.4 us (26%)
  local copies, waits for them, and re-layouts  0.88 us (2%)
    ppermute x11, starting transfers between devices, swap(): return lax.ppermute(values, 'lat', [(i, i ^ mask) for i in range(owners)])  17.6 us
    ppermute x11, waiting for transfers between devices, swap(): return lax.ppermute(values, 'lat', [(i, i ^ mask) for i in range(owners)])  16.3 us
    pallas_call x1, Pallas kernels, stage_decoder(): pl.pallas_call(stage_decoder_kernel, out_shape=jax.ShapeDtypeStruct((tile...  5.61 us
    pallas_call x2, Pallas kernels, send_columns(): pl.pallas_call(functools.partial(send_columns_kernel, step=step, base=bas...  4.56 us
    ppermute x2, starting transfers between devices, rotate(): return lax.ppermute(values, 'lat', pairs)  4.11 us
    pallas_call x1, Pallas kernels, own_columns(): pl.pallas_call(functools.partial(own_columns_kernel, step=step), out_shap...  2.22 us
    ppermute x5, waiting for transfers between devices, across(): return lax.ppermute(values, 'ckpt', [(0, 1), (1, 0)])  2.2 us
    pallas_call x1, Pallas kernels, decode(): pl.pallas_call(decode_kernel, out_shape=jax.ShapeDtypeStruct((features, t...  1.55 us
  transfers between devices with their start and end apart: 19, of which 9 were waited for; matrix products, arithmetic and copies ran while one was open for 0% of the time, Pallas kernels for 18%

profile of v3, /device:TPU:0, one launch (start us, length us, event | category | flops | bytes accessed | tf_op | source)
XLA Modules:
  0.0 58.2 jit_solution(13082940597868574964)
XLA Ops:
  0.0 0.7 %copy-done.1 = s32[4,16]{1,0:T(4,128)S(1)} copy-done((s32[4,16]{1,0:T(4,128)S(1)}, s32[4,16]{1,0:T(4,128)}, u32[]{:S(2)}) %copy-start.1) | copy-done | bytes 280
  0.7 2.0 %send_columns.3 = bf16[32,4096]{1,0:T(8,128)(2,1)S(1)} custom-call(s32[4,16]{1,0:T(4,128)S(1)} %copy-done.1, bf16[4096,2048]{1,0:T(8,128)(2,1)} %bitcast.15), custom_call_target="tpu_custom_call" | custom-call | bytes 786432 | tf_op jit(solution)/shard_map/send_columns/pallas_call | solution.py:134
  2.8 3.0 %collective-permute-start.3 = (bf16[32,4096]{1,0:T(8,128)(2,1)S(1)}, bf16[32,4096]{1,0:T(8,128)(2,1)S(1)}, u32[]{:S(2)}, u32[]{:S(2)}) collective-permute-start(bf16[32,4096]{1,0:T(8,128)(2,1)S(1)} %get-tuple-element.20), channel_id=1, source_target_pairs={{0,8},{2,10},{4,12},{6,14},{8,24},{10,26},{12,28},{14,30},{16,0},{... | collective-permute-start | bytes 786440 | tf_op jit(solution)/shard_map/ppermute | solution.py:336
  5.9 1.1 %collective-permute-start.4 = (bf16[32,4096]{1,0:T(8,128)(2,1)S(1)}, bf16[32,4096]{1,0:T(8,128)(2,1)S(1)}, u32[]{:S(2)}, u32[]{:S(2)}) collective-permute-start(bf16[32,4096]{1,0:T(8,128)(2,1)S(1)} %get-tuple-element.19), channel_id=1, source_target_pairs={{0,16},{2,18},{4,20},{6,22},{8,0},{10,2},{12,4},{14,6},{16,24},{18... | collective-permute-start | bytes 786440 | tf_op jit(solution)/shard_map/ppermute | solution.py:336
  7.0 1.8 %collective-permute-start = (bf16[32,4096]{1,0:T(8,128)(2,1)S(1)}, bf16[32,4096]{1,0:T(8,128)(2,1)S(1)}, u32[]{:S(2)}, u32[]{:S(2)}) collective-permute-start(bf16[32,4096]{1,0:T(8,128)(2,1)S(1)} %bitcast.9), channel_id=1, source_target_pairs={{0,2},{2,0},{4,6},{6,4},{8,10},{10,8},{12,14},{14,12},{16,18},{18,... | collective-permute-start | bytes 786440 | tf_op jit(solution)/shard_map/ppermute | solution.py:321
  8.7 1.6 %collective-permute-start.1 = (bf16[32,4096]{1,0:T(8,128)(2,1)S(1)}, bf16[32,4096]{1,0:T(8,128)(2,1)S(1)}, u32[]{:S(2)}, u32[]{:S(2)}) collective-permute-start(bf16[32,4096]{1,0:T(8,128)(2,1)S(1)} %bitcast.10), channel_id=1, source_target_pairs={{0,4},{2,6},{4,0},{6,2},{8,12},{10,14},{12,8},{14,10},{16,20},{18,... | collective-permute-start | bytes 786440 | tf_op jit(solution)/shard_map/ppermute | solution.py:321
  10.3 0.2 collective-permute-start.2
  10.4 2.2 %own_columns.1.refs_8_ = bf16[2,4096,128]{2,1,0:T(8,128)(2,1)S(1)} custom-call(s32[4,16]{1,0:T(4,128)S(1)} %copy-done.1, bf16[4096,2048]{1,0:T(8,128)(2,1)} %bitcast.16), custom_call_target="tpu_custom_call" | custom-call | bytes 4194304 | tf_op jit(solution)/shard_map/own_columns/pallas_call | solution.py:165
  12.7 2.5 %send_columns.2 = bf16[3088,128]{1,0:T(8,128)(2,1)S(1)} custom-call(s32[4,16]{1,0:T(4,128)S(1)} %copy-done.1, bf16[4096,2048]{1,0:T(8,128)(2,1)} %bitcast.17, f32[16,128]{1,0:T(8,128)S(1)} %bitcast.13), custom_call_target="tpu_custom_call" | custom-call | bytes 2359296 | tf_op jit(solution)/shard_map/send_columns/pallas_call | solution.py:134
  15.3 4.2 %collective-permute-start.8 = (bf16[3088,128]{1,0:T(8,128)(2,1)S(1)}, bf16[3088,128]{1,0:T(8,128)(2,1)S(1)}, u32[]{:S(2)}, u32[]{:S(2)}) collective-permute-start(bf16[3088,128]{1,0:T(8,128)(2,1)S(1)} %send_columns.2), channel_id=1, source_target_pairs={{0,8},{2,10},{4,12},{6,14},{8,0},{10,2},{12,4},{14,6},{16,24},{18,... | collective-permute-start | bytes 2371592 | tf_op jit(solution)/shard_map/ppermute | solution.py:321
  19.6 1.6 %collective-permute-start.5 = (bf16[32,4096]{1,0:T(8,128)(2,1)S(1)}, bf16[32,4096]{1,0:T(8,128)(2,1)S(1)}, u32[]{:S(2)}, u32[]{:S(2)}) collective-permute-start(bf16[32,4096]{1,0:T(8,128)(2,1)S(1)} %get-tuple-element.12.refs_4_), channel_id=1, source_target_pairs={{0,2},{2,0},{4,6},{6,4},{8,10},{10,8},{12,14},{14,12},{16,18},{18,... | collective-permute-start | bytes 786440 | tf_op jit(solution)/shard_map/ppermute | solution.py:321
  21.1 1.5 %collective-permute-start.6 = (bf16[32,4096]{1,0:T(8,128)(2,1)S(1)}, bf16[32,4096]{1,0:T(8,128)(2,1)S(1)}, u32[]{:S(2)}, u32[]{:S(2)}) collective-permute-start(bf16[32,4096]{1,0:T(8,128)(2,1)S(1)} %get-tuple-element.12.refs_4_), channel_id=1, source_target_pairs={{0,4},{2,6},{4,0},{6,2},{8,12},{10,14},{12,8},{14,10},{16,20},{18,... | collective-permute-start | bytes 786440 | tf_op jit(solution)/shard_map/ppermute | solution.py:321
  22.6 0.5 collective-permute-start.7
  23.1 5.6 %stage_decoder.1.refs_8_ = bf16[4,256,1024]{2,1,0:T(8,128)(2,1)S(1)} custom-call(s32[4,16]{1,0:T(4,128)S(1)} %copy-done.1, bf16[256,32768]{1,0:T(8,128)(2,1)} %bitcast.18), custom_call_target="tpu_custom_call" | custom-call | bytes 6291456 | tf_op jit(solution)/shard_map/stage_decoder/pallas_call | solution.py:253
  28.8 0.1 collective-permute-done.5.refs_5_
  28.9 5.2 %collective-permute-done.6.refs_6_ = bf16[32,4096]{1,0:T(8,128)(2,1)S(1)} collective-permute-done((bf16[32,4096]{1,0:T(8,128)(2,1)S(1)}, bf16[32,4096]{1,0:T(8,128)(2,1)S(1)}, u32[]{:S(2)}, u32[]{:S(2)}) %collective-permute-start.6) | collective-permute-done | bytes 262176 | tf_op jit(solution)/shard_map/ppermute | solution.py:321
  34.0 1.7 %collective-permute-done.8.refs_10_ = bf16[3088,128]{1,0:T(8,128)(2,1)S(1)} collective-permute-done((bf16[3088,128]{1,0:T(8,128)(2,1)S(1)}, bf16[3088,128]{1,0:T(8,128)(2,1)S(1)}, u32[]{:S(2)}, u32[]{:S(2)}) %collective-permute-start.8) | collective-permute-done | bytes 790560 | tf_op jit(solution)/shard_map/ppermute | solution.py:321
  35.8 1.5 %encode.1 = f32[4,64,128]{2,1,0:T(8,128)S(1)} custom-call(s32[4,16]{1,0:T(4,128)S(1)} %copy-done.1, s32[4,16]{1,0:T(4,128)S(1)} %copy-done.3, bf16[32,4096]{1,0:T(8,128)(2,1)S(1)} %bitcast.12, bf16[32,4096]{1,0:T(8,128)(2,1)S(1)} %collective-permute-done.refs_1_, bf16[32,4096]{1,0:T(8,128)(2,1)S(1)} %collective-permute-done.1.refs_2_, ...), custom_call_target="tpu_custom_call" | custom-call | flops 536870912 | bytes 5242880 | tf_op jit(solution)/shard_map/encode/pallas_call | solution.py:214
  37.3 1.3 %collective-permute-done.9 = f32[4,64,128]{2,1,0:T(8,128)S(1)} collective-permute-done((f32[4,64,128]{2,1,0:T(8,128)S(1)}, f32[4,64,128]{2,1,0:T(8,128)S(1)}, u32[]{:S(2)}, u32[]{:S(2)}) %collective-permute-start.9) | collective-permute-done | bytes 131104 | tf_op jit(solution)/shard_map/ppermute | solution.py:324
  38.7 0.8 %collective-permute-start.10 = (bf16[2,2,64,128]{3,2,1,0:T(8,128)(2,1)S(1)}, bf16[2,2,64,128]{3,2,1,0:T(8,128)(2,1)S(1)}, u32[]{:S(2)}, u32[]{:S(2)}) collective-permute-start(bf16[2,2,64,128]{3,2,1,0:T(8,128)(2,1)S(1)} %bitcast.19), channel_id=1, source_target_pairs={{0,8},{2,10},{4,12},{6,14},{8,0},{10,2},{12,4},{14,6},{16,24},{18,... | collective-permute-start | bytes 196616 | tf_op jit(solution)/shard_map/ppermute | solution.py:355
  39.5 2.7 %collective-permute-start.11 = (bf16[1,2,64,128]{3,2,1,0:T(8,128)(2,1)S(1)}, bf16[1,2,64,128]{3,2,1,0:T(8,128)(2,1)S(1)}, u32[]{:S(2)}, u32[]{:S(2)}) collective-permute-start(bf16[1,2,64,128]{3,2,1,0:T(8,128)(2,1)S(1)} %constant_dynamic-slice_fusion), channel_id=1, source_target_pairs={{0,16},{2,18},{4,20},{6,22},{8,24},{10,26},{12,28},{14,30},{16,0},... | collective-permute-start | bytes 98312 | tf_op jit(solution)/shard_map/ppermute | solution.py:321
  42.3 2.4 %collective-permute-done.11 = bf16[1,2,64,128]{3,2,1,0:T(8,128)(2,1)S(1)} collective-permute-done((bf16[1,2,64,128]{3,2,1,0:T(8,128)(2,1)S(1)}, bf16[1,2,64,128]{3,2,1,0:T(8,128)(2,1)S(1)}, u32[]{:S(2)}, u32[]{:S(2)}) %collective-permute-start.11) | collective-permute-done | bytes 32800 | tf_op jit(solution)/shard_map/ppermute | solution.py:321
  44.7 1.6 %collective-permute-start.12 = (bf16[4,2,64,128]{3,2,1,0:T(8,128)(2,1)S(1)}, bf16[4,2,64,128]{3,2,1,0:T(8,128)(2,1)S(1)}, u32[]{:S(2)}, u32[]{:S(2)}) collective-permute-start(bf16[4,2,64,128]{3,2,1,0:T(8,128)(2,1)S(1)} %pad_maximum_fusion.refs_0_), channel_id=1, source_target_pairs={{0,2},{2,0},{4,6},{6,4},{8,10},{10,8},{12,14},{14,12},{16,18},{18,... | collective-permute-start | bytes 393224 | tf_op jit(solution)/shard_map/ppermute | solution.py:321
  46.3 1.5 %collective-permute-start.13 = (bf16[4,2,64,128]{3,2,1,0:T(8,128)(2,1)S(1)}, bf16[4,2,64,128]{3,2,1,0:T(8,128)(2,1)S(1)}, u32[]{:S(2)}, u32[]{:S(2)}) collective-permute-start(bf16[4,2,64,128]{3,2,1,0:T(8,128)(2,1)S(1)} %pad_maximum_fusion.refs_0_), channel_id=1, source_target_pairs={{0,4},{2,6},{4,0},{6,2},{8,12},{10,14},{12,8},{14,10},{16,20},{18,... | collective-permute-start | bytes 393224 | tf_op jit(solution)/shard_map/ppermute | solution.py:321
  47.8 0.5 collective-permute-start.14
  48.3 2.8 %collective-permute-done.12.refs_1_ = bf16[4,2,64,128]{3,2,1,0:T(8,128)(2,1)S(1)} collective-permute-done((bf16[4,2,64,128]{3,2,1,0:T(8,128)(2,1)S(1)}, bf16[4,2,64,128]{3,2,1,0:T(8,128)(2,1)S(1)}, u32[]{:S(2)}, u32[]{:S(2)}) %collective-permute-start.12) | collective-permute-done | bytes 131104 | tf_op jit(solution)/shard_map/ppermute | solution.py:321
  51.2 4.0 %collective-permute-done.13.refs_2_ = bf16[4,2,64,128]{3,2,1,0:T(8,128)(2,1)S(1)} collective-permute-done((bf16[4,2,64,128]{3,2,1,0:T(8,128)(2,1)S(1)}, bf16[4,2,64,128]{3,2,1,0:T(8,128)(2,1)S(1)}, u32[]{:S(2)}, u32[]{:S(2)}) %collective-permute-start.13) | collective-permute-done | bytes 131104 | tf_op jit(solution)/shard_map/ppermute | solution.py:321
  55.1 0.5 collective-permute-start.18
  55.7 0.1 copy.8.refs_9_
  55.8 0.7 %collective-permute-done.17.refs_6_ = bf16[4,2,64,128]{3,2,1,0:T(8,128)(2,1)S(1)} collective-permute-done((bf16[4,2,64,128]{3,2,1,0:T(8,128)(2,1)S(1)}, bf16[4,2,64,128]{3,2,1,0:T(8,128)(2,1)S(1)}, u32[]{:S(2)}, u32[]{:S(2)}) %collective-permute-start.17) | collective-permute-done | bytes 131104 | tf_op jit(solution)/shard_map/ppermute | solution.py:324
  56.5 0.2 collective-permute-done.18.refs_7_
  56.7 1.5 %decode.1 = bf16[256,512]{1,0:T(8,128)(2,1)} custom-call(bf16[4,2,64,128]{3,2,1,0:T(8,128)(2,1)S(1)} %pad_maximum_fusion.refs_0_, bf16[4,2,64,128]{3,2,1,0:T(8,128)(2,1)S(1)} %collective-permute-done.12.refs_1_, bf16[4,2,64,128]{3,2,1,0:T(8,128)(2,1)S(1)} %collective-permute-done.13.refs_2_, bf16[4,2,64,128]{3,2,1,0:T(8,128)(2,1)S(1)} %collective-permute-done.14.refs_3_, ...), custom_call_target="tpu_custom_call" | custom-call | flops 268435456 | bytes 4194304 | tf_op jit(solution)/shard_map/decode/pallas_call | solution.py:300
  (28 shorter events, 0.3 us)
Async XLA Ops:
  0.0 2.8 %copy-start = (bf16[1,32,4096]{2,1,0:T(8,128)(2,1)S(1)}, bf16[1,32,4096]{2,1,0:T(8,128)(2,1)}, u32[]{:S(2)}) copy-start(bf16[1,32,4096]{2,1,0:T(8,128)(2,1)} %param.7) | copy-start | bytes 786436
  0.0 0.7 %copy-start.1 = (s32[4,16]{1,0:T(4,128)S(1)}, s32[4,16]{1,0:T(4,128)}, u32[]{:S(2)}) copy-start(s32[4,16]{1,0:T(4,128)} %ids_ref.9) | copy-start | bytes 772
  0.7 11.9 %copy-start.2 = (f32[2048]{0:T(1024)S(1)}, f32[2048]{0:T(1024)}, u32[]{:S(2)}) copy-start(f32[2048]{0:T(1024)} %param.9) | copy-start | bytes 24580
  2.8 12.4 %collective-permute-start.3 = (bf16[32,4096]{1,0:T(8,128)(2,1)S(1)}, bf16[32,4096]{1,0:T(8,128)(2,1)S(1)}, u32[]{:S(2)}, u32[]{:S(2)}) collective-permute-start(bf16[32,4096]{1,0:T(8,128)(2,1)S(1)} %get-tuple-element.20), channel_id=1, source_target_pairs={{0,8},{2,10},{4,12},{6,14},{8,24},{10,26},{12,28},{14,30},{16,0},{... | collective-permute-start | bytes 786440 | tf_op jit(solution)/shard_map/ppermute | solution.py:336
  5.9 13.6 %collective-permute-start.4 = (bf16[32,4096]{1,0:T(8,128)(2,1)S(1)}, bf16[32,4096]{1,0:T(8,128)(2,1)S(1)}, u32[]{:S(2)}, u32[]{:S(2)}) collective-permute-start(bf16[32,4096]{1,0:T(8,128)(2,1)S(1)} %get-tuple-element.19), channel_id=1, source_target_pairs={{0,16},{2,18},{4,20},{6,22},{8,0},{10,2},{12,4},{14,6},{16,24},{18... | collective-permute-start | bytes 786440 | tf_op jit(solution)/shard_map/ppermute | solution.py:336
  7.0 14.2 %collective-permute-start = (bf16[32,4096]{1,0:T(8,128)(2,1)S(1)}, bf16[32,4096]{1,0:T(8,128)(2,1)S(1)}, u32[]{:S(2)}, u32[]{:S(2)}) collective-permute-start(bf16[32,4096]{1,0:T(8,128)(2,1)S(1)} %bitcast.9), channel_id=1, source_target_pairs={{0,2},{2,0},{4,6},{6,4},{8,10},{10,8},{12,14},{14,12},{16,18},{18,... | collective-permute-start | bytes 786440 | tf_op jit(solution)/shard_map/ppermute | solution.py:321
  8.7 13.9 %collective-permute-start.1 = (bf16[32,4096]{1,0:T(8,128)(2,1)S(1)}, bf16[32,4096]{1,0:T(8,128)(2,1)S(1)}, u32[]{:S(2)}, u32[]{:S(2)}) collective-permute-start(bf16[32,4096]{1,0:T(8,128)(2,1)S(1)} %bitcast.10), channel_id=1, source_target_pairs={{0,4},{2,6},{4,0},{6,2},{8,12},{10,14},{12,8},{14,10},{16,20},{18,... | collective-permute-start | bytes 786440 | tf_op jit(solution)/shard_map/ppermute | solution.py:321
  10.3 18.5 %collective-permute-start.2 = (bf16[32,4096]{1,0:T(8,128)(2,1)S(1)}, bf16[32,4096]{1,0:T(8,128)(2,1)S(1)}, u32[]{:S(2)}, u32[]{:S(2)}) collective-permute-start(bf16[32,4096]{1,0:T(8,128)(2,1)S(1)} %bitcast.11), channel_id=1, source_target_pairs={{0,6},{2,4},{4,2},{6,0},{8,14},{10,12},{12,10},{14,8},{16,22},{18,... | collective-permute-start | bytes 786440 | tf_op jit(solution)/shard_map/ppermute | solution.py:321
  12.7 23.1 %copy-start.3 = (s32[4,16]{1,0:T(4,128)S(1)}, s32[4,16]{1,0:T(4,128)}, u32[]{:S(2)}) copy-start(s32[4,16]{1,0:T(4,128)} %live_ref.1) | copy-start | bytes 772
  15.2 40.4 %copy-start.4 = (f32[1,256]{1,0:T(1,128)S(1)}, f32[1,256]{1,0:T(1,128)}, u32[]{:S(2)}) copy-start(f32[1,256]{1,0:T(1,128)} %param.11) | copy-start | bytes 3076
  15.3 20.5 %collective-permute-start.8 = (bf16[3088,128]{1,0:T(8,128)(2,1)S(1)}, bf16[3088,128]{1,0:T(8,128)(2,1)S(1)}, u32[]{:S(2)}, u32[]{:S(2)}) collective-permute-start(bf16[3088,128]{1,0:T(8,128)(2,1)S(1)} %send_columns.2), channel_id=1, source_target_pairs={{0,8},{2,10},{4,12},{6,14},{8,0},{10,2},{12,4},{14,6},{16,24},{18,... | collective-permute-start | bytes 2371592 | tf_op jit(solution)/shard_map/ppermute | solution.py:321
  19.6 9.3 %collective-permute-start.5 = (bf16[32,4096]{1,0:T(8,128)(2,1)S(1)}, bf16[32,4096]{1,0:T(8,128)(2,1)S(1)}, u32[]{:S(2)}, u32[]{:S(2)}) collective-permute-start(bf16[32,4096]{1,0:T(8,128)(2,1)S(1)} %get-tuple-element.12.refs_4_), channel_id=1, source_target_pairs={{0,2},{2,0},{4,6},{6,4},{8,10},{10,8},{12,14},{14,12},{16,18},{18,... | collective-permute-start | bytes 786440 | tf_op jit(solution)/shard_map/ppermute | solution.py:321
  21.1 12.9 %collective-permute-start.6 = (bf16[32,4096]{1,0:T(8,128)(2,1)S(1)}, bf16[32,4096]{1,0:T(8,128)(2,1)S(1)}, u32[]{:S(2)}, u32[]{:S(2)}) collective-permute-start(bf16[32,4096]{1,0:T(8,128)(2,1)S(1)} %get-tuple-element.12.refs_4_), channel_id=1, source_target_pairs={{0,4},{2,6},{4,0},{6,2},{8,12},{10,14},{12,8},{14,10},{16,20},{18,... | collective-permute-start | bytes 786440 | tf_op jit(solution)/shard_map/ppermute | solution.py:321
  22.6 11.4 %collective-permute-start.7 = (bf16[32,4096]{1,0:T(8,128)(2,1)S(1)}, bf16[32,4096]{1,0:T(8,128)(2,1)S(1)}, u32[]{:S(2)}, u32[]{:S(2)}) collective-permute-start(bf16[32,4096]{1,0:T(8,128)(2,1)S(1)} %get-tuple-element.12.refs_4_), channel_id=1, source_target_pairs={{0,6},{2,4},{4,2},{6,0},{8,14},{10,12},{12,10},{14,8},{16,22},{18,... | collective-permute-start | bytes 786440 | tf_op jit(solution)/shard_map/ppermute | solution.py:321
  37.3 1.4 %collective-permute-start.9 = (f32[4,64,128]{2,1,0:T(8,128)S(1)}, f32[4,64,128]{2,1,0:T(8,128)S(1)}, u32[]{:S(2)}, u32[]{:S(2)}) collective-permute-start(f32[4,64,128]{2,1,0:T(8,128)S(1)} %encode.1), channel_id=1, source_target_pairs={{0,1},{1,0},{2,3},{3,2},{4,5},{5,4},{6,7},{7,6},{8,9},{9,8},{10,11... | collective-permute-start | bytes 393224 | tf_op jit(solution)/shard_map/ppermute | solution.py:324
  38.7 6.0 %collective-permute-start.10 = (bf16[2,2,64,128]{3,2,1,0:T(8,128)(2,1)S(1)}, bf16[2,2,64,128]{3,2,1,0:T(8,128)(2,1)S(1)}, u32[]{:S(2)}, u32[]{:S(2)}) collective-permute-start(bf16[2,2,64,128]{3,2,1,0:T(8,128)(2,1)S(1)} %bitcast.19), channel_id=1, source_target_pairs={{0,8},{2,10},{4,12},{6,14},{8,0},{10,2},{12,4},{14,6},{16,24},{18,... | collective-permute-start | bytes 196616 | tf_op jit(solution)/shard_map/ppermute | solution.py:355
  39.5 5.2 %collective-permute-start.11 = (bf16[1,2,64,128]{3,2,1,0:T(8,128)(2,1)S(1)}, bf16[1,2,64,128]{3,2,1,0:T(8,128)(2,1)S(1)}, u32[]{:S(2)}, u32[]{:S(2)}) collective-permute-start(bf16[1,2,64,128]{3,2,1,0:T(8,128)(2,1)S(1)} %constant_dynamic-slice_fusion), channel_id=1, source_target_pairs={{0,16},{2,18},{4,20},{6,22},{8,24},{10,26},{12,28},{14,30},{16,0},... | collective-permute-start | bytes 98312 | tf_op jit(solution)/shard_map/ppermute | solution.py:321
  44.7 6.4 %collective-permute-start.12 = (bf16[4,2,64,128]{3,2,1,0:T(8,128)(2,1)S(1)}, bf16[4,2,64,128]{3,2,1,0:T(8,128)(2,1)S(1)}, u32[]{:S(2)}, u32[]{:S(2)}) collective-permute-start(bf16[4,2,64,128]{3,2,1,0:T(8,128)(2,1)S(1)} %pad_maximum_fusion.refs_0_), channel_id=1, source_target_pairs={{0,2},{2,0},{4,6},{6,4},{8,10},{10,8},{12,14},{14,12},{16,18},{18,... | collective-permute-start | bytes 393224 | tf_op jit(solution)/shard_map/ppermute | solution.py:321
  46.3 8.9 %collective-permute-start.13 = (bf16[4,2,64,128]{3,2,1,0:T(8,128)(2,1)S(1)}, bf16[4,2,64,128]{3,2,1,0:T(8,128)(2,1)S(1)}, u32[]{:S(2)}, u32[]{:S(2)}) collective-permute-start(bf16[4,2,64,128]{3,2,1,0:T(8,128)(2,1)S(1)} %pad_maximum_fusion.refs_0_), channel_id=1, source_target_pairs={{0,4},{2,6},{4,0},{6,2},{8,12},{10,14},{12,8},{14,10},{16,20},{18,... | collective-permute-start | bytes 393224 | tf_op jit(solution)/shard_map/ppermute | solution.py:321
  47.8 7.3 %collective-permute-start.14 = (bf16[4,2,64,128]{3,2,1,0:T(8,128)(2,1)S(1)}, bf16[4,2,64,128]{3,2,1,0:T(8,128)(2,1)S(1)}, u32[]{:S(2)}, u32[]{:S(2)}) collective-permute-start(bf16[4,2,64,128]{3,2,1,0:T(8,128)(2,1)S(1)} %pad_maximum_fusion.refs_0_), channel_id=1, source_target_pairs={{0,6},{2,4},{4,2},{6,0},{8,14},{10,12},{12,10},{14,8},{16,22},{18,... | collective-permute-start | bytes 393224 | tf_op jit(solution)/shard_map/ppermute | solution.py:321
  48.3 7.5 %collective-permute-start.15 = (bf16[4,2,64,128]{3,2,1,0:T(8,128)(2,1)S(1)}, bf16[4,2,64,128]{3,2,1,0:T(8,128)(2,1)S(1)}, u32[]{:S(2)}, u32[]{:S(2)}) collective-permute-start(bf16[4,2,64,128]{3,2,1,0:T(8,128)(2,1)S(1)} %pad_maximum_fusion.refs_0_), channel_id=1, source_target_pairs={{0,1},{1,0},{2,3},{3,2},{4,5},{5,4},{6,7},{7,6},{8,9},{9,8},{10,11... | collective-permute-start | bytes 393224 | tf_op jit(solution)/shard_map/ppermute | solution.py:324
  51.2 4.7 %collective-permute-start.16 = (bf16[4,2,64,128]{3,2,1,0:T(8,128)(2,1)S(1)}, bf16[4,2,64,128]{3,2,1,0:T(8,128)(2,1)S(1)}, u32[]{:S(2)}, u32[]{:S(2)}) collective-permute-start(bf16[4,2,64,128]{3,2,1,0:T(8,128)(2,1)S(1)} %collective-permute-done.12.refs_1_), channel_id=1, source_target_pairs={{0,1},{1,0},{2,3},{3,2},{4,5},{5,4},{6,7},{7,6},{8,9},{9,8},{10,11... | collective-permute-start | bytes 393224 | tf_op jit(solution)/shard_map/ppermute | solution.py:324
  55.1 1.3 %collective-permute-start.17 = (bf16[4,2,64,128]{3,2,1,0:T(8,128)(2,1)S(1)}, bf16[4,2,64,128]{3,2,1,0:T(8,128)(2,1)S(1)}, u32[]{:S(2)}, u32[]{:S(2)}) collective-permute-start(bf16[4,2,64,128]{3,2,1,0:T(8,128)(2,1)S(1)} %collective-permute-done.13.refs_2_), channel_id=1, source_target_pairs={{0,1},{1,0},{2,3},{3,2},{4,5},{5,4},{6,7},{7,6},{8,9},{9,8},{10,11... | collective-permute-start | bytes 393224 | tf_op jit(solution)/shard_map/ppermute | solution.py:324
  55.1 1.5 %collective-permute-start.18 = (bf16[4,2,64,128]{3,2,1,0:T(8,128)(2,1)S(1)}, bf16[4,2,64,128]{3,2,1,0:T(8,128)(2,1)S(1)}, u32[]{:S(2)}, u32[]{:S(2)}) collective-permute-start(bf16[4,2,64,128]{3,2,1,0:T(8,128)(2,1)S(1)} %collective-permute-done.14.refs_3_), channel_id=1, source_target_pairs={{0,1},{1,0},{2,3},{3,2},{4,5},{5,4},{6,7},{7,6},{8,9},{9,8},{10,11... | collective-permute-start | bytes 393224 | tf_op jit(solution)/shard_map/ppermute | solution.py:324

commit v4 on v3

--- a/solution.py
+++ b/solution.py
@@ -83,8 +83,11 @@
     return pl.CostEstimate(flops=flops, bytes_accessed=moved, transcendentals=0)
 
 
-def send_columns_kernel(ids_ref, weight_ref, *refs, step, base):
-    *bias_refs, out_ref, in_ref, sems = refs
+def send_columns_kernel(all_ids_ref, weight_ref, *refs, step, base):
+    *bias_refs, out_ref, in_ref, ids_ref, ids_sem, sems = refs
+    ids_copy = pltpu.make_async_copy(all_ids_ref, ids_ref, ids_sem)
+    ids_copy.start()
+    ids_copy.wait()
     lat = lax.axis_index("lat")
     plane = lat // 4
     depth = in_ref.shape[1]
@@ -134,9 +137,14 @@
     return pl.pallas_call(
         functools.partial(send_columns_kernel, step=step, base=base),
         out_shape=jax.ShapeDtypeStruct(shape, BF16),
-        in_specs=[SMEM, ANY] + [VMEM] * len(bias),
+        in_specs=[ANY, ANY] + [VMEM] * len(bias),
         out_specs=VMEM,
-        scratch_shapes=[pltpu.VMEM((2, depth, PAIR), BF16), pltpu.SemaphoreType.DMA((2, depth // step))],
+        scratch_shapes=[
+            pltpu.VMEM((2, depth, PAIR), BF16),
+            pltpu.SMEM(ids.shape, jnp.int32),
+            pltpu.SemaphoreType.DMA,
+            pltpu.SemaphoreType.DMA((2, depth // step)),
+        ],
         compiler_params=params(),
         cost_estimate=cost(0, 3 * depth * PAIR * 2),
         name="send_columns",
@@ -327,7 +335,7 @@
     near = [near_own] + [swap(near_own, place) for place in range(1, 4)]
     bias = enc_bias.reshape(-1, PAIR)
     depth = enc_weight.shape[1]
-    first = send_columns(block_ids, enc_weight[0], [], 0, FIRST, near_own.shape, 256)
+    first = send_columns(block_ids, enc_weight[0], [], 0, FIRST, near_own.shape, 512)
     plane = lax.axis_index("lat") // 4
     at_end = (plane == 0) | (plane == 3)
 
@@ -343,7 +351,6 @@
     far_own = jnp.where(at_end, one, two)
     first = jnp.where(at_end, two, one)
     own = own_columns(block_ids, enc_weight[0])
-    far_own, own = lax.optimization_barrier((far_own, own))
     columns = stage_decoder(block_ids, dec_weight[0])
     far = [far_own] + [swap(far_own, place) for place in range(1, 4)]
 

time: 58.5 us -> 58.3 us (level)
  starting transfers between devices: 23.1 us -> 25.2 us
  waiting for transfers between devices: 18.5 us -> 16.5 us
    ppermute x11, waiting for transfers between devices: 16.3 us -> 14 us  [swap(): return lax.ppermute(values, 'lat', [(i, i ^ mask) for i in range(owners)])]
    ppermute x11, starting transfers between devices: 17.6 us -> 19.5 us  [swap(): return lax.ppermute(values, 'lat', [(i, i ^ mask) for i in range(owners)])]
where the time goes in v4:
time: 58.3 us; the launch traced here: 58.1 us
  starting transfers between devices  25.2 us (43%)
  waiting for transfers between devices  16.5 us (28%)
  Pallas kernels  15.3 us (26%)
  local copies, waits for them, and re-layouts  0.88 us (2%)
    ppermute x11, starting transfers between devices, swap(): return lax.ppermute(values, 'lat', [(i, i ^ mask) for i in range(owners)])  19.5 us
    ppermute x11, waiting for transfers between devices, swap(): return lax.ppermute(values, 'lat', [(i, i ^ mask) for i in range(owners)])  14 us
    pallas_call x1, Pallas kernels, stage_decoder(): pl.pallas_call(stage_decoder_kernel, out_shape=jax.ShapeDtypeStruct((tile...  5.61 us
    pallas_call x2, Pallas kernels, send_columns(): pl.pallas_call(functools.partial(send_columns_kernel, step=step, base=bas...  4.44 us
    ppermute x2, starting transfers between devices, rotate(): return lax.ppermute(values, 'lat', pairs)  4.15 us
    pallas_call x1, Pallas kernels, own_columns(): pl.pallas_call(functools.partial(own_columns_kernel, step=step), out_shap...  2.22 us
    ppermute x5, waiting for transfers between devices, across(): return lax.ppermute(values, 'ckpt', [(0, 1), (1, 0)])  2.2 us
    pallas_call x1, Pallas kernels, decode(): pl.pallas_call(decode_kernel, out_shape=jax.ShapeDtypeStruct((features, t...  1.55 us
  transfers between devices with their start and end apart: 19, of which 9 were waited for; matrix products, arithmetic and copies ran while one was open for 0% of the time, Pallas kernels for 18%

profile of v4, /device:TPU:0, one launch (start us, length us, event | category | flops | bytes accessed | tf_op | source)
XLA Modules:
  0.0 58.1 jit_solution(14297277962392534798)
XLA Ops:
  0.0 0.7 %copy-done.1 = s32[4,16]{1,0:T(4,128)S(1)} copy-done((s32[4,16]{1,0:T(4,128)S(1)}, s32[4,16]{1,0:T(4,128)}, u32[]{:S(2)}) %copy-start.1) | copy-done | bytes 280
  0.7 1.9 %send_columns.3 = bf16[32,4096]{1,0:T(8,128)(2,1)S(1)} custom-call(s32[4,16]{1,0:T(4,128)S(1)} %copy-done.1, bf16[4096,2048]{1,0:T(8,128)(2,1)} %bitcast.15), custom_call_target="tpu_custom_call" | custom-call | bytes 786432 | tf_op jit(solution)/shard_map/send_columns/pallas_call | solution.py:137
  2.7 3.1 %collective-permute-start.3 = (bf16[32,4096]{1,0:T(8,128)(2,1)S(1)}, bf16[32,4096]{1,0:T(8,128)(2,1)S(1)}, u32[]{:S(2)}, u32[]{:S(2)}) collective-permute-start(bf16[32,4096]{1,0:T(8,128)(2,1)S(1)} %get-tuple-element.16), channel_id=1, source_target_pairs={{0,8},{2,10},{4,12},{6,14},{8,24},{10,26},{12,28},{14,30},{16,0},{... | collective-permute-start | bytes 786440 | tf_op jit(solution)/shard_map/ppermute | solution.py:344
  5.8 1.1 %collective-permute-start.4 = (bf16[32,4096]{1,0:T(8,128)(2,1)S(1)}, bf16[32,4096]{1,0:T(8,128)(2,1)S(1)}, u32[]{:S(2)}, u32[]{:S(2)}) collective-permute-start(bf16[32,4096]{1,0:T(8,128)(2,1)S(1)} %get-tuple-element.15), channel_id=1, source_target_pairs={{0,16},{2,18},{4,20},{6,22},{8,0},{10,2},{12,4},{14,6},{16,24},{18... | collective-permute-start | bytes 786440 | tf_op jit(solution)/shard_map/ppermute | solution.py:344
  6.9 1.8 %collective-permute-start = (bf16[32,4096]{1,0:T(8,128)(2,1)S(1)}, bf16[32,4096]{1,0:T(8,128)(2,1)S(1)}, u32[]{:S(2)}, u32[]{:S(2)}) collective-permute-start(bf16[32,4096]{1,0:T(8,128)(2,1)S(1)} %bitcast.9), channel_id=1, source_target_pairs={{0,2},{2,0},{4,6},{6,4},{8,10},{10,8},{12,14},{14,12},{16,18},{18,... | collective-permute-start | bytes 786440 | tf_op jit(solution)/shard_map/ppermute | solution.py:329
  8.6 1.5 %collective-permute-start.1 = (bf16[32,4096]{1,0:T(8,128)(2,1)S(1)}, bf16[32,4096]{1,0:T(8,128)(2,1)S(1)}, u32[]{:S(2)}, u32[]{:S(2)}) collective-permute-start(bf16[32,4096]{1,0:T(8,128)(2,1)S(1)} %bitcast.10), channel_id=1, source_target_pairs={{0,4},{2,6},{4,0},{6,2},{8,12},{10,14},{12,8},{14,10},{16,20},{18,... | collective-permute-start | bytes 786440 | tf_op jit(solution)/shard_map/ppermute | solution.py:329
  10.1 0.2 collective-permute-start.2
  10.4 2.5 %send_columns.2 = bf16[3088,128]{1,0:T(8,128)(2,1)S(1)} custom-call(s32[4,16]{1,0:T(4,128)S(1)} %copy-done.1, bf16[4096,2048]{1,0:T(8,128)(2,1)} %bitcast.16, f32[16,128]{1,0:T(8,128)S(1)} %bitcast.13), custom_call_target="tpu_custom_call" | custom-call | bytes 2359296 | tf_op jit(solution)/shard_map/send_columns/pallas_call | solution.py:137
  12.9 0.3 collective-permute-done.3
  13.2 6.2 %collective-permute-start.8 = (bf16[3088,128]{1,0:T(8,128)(2,1)S(1)}, bf16[3088,128]{1,0:T(8,128)(2,1)S(1)}, u32[]{:S(2)}, u32[]{:S(2)}) collective-permute-start(bf16[3088,128]{1,0:T(8,128)(2,1)S(1)} %send_columns.2), channel_id=1, source_target_pairs={{0,8},{2,10},{4,12},{6,14},{8,0},{10,2},{12,4},{14,6},{16,24},{18,... | collective-permute-start | bytes 2371592 | tf_op jit(solution)/shard_map/ppermute | solution.py:329
  19.5 1.6 %collective-permute-start.5 = (bf16[32,4096]{1,0:T(8,128)(2,1)S(1)}, bf16[32,4096]{1,0:T(8,128)(2,1)S(1)}, u32[]{:S(2)}, u32[]{:S(2)}) collective-permute-start(bf16[32,4096]{1,0:T(8,128)(2,1)S(1)} %get-tuple-element.14.refs_4_), channel_id=1, source_target_pairs={{0,2},{2,0},{4,6},{6,4},{8,10},{10,8},{12,14},{14,12},{16,18},{18,... | collective-permute-start | bytes 786440 | tf_op jit(solution)/shard_map/ppermute | solution.py:329
  21.1 1.5 %collective-permute-start.6 = (bf16[32,4096]{1,0:T(8,128)(2,1)S(1)}, bf16[32,4096]{1,0:T(8,128)(2,1)S(1)}, u32[]{:S(2)}, u32[]{:S(2)}) collective-permute-start(bf16[32,4096]{1,0:T(8,128)(2,1)S(1)} %get-tuple-element.14.refs_4_), channel_id=1, source_target_pairs={{0,4},{2,6},{4,0},{6,2},{8,12},{10,14},{12,8},{14,10},{16,20},{18,... | collective-permute-start | bytes 786440 | tf_op jit(solution)/shard_map/ppermute | solution.py:329
  22.6 0.5 collective-permute-start.7
  23.1 2.2 %own_columns.1.refs_8_ = bf16[2,4096,128]{2,1,0:T(8,128)(2,1)S(1)} custom-call(s32[4,16]{1,0:T(4,128)S(1)} %copy-done.1, bf16[4096,2048]{1,0:T(8,128)(2,1)} %bitcast.17), custom_call_target="tpu_custom_call" | custom-call | bytes 4194304 | tf_op jit(solution)/shard_map/own_columns/pallas_call | solution.py:173
  25.3 5.6 %stage_decoder.1.refs_8_ = bf16[4,256,1024]{2,1,0:T(8,128)(2,1)S(1)} custom-call(s32[4,16]{1,0:T(4,128)S(1)} %copy-done.1, bf16[256,32768]{1,0:T(8,128)(2,1)} %bitcast.18), custom_call_target="tpu_custom_call" | custom-call | bytes 6291456 | tf_op jit(solution)/shard_map/stage_decoder/pallas_call | solution.py:261
  30.9 3.0 %collective-permute-done.6.refs_6_ = bf16[32,4096]{1,0:T(8,128)(2,1)S(1)} collective-permute-done((bf16[32,4096]{1,0:T(8,128)(2,1)S(1)}, bf16[32,4096]{1,0:T(8,128)(2,1)S(1)}, u32[]{:S(2)}, u32[]{:S(2)}) %collective-permute-start.6) | collective-permute-done | bytes 262176 | tf_op jit(solution)/shard_map/ppermute | solution.py:329
  34.0 1.7 %collective-permute-done.8.refs_10_ = bf16[3088,128]{1,0:T(8,128)(2,1)S(1)} collective-permute-done((bf16[3088,128]{1,0:T(8,128)(2,1)S(1)}, bf16[3088,128]{1,0:T(8,128)(2,1)S(1)}, u32[]{:S(2)}, u32[]{:S(2)}) %collective-permute-start.8) | collective-permute-done | bytes 790560 | tf_op jit(solution)/shard_map/ppermute | solution.py:329
  35.7 1.5 %encode.1 = f32[4,64,128]{2,1,0:T(8,128)S(1)} custom-call(s32[4,16]{1,0:T(4,128)S(1)} %copy-done.1, s32[4,16]{1,0:T(4,128)S(1)} %copy-done.3, bf16[32,4096]{1,0:T(8,128)(2,1)S(1)} %bitcast.12, bf16[32,4096]{1,0:T(8,128)(2,1)S(1)} %collective-permute-done.refs_1_, bf16[32,4096]{1,0:T(8,128)(2,1)S(1)} %collective-permute-done.1.refs_2_, ...), custom_call_target="tpu_custom_call" | custom-call | flops 536870912 | bytes 5242880 | tf_op jit(solution)/shard_map/encode/pallas_call | solution.py:222
  37.2 1.3 %collective-permute-done.9 = f32[4,64,128]{2,1,0:T(8,128)S(1)} collective-permute-done((f32[4,64,128]{2,1,0:T(8,128)S(1)}, f32[4,64,128]{2,1,0:T(8,128)S(1)}, u32[]{:S(2)}, u32[]{:S(2)}) %collective-permute-start.9) | collective-permute-done | bytes 131104 | tf_op jit(solution)/shard_map/ppermute | solution.py:332
  38.6 0.8 %collective-permute-start.10 = (bf16[2,2,64,128]{3,2,1,0:T(8,128)(2,1)S(1)}, bf16[2,2,64,128]{3,2,1,0:T(8,128)(2,1)S(1)}, u32[]{:S(2)}, u32[]{:S(2)}) collective-permute-start(bf16[2,2,64,128]{3,2,1,0:T(8,128)(2,1)S(1)} %bitcast.19), channel_id=1, source_target_pairs={{0,8},{2,10},{4,12},{6,14},{8,0},{10,2},{12,4},{14,6},{16,24},{18,... | collective-permute-start | bytes 196616 | tf_op jit(solution)/shard_map/ppermute | solution.py:362
  39.4 2.7 %collective-permute-start.11 = (bf16[1,2,64,128]{3,2,1,0:T(8,128)(2,1)S(1)}, bf16[1,2,64,128]{3,2,1,0:T(8,128)(2,1)S(1)}, u32[]{:S(2)}, u32[]{:S(2)}) collective-permute-start(bf16[1,2,64,128]{3,2,1,0:T(8,128)(2,1)S(1)} %constant_dynamic-slice_fusion), channel_id=1, source_target_pairs={{0,16},{2,18},{4,20},{6,22},{8,24},{10,26},{12,28},{14,30},{16,0},... | collective-permute-start | bytes 98312 | tf_op jit(solution)/shard_map/ppermute | solution.py:329
  42.2 2.4 %collective-permute-done.11 = bf16[1,2,64,128]{3,2,1,0:T(8,128)(2,1)S(1)} collective-permute-done((bf16[1,2,64,128]{3,2,1,0:T(8,128)(2,1)S(1)}, bf16[1,2,64,128]{3,2,1,0:T(8,128)(2,1)S(1)}, u32[]{:S(2)}, u32[]{:S(2)}) %collective-permute-start.11) | collective-permute-done | bytes 32800 | tf_op jit(solution)/shard_map/ppermute | solution.py:329
  44.6 1.6 %collective-permute-start.12 = (bf16[4,2,64,128]{3,2,1,0:T(8,128)(2,1)S(1)}, bf16[4,2,64,128]{3,2,1,0:T(8,128)(2,1)S(1)}, u32[]{:S(2)}, u32[]{:S(2)}) collective-permute-start(bf16[4,2,64,128]{3,2,1,0:T(8,128)(2,1)S(1)} %pad_maximum_fusion.refs_0_), channel_id=1, source_target_pairs={{0,2},{2,0},{4,6},{6,4},{8,10},{10,8},{12,14},{14,12},{16,18},{18,... | collective-permute-start | bytes 393224 | tf_op jit(solution)/shard_map/ppermute | solution.py:329
  46.2 1.5 %collective-permute-start.13 = (bf16[4,2,64,128]{3,2,1,0:T(8,128)(2,1)S(1)}, bf16[4,2,64,128]{3,2,1,0:T(8,128)(2,1)S(1)}, u32[]{:S(2)}, u32[]{:S(2)}) collective-permute-start(bf16[4,2,64,128]{3,2,1,0:T(8,128)(2,1)S(1)} %pad_maximum_fusion.refs_0_), channel_id=1, source_target_pairs={{0,4},{2,6},{4,0},{6,2},{8,12},{10,14},{12,8},{14,10},{16,20},{18,... | collective-permute-start | bytes 393224 | tf_op jit(solution)/shard_map/ppermute | solution.py:329
  47.7 0.5 collective-permute-start.14
  48.2 2.8 %collective-permute-done.12.refs_1_ = bf16[4,2,64,128]{3,2,1,0:T(8,128)(2,1)S(1)} collective-permute-done((bf16[4,2,64,128]{3,2,1,0:T(8,128)(2,1)S(1)}, bf16[4,2,64,128]{3,2,1,0:T(8,128)(2,1)S(1)}, u32[]{:S(2)}, u32[]{:S(2)}) %collective-permute-start.12) | collective-permute-done | bytes 131104 | tf_op jit(solution)/shard_map/ppermute | solution.py:329
  51.1 4.0 %collective-permute-done.13.refs_2_ = bf16[4,2,64,128]{3,2,1,0:T(8,128)(2,1)S(1)} collective-permute-done((bf16[4,2,64,128]{3,2,1,0:T(8,128)(2,1)S(1)}, bf16[4,2,64,128]{3,2,1,0:T(8,128)(2,1)S(1)}, u32[]{:S(2)}, u32[]{:S(2)}) %collective-permute-start.13) | collective-permute-done | bytes 131104 | tf_op jit(solution)/shard_map/ppermute | solution.py:329
  55.1 0.5 collective-permute-start.18
  55.6 0.1 copy.8.refs_9_
  55.7 0.7 %collective-permute-done.17.refs_6_ = bf16[4,2,64,128]{3,2,1,0:T(8,128)(2,1)S(1)} collective-permute-done((bf16[4,2,64,128]{3,2,1,0:T(8,128)(2,1)S(1)}, bf16[4,2,64,128]{3,2,1,0:T(8,128)(2,1)S(1)}, u32[]{:S(2)}, u32[]{:S(2)}) %collective-permute-start.17) | collective-permute-done | bytes 131104 | tf_op jit(solution)/shard_map/ppermute | solution.py:332
  56.4 0.2 collective-permute-done.18.refs_7_
  56.6 1.5 %decode.1 = bf16[256,512]{1,0:T(8,128)(2,1)} custom-call(bf16[4,2,64,128]{3,2,1,0:T(8,128)(2,1)S(1)} %pad_maximum_fusion.refs_0_, bf16[4,2,64,128]{3,2,1,0:T(8,128)(2,1)S(1)} %collective-permute-done.12.refs_1_, bf16[4,2,64,128]{3,2,1,0:T(8,128)(2,1)S(1)} %collective-permute-done.13.refs_2_, bf16[4,2,64,128]{3,2,1,0:T(8,128)(2,1)S(1)} %collective-permute-done.14.refs_3_, ...), custom_call_target="tpu_custom_call" | custom-call | flops 268435456 | bytes 4194304 | tf_op jit(solution)/shard_map/decode/pallas_call | solution.py:308
  (28 shorter events, 0.3 us)
Async XLA Ops:
  0.0 2.6 %copy-start = (bf16[1,32,4096]{2,1,0:T(8,128)(2,1)S(1)}, bf16[1,32,4096]{2,1,0:T(8,128)(2,1)}, u32[]{:S(2)}) copy-start(bf16[1,32,4096]{2,1,0:T(8,128)(2,1)} %param.7) | copy-start | bytes 786436
  0.0 0.7 %copy-start.1 = (s32[4,16]{1,0:T(4,128)S(1)}, s32[4,16]{1,0:T(4,128)}, u32[]{:S(2)}) copy-start(s32[4,16]{1,0:T(4,128)} %ids_ref.5) | copy-start | bytes 772
  0.7 9.6 %copy-start.2 = (f32[2048]{0:T(1024)S(1)}, f32[2048]{0:T(1024)}, u32[]{:S(2)}) copy-start(f32[2048]{0:T(1024)} %param.9) | copy-start | bytes 24580
  2.7 10.5 %collective-permute-start.3 = (bf16[32,4096]{1,0:T(8,128)(2,1)S(1)}, bf16[32,4096]{1,0:T(8,128)(2,1)S(1)}, u32[]{:S(2)}, u32[]{:S(2)}) collective-permute-start(bf16[32,4096]{1,0:T(8,128)(2,1)S(1)} %get-tuple-element.16), channel_id=1, source_target_pairs={{0,8},{2,10},{4,12},{6,14},{8,24},{10,26},{12,28},{14,30},{16,0},{... | collective-permute-start | bytes 786440 | tf_op jit(solution)/shard_map/ppermute | solution.py:344
  5.8 13.6 %collective-permute-start.4 = (bf16[32,4096]{1,0:T(8,128)(2,1)S(1)}, bf16[32,4096]{1,0:T(8,128)(2,1)S(1)}, u32[]{:S(2)}, u32[]{:S(2)}) collective-permute-start(bf16[32,4096]{1,0:T(8,128)(2,1)S(1)} %get-tuple-element.15), channel_id=1, source_target_pairs={{0,16},{2,18},{4,20},{6,22},{8,0},{10,2},{12,4},{14,6},{16,24},{18... | collective-permute-start | bytes 786440 | tf_op jit(solution)/shard_map/ppermute | solution.py:344
  6.9 14.2 %collective-permute-start = (bf16[32,4096]{1,0:T(8,128)(2,1)S(1)}, bf16[32,4096]{1,0:T(8,128)(2,1)S(1)}, u32[]{:S(2)}, u32[]{:S(2)}) collective-permute-start(bf16[32,4096]{1,0:T(8,128)(2,1)S(1)} %bitcast.9), channel_id=1, source_target_pairs={{0,2},{2,0},{4,6},{6,4},{8,10},{10,8},{12,14},{14,12},{16,18},{18,... | collective-permute-start | bytes 786440 | tf_op jit(solution)/shard_map/ppermute | solution.py:329
  8.6 13.9 %collective-permute-start.1 = (bf16[32,4096]{1,0:T(8,128)(2,1)S(1)}, bf16[32,4096]{1,0:T(8,128)(2,1)S(1)}, u32[]{:S(2)}, u32[]{:S(2)}) collective-permute-start(bf16[32,4096]{1,0:T(8,128)(2,1)S(1)} %bitcast.10), channel_id=1, source_target_pairs={{0,4},{2,6},{4,0},{6,2},{8,12},{10,14},{12,8},{14,10},{16,20},{18,... | collective-permute-start | bytes 786440 | tf_op jit(solution)/shard_map/ppermute | solution.py:329
  10.1 20.8 %collective-permute-start.2 = (bf16[32,4096]{1,0:T(8,128)(2,1)S(1)}, bf16[32,4096]{1,0:T(8,128)(2,1)S(1)}, u32[]{:S(2)}, u32[]{:S(2)}) collective-permute-start(bf16[32,4096]{1,0:T(8,128)(2,1)S(1)} %bitcast.11), channel_id=1, source_target_pairs={{0,6},{2,4},{4,2},{6,0},{8,14},{10,12},{12,10},{14,8},{16,22},{18,... | collective-permute-start | bytes 786440 | tf_op jit(solution)/shard_map/ppermute | solution.py:329
  13.2 22.5 %collective-permute-start.8 = (bf16[3088,128]{1,0:T(8,128)(2,1)S(1)}, bf16[3088,128]{1,0:T(8,128)(2,1)S(1)}, u32[]{:S(2)}, u32[]{:S(2)}) collective-permute-start(bf16[3088,128]{1,0:T(8,128)(2,1)S(1)} %send_columns.2), channel_id=1, source_target_pairs={{0,8},{2,10},{4,12},{6,14},{8,0},{10,2},{12,4},{14,6},{16,24},{18,... | collective-permute-start | bytes 2371592 | tf_op jit(solution)/shard_map/ppermute | solution.py:329
  19.5 16.2 %copy-start.3 = (s32[4,16]{1,0:T(4,128)S(1)}, s32[4,16]{1,0:T(4,128)}, u32[]{:S(2)}) copy-start(s32[4,16]{1,0:T(4,128)} %live_ref.1) | copy-start | bytes 772
  19.5 11.4 %collective-permute-start.5 = (bf16[32,4096]{1,0:T(8,128)(2,1)S(1)}, bf16[32,4096]{1,0:T(8,128)(2,1)S(1)}, u32[]{:S(2)}, u32[]{:S(2)}) collective-permute-start(bf16[32,4096]{1,0:T(8,128)(2,1)S(1)} %get-tuple-element.14.refs_4_), channel_id=1, source_target_pairs={{0,2},{2,0},{4,6},{6,4},{8,10},{10,8},{12,14},{14,12},{16,18},{18,... | collective-permute-start | bytes 786440 | tf_op jit(solution)/shard_map/ppermute | solution.py:329
  21.1 12.9 %collective-permute-start.6 = (bf16[32,4096]{1,0:T(8,128)(2,1)S(1)}, bf16[32,4096]{1,0:T(8,128)(2,1)S(1)}, u32[]{:S(2)}, u32[]{:S(2)}) collective-permute-start(bf16[32,4096]{1,0:T(8,128)(2,1)S(1)} %get-tuple-element.14.refs_4_), channel_id=1, source_target_pairs={{0,4},{2,6},{4,0},{6,2},{8,12},{10,14},{12,8},{14,10},{16,20},{18,... | collective-permute-start | bytes 786440 | tf_op jit(solution)/shard_map/ppermute | solution.py:329
  22.6 11.4 %collective-permute-start.7 = (bf16[32,4096]{1,0:T(8,128)(2,1)S(1)}, bf16[32,4096]{1,0:T(8,128)(2,1)S(1)}, u32[]{:S(2)}, u32[]{:S(2)}) collective-permute-start(bf16[32,4096]{1,0:T(8,128)(2,1)S(1)} %get-tuple-element.14.refs_4_), channel_id=1, source_target_pairs={{0,6},{2,4},{4,2},{6,0},{8,14},{10,12},{12,10},{14,8},{16,22},{18,... | collective-permute-start | bytes 786440 | tf_op jit(solution)/shard_map/ppermute | solution.py:329
  25.3 30.3 %copy-start.4 = (f32[1,256]{1,0:T(1,128)S(1)}, f32[1,256]{1,0:T(1,128)}, u32[]{:S(2)}) copy-start(f32[1,256]{1,0:T(1,128)} %param.11) | copy-start | bytes 3076
  37.2 1.4 %collective-permute-start.9 = (f32[4,64,128]{2,1,0:T(8,128)S(1)}, f32[4,64,128]{2,1,0:T(8,128)S(1)}, u32[]{:S(2)}, u32[]{:S(2)}) collective-permute-start(f32[4,64,128]{2,1,0:T(8,128)S(1)} %encode.1), channel_id=1, source_target_pairs={{0,1},{1,0},{2,3},{3,2},{4,5},{5,4},{6,7},{7,6},{8,9},{9,8},{10,11... | collective-permute-start | bytes 393224 | tf_op jit(solution)/shard_map/ppermute | solution.py:332
  38.6 6.0 %collective-permute-start.10 = (bf16[2,2,64,128]{3,2,1,0:T(8,128)(2,1)S(1)}, bf16[2,2,64,128]{3,2,1,0:T(8,128)(2,1)S(1)}, u32[]{:S(2)}, u32[]{:S(2)}) collective-permute-start(bf16[2,2,64,128]{3,2,1,0:T(8,128)(2,1)S(1)} %bitcast.19), channel_id=1, source_target_pairs={{0,8},{2,10},{4,12},{6,14},{8,0},{10,2},{12,4},{14,6},{16,24},{18,... | collective-permute-start | bytes 196616 | tf_op jit(solution)/shard_map/ppermute | solution.py:362
  39.4 5.2 %collective-permute-start.11 = (bf16[1,2,64,128]{3,2,1,0:T(8,128)(2,1)S(1)}, bf16[1,2,64,128]{3,2,1,0:T(8,128)(2,1)S(1)}, u32[]{:S(2)}, u32[]{:S(2)}) collective-permute-start(bf16[1,2,64,128]{3,2,1,0:T(8,128)(2,1)S(1)} %constant_dynamic-slice_fusion), channel_id=1, source_target_pairs={{0,16},{2,18},{4,20},{6,22},{8,24},{10,26},{12,28},{14,30},{16,0},... | collective-permute-start | bytes 98312 | tf_op jit(solution)/shard_map/ppermute | solution.py:329
  44.6 6.4 %collective-permute-start.12 = (bf16[4,2,64,128]{3,2,1,0:T(8,128)(2,1)S(1)}, bf16[4,2,64,128]{3,2,1,0:T(8,128)(2,1)S(1)}, u32[]{:S(2)}, u32[]{:S(2)}) collective-permute-start(bf16[4,2,64,128]{3,2,1,0:T(8,128)(2,1)S(1)} %pad_maximum_fusion.refs_0_), channel_id=1, source_target_pairs={{0,2},{2,0},{4,6},{6,4},{8,10},{10,8},{12,14},{14,12},{16,18},{18,... | collective-permute-start | bytes 393224 | tf_op jit(solution)/shard_map/ppermute | solution.py:329
  46.2 8.9 %collective-permute-start.13 = (bf16[4,2,64,128]{3,2,1,0:T(8,128)(2,1)S(1)}, bf16[4,2,64,128]{3,2,1,0:T(8,128)(2,1)S(1)}, u32[]{:S(2)}, u32[]{:S(2)}) collective-permute-start(bf16[4,2,64,128]{3,2,1,0:T(8,128)(2,1)S(1)} %pad_maximum_fusion.refs_0_), channel_id=1, source_target_pairs={{0,4},{2,6},{4,0},{6,2},{8,12},{10,14},{12,8},{14,10},{16,20},{18,... | collective-permute-start | bytes 393224 | tf_op jit(solution)/shard_map/ppermute | solution.py:329
  47.7 7.3 %collective-permute-start.14 = (bf16[4,2,64,128]{3,2,1,0:T(8,128)(2,1)S(1)}, bf16[4,2,64,128]{3,2,1,0:T(8,128)(2,1)S(1)}, u32[]{:S(2)}, u32[]{:S(2)}) collective-permute-start(bf16[4,2,64,128]{3,2,1,0:T(8,128)(2,1)S(1)} %pad_maximum_fusion.refs_0_), channel_id=1, source_target_pairs={{0,6},{2,4},{4,2},{6,0},{8,14},{10,12},{12,10},{14,8},{16,22},{18,... | collective-permute-start | bytes 393224 | tf_op jit(solution)/shard_map/ppermute | solution.py:329
  48.2 7.5 %collective-permute-start.15 = (bf16[4,2,64,128]{3,2,1,0:T(8,128)(2,1)S(1)}, bf16[4,2,64,128]{3,2,1,0:T(8,128)(2,1)S(1)}, u32[]{:S(2)}, u32[]{:S(2)}) collective-permute-start(bf16[4,2,64,128]{3,2,1,0:T(8,128)(2,1)S(1)} %pad_maximum_fusion.refs_0_), channel_id=1, source_target_pairs={{0,1},{1,0},{2,3},{3,2},{4,5},{5,4},{6,7},{7,6},{8,9},{9,8},{10,11... | collective-permute-start | bytes 393224 | tf_op jit(solution)/shard_map/ppermute | solution.py:332
  51.1 4.7 %collective-permute-start.16 = (bf16[4,2,64,128]{3,2,1,0:T(8,128)(2,1)S(1)}, bf16[4,2,64,128]{3,2,1,0:T(8,128)(2,1)S(1)}, u32[]{:S(2)}, u32[]{:S(2)}) collective-permute-start(bf16[4,2,64,128]{3,2,1,0:T(8,128)(2,1)S(1)} %collective-permute-done.12.refs_1_), channel_id=1, source_target_pairs={{0,1},{1,0},{2,3},{3,2},{4,5},{5,4},{6,7},{7,6},{8,9},{9,8},{10,11... | collective-permute-start | bytes 393224 | tf_op jit(solution)/shard_map/ppermute | solution.py:332
  55.0 1.3 %collective-permute-start.17 = (bf16[4,2,64,128]{3,2,1,0:T(8,128)(2,1)S(1)}, bf16[4,2,64,128]{3,2,1,0:T(8,128)(2,1)S(1)}, u32[]{:S(2)}, u32[]{:S(2)}) collective-permute-start(bf16[4,2,64,128]{3,2,1,0:T(8,128)(2,1)S(1)} %collective-permute-done.13.refs_2_), channel_id=1, source_target_pairs={{0,1},{1,0},{2,3},{3,2},{4,5},{5,4},{6,7},{7,6},{8,9},{9,8},{10,11... | collective-permute-start | bytes 393224 | tf_op jit(solution)/shard_map/ppermute | solution.py:332
  55.1 1.5 %collective-permute-start.18 = (bf16[4,2,64,128]{3,2,1,0:T(8,128)(2,1)S(1)}, bf16[4,2,64,128]{3,2,1,0:T(8,128)(2,1)S(1)}, u32[]{:S(2)}, u32[]{:S(2)}) collective-permute-start(bf16[4,2,64,128]{3,2,1,0:T(8,128)(2,1)S(1)} %collective-permute-done.14.refs_3_), channel_id=1, source_target_pairs={{0,1},{1,0},{2,3},{3,2},{4,5},{5,4},{6,7},{7,6},{8,9},{9,8},{10,11... | collective-permute-start | bytes 393224 | tf_op jit(solution)/shard_map/ppermute | solution.py:332

commit v5 on v4

--- a/solution.py
+++ b/solution.py
@@ -363,8 +363,11 @@
     mine_half = lax.dynamic_slice_in_dim(acts, core, 1, 0)
     middle = swap(mine_half, 8)
     payload = jnp.concatenate([mine_half, along, middle], axis=0)
-    mine = [payload] + [swap(payload, place) for place in range(1, 4)]
-    theirs = [across(values) for values in mine]
+    other = across(payload)
+    diagonal = swap(payload, 3)
+    payload, other = lax.optimization_barrier((payload, other))
+    mine = [payload, swap(payload, 1), swap(payload, 2), diagonal]
+    theirs = [other] + [across(values) for values in mine[1:]]
     recon = decode(mine, theirs, columns, dec_bias.reshape(-1, 1))
     return recon[None]
 

time: 58.3 us -> 58.2 us (level)
  waiting for transfers between devices: 16.5 us -> 14.9 us
  starting transfers between devices: 25.2 us -> 26.6 us
    ppermute x11, waiting for transfers between devices: 14 us -> 12.4 us  [swap(): return lax.ppermute(values, 'lat', [(i, i ^ mask) for i in range(owners)])]
    ppermute x5, starting transfers between devices: 0.63 us -> 1.53 us  [across(): return lax.ppermute(values, 'ckpt', [(0, 1), (1, 0)])]
where the time goes in v5:
time: 58.2 us; the launch traced here: 58 us
  starting transfers between devices  26.6 us (46%)
  Pallas kernels  15.3 us (26%)
  waiting for transfers between devices  14.9 us (26%)
  local copies, waits for them, and re-layouts  0.88 us (2%)
    ppermute x11, starting transfers between devices, swap(): return lax.ppermute(values, 'lat', [(i, i ^ mask) for i in range(owners)])  20 us
    ppermute x11, waiting for transfers between devices, swap(): return lax.ppermute(values, 'lat', [(i, i ^ mask) for i in range(owners)])  12.4 us
    pallas_call x1, Pallas kernels, stage_decoder(): pl.pallas_call(stage_decoder_kernel, out_shape=jax.ShapeDtypeStruct((tile...  5.61 us
    pallas_call x2, Pallas kernels, send_columns(): pl.pallas_call(functools.partial(send_columns_kernel, step=step, base=bas...  4.44 us
    ppermute x2, starting transfers between devices, rotate(): return lax.ppermute(values, 'lat', pairs)  4.15 us
    pallas_call x1, Pallas kernels, own_columns(): pl.pallas_call(functools.partial(own_columns_kernel, step=step), out_shap...  2.22 us
    ppermute x5, waiting for transfers between devices, across(): return lax.ppermute(values, 'ckpt', [(0, 1), (1, 0)])  2.21 us
    pallas_call x1, Pallas kernels, decode(): pl.pallas_call(decode_kernel, out_shape=jax.ShapeDtypeStruct((features, t...  1.55 us
  transfers between devices with their start and end apart: 19, of which 9 were waited for; matrix products, arithmetic and copies ran while one was open for 0% of the time, Pallas kernels for 18%

profile of v5, /device:TPU:0, one launch (start us, length us, event | category | flops | bytes accessed | tf_op | source)
XLA Modules:
  0.0 58.0 jit_solution(2574359778263246935)
XLA Ops:
  0.0 0.7 %copy-done.1 = s32[4,16]{1,0:T(4,128)S(1)} copy-done((s32[4,16]{1,0:T(4,128)S(1)}, s32[4,16]{1,0:T(4,128)}, u32[]{:S(2)}) %copy-start.1) | copy-done | bytes 280
  0.7 1.9 %send_columns.3 = bf16[32,4096]{1,0:T(8,128)(2,1)S(1)} custom-call(s32[4,16]{1,0:T(4,128)S(1)} %copy-done.1, bf16[4096,2048]{1,0:T(8,128)(2,1)} %bitcast.15), custom_call_target="tpu_custom_call" | custom-call | bytes 786432 | tf_op jit(solution)/shard_map/send_columns/pallas_call | solution.py:137
  2.7 3.1 %collective-permute-start.3 = (bf16[32,4096]{1,0:T(8,128)(2,1)S(1)}, bf16[32,4096]{1,0:T(8,128)(2,1)S(1)}, u32[]{:S(2)}, u32[]{:S(2)}) collective-permute-start(bf16[32,4096]{1,0:T(8,128)(2,1)S(1)} %get-tuple-element.20), channel_id=1, source_target_pairs={{0,8},{2,10},{4,12},{6,14},{8,24},{10,26},{12,28},{14,30},{16,0},{... | collective-permute-start | bytes 786440 | tf_op jit(solution)/shard_map/ppermute | solution.py:344
  5.8 1.1 %collective-permute-start.4 = (bf16[32,4096]{1,0:T(8,128)(2,1)S(1)}, bf16[32,4096]{1,0:T(8,128)(2,1)S(1)}, u32[]{:S(2)}, u32[]{:S(2)}) collective-permute-start(bf16[32,4096]{1,0:T(8,128)(2,1)S(1)} %get-tuple-element.19), channel_id=1, source_target_pairs={{0,16},{2,18},{4,20},{6,22},{8,0},{10,2},{12,4},{14,6},{16,24},{18... | collective-permute-start | bytes 786440 | tf_op jit(solution)/shard_map/ppermute | solution.py:344
  6.9 1.8 %collective-permute-start = (bf16[32,4096]{1,0:T(8,128)(2,1)S(1)}, bf16[32,4096]{1,0:T(8,128)(2,1)S(1)}, u32[]{:S(2)}, u32[]{:S(2)}) collective-permute-start(bf16[32,4096]{1,0:T(8,128)(2,1)S(1)} %bitcast.9), channel_id=1, source_target_pairs={{0,2},{2,0},{4,6},{6,4},{8,10},{10,8},{12,14},{14,12},{16,18},{18,... | collective-permute-start | bytes 786440 | tf_op jit(solution)/shard_map/ppermute | solution.py:329
  8.6 1.5 %collective-permute-start.1 = (bf16[32,4096]{1,0:T(8,128)(2,1)S(1)}, bf16[32,4096]{1,0:T(8,128)(2,1)S(1)}, u32[]{:S(2)}, u32[]{:S(2)}) collective-permute-start(bf16[32,4096]{1,0:T(8,128)(2,1)S(1)} %bitcast.10), channel_id=1, source_target_pairs={{0,4},{2,6},{4,0},{6,2},{8,12},{10,14},{12,8},{14,10},{16,20},{18,... | collective-permute-start | bytes 786440 | tf_op jit(solution)/shard_map/ppermute | solution.py:329
  10.1 0.2 collective-permute-start.2
  10.4 2.5 %send_columns.2 = bf16[3088,128]{1,0:T(8,128)(2,1)S(1)} custom-call(s32[4,16]{1,0:T(4,128)S(1)} %copy-done.1, bf16[4096,2048]{1,0:T(8,128)(2,1)} %bitcast.16, f32[16,128]{1,0:T(8,128)S(1)} %bitcast.13), custom_call_target="tpu_custom_call" | custom-call | bytes 2359296 | tf_op jit(solution)/shard_map/send_columns/pallas_call | solution.py:137
  12.9 0.3 collective-permute-done.3
  13.2 6.2 %collective-permute-start.8 = (bf16[3088,128]{1,0:T(8,128)(2,1)S(1)}, bf16[3088,128]{1,0:T(8,128)(2,1)S(1)}, u32[]{:S(2)}, u32[]{:S(2)}) collective-permute-start(bf16[3088,128]{1,0:T(8,128)(2,1)S(1)} %send_columns.2), channel_id=1, source_target_pairs={{0,8},{2,10},{4,12},{6,14},{8,0},{10,2},{12,4},{14,6},{16,24},{18,... | collective-permute-start | bytes 2371592 | tf_op jit(solution)/shard_map/ppermute | solution.py:329
  19.5 1.6 %collective-permute-start.5 = (bf16[32,4096]{1,0:T(8,128)(2,1)S(1)}, bf16[32,4096]{1,0:T(8,128)(2,1)S(1)}, u32[]{:S(2)}, u32[]{:S(2)}) collective-permute-start(bf16[32,4096]{1,0:T(8,128)(2,1)S(1)} %get-tuple-element.18.refs_4_), channel_id=1, source_target_pairs={{0,2},{2,0},{4,6},{6,4},{8,10},{10,8},{12,14},{14,12},{16,18},{18,... | collective-permute-start | bytes 786440 | tf_op jit(solution)/shard_map/ppermute | solution.py:329
  21.1 1.5 %collective-permute-start.6 = (bf16[32,4096]{1,0:T(8,128)(2,1)S(1)}, bf16[32,4096]{1,0:T(8,128)(2,1)S(1)}, u32[]{:S(2)}, u32[]{:S(2)}) collective-permute-start(bf16[32,4096]{1,0:T(8,128)(2,1)S(1)} %get-tuple-element.18.refs_4_), channel_id=1, source_target_pairs={{0,4},{2,6},{4,0},{6,2},{8,12},{10,14},{12,8},{14,10},{16,20},{18,... | collective-permute-start | bytes 786440 | tf_op jit(solution)/shard_map/ppermute | solution.py:329
  22.6 0.5 collective-permute-start.7
  23.1 2.2 %own_columns.1.refs_8_ = bf16[2,4096,128]{2,1,0:T(8,128)(2,1)S(1)} custom-call(s32[4,16]{1,0:T(4,128)S(1)} %copy-done.1, bf16[4096,2048]{1,0:T(8,128)(2,1)} %bitcast.17), custom_call_target="tpu_custom_call" | custom-call | bytes 4194304 | tf_op jit(solution)/shard_map/own_columns/pallas_call | solution.py:173
  25.3 5.6 %stage_decoder.1.refs_8_ = bf16[4,256,1024]{2,1,0:T(8,128)(2,1)S(1)} custom-call(s32[4,16]{1,0:T(4,128)S(1)} %copy-done.1, bf16[256,32768]{1,0:T(8,128)(2,1)} %bitcast.18), custom_call_target="tpu_custom_call" | custom-call | bytes 6291456 | tf_op jit(solution)/shard_map/stage_decoder/pallas_call | solution.py:261
  30.9 3.0 %collective-permute-done.6.refs_6_ = bf16[32,4096]{1,0:T(8,128)(2,1)S(1)} collective-permute-done((bf16[32,4096]{1,0:T(8,128)(2,1)S(1)}, bf16[32,4096]{1,0:T(8,128)(2,1)S(1)}, u32[]{:S(2)}, u32[]{:S(2)}) %collective-permute-start.6) | collective-permute-done | bytes 262176 | tf_op jit(solution)/shard_map/ppermute | solution.py:329
  34.0 1.7 %collective-permute-done.8.refs_10_ = bf16[3088,128]{1,0:T(8,128)(2,1)S(1)} collective-permute-done((bf16[3088,128]{1,0:T(8,128)(2,1)S(1)}, bf16[3088,128]{1,0:T(8,128)(2,1)S(1)}, u32[]{:S(2)}, u32[]{:S(2)}) %collective-permute-start.8) | collective-permute-done | bytes 790560 | tf_op jit(solution)/shard_map/ppermute | solution.py:329
  35.7 1.5 %encode.1 = f32[4,64,128]{2,1,0:T(8,128)S(1)} custom-call(s32[4,16]{1,0:T(4,128)S(1)} %copy-done.1, s32[4,16]{1,0:T(4,128)S(1)} %copy-done.3, bf16[32,4096]{1,0:T(8,128)(2,1)S(1)} %bitcast.12, bf16[32,4096]{1,0:T(8,128)(2,1)S(1)} %collective-permute-done.refs_1_, bf16[32,4096]{1,0:T(8,128)(2,1)S(1)} %collective-permute-done.1.refs_2_, ...), custom_call_target="tpu_custom_call" | custom-call | flops 536870912 | bytes 5242880 | tf_op jit(solution)/shard_map/encode/pallas_call | solution.py:222
  37.2 1.3 %collective-permute-done.9 = f32[4,64,128]{2,1,0:T(8,128)S(1)} collective-permute-done((f32[4,64,128]{2,1,0:T(8,128)S(1)}, f32[4,64,128]{2,1,0:T(8,128)S(1)}, u32[]{:S(2)}, u32[]{:S(2)}) %collective-permute-start.9) | collective-permute-done | bytes 131104 | tf_op jit(solution)/shard_map/ppermute | solution.py:332
  38.6 0.8 %collective-permute-start.10 = (bf16[2,2,64,128]{3,2,1,0:T(8,128)(2,1)S(1)}, bf16[2,2,64,128]{3,2,1,0:T(8,128)(2,1)S(1)}, u32[]{:S(2)}, u32[]{:S(2)}) collective-permute-start(bf16[2,2,64,128]{3,2,1,0:T(8,128)(2,1)S(1)} %bitcast.19), channel_id=1, source_target_pairs={{0,8},{2,10},{4,12},{6,14},{8,0},{10,2},{12,4},{14,6},{16,24},{18,... | collective-permute-start | bytes 196616 | tf_op jit(solution)/shard_map/ppermute | solution.py:362
  39.4 2.7 %collective-permute-start.11 = (bf16[1,2,64,128]{3,2,1,0:T(8,128)(2,1)S(1)}, bf16[1,2,64,128]{3,2,1,0:T(8,128)(2,1)S(1)}, u32[]{:S(2)}, u32[]{:S(2)}) collective-permute-start(bf16[1,2,64,128]{3,2,1,0:T(8,128)(2,1)S(1)} %constant_dynamic-slice_fusion), channel_id=1, source_target_pairs={{0,16},{2,18},{4,20},{6,22},{8,24},{10,26},{12,28},{14,30},{16,0},... | collective-permute-start | bytes 98312 | tf_op jit(solution)/shard_map/ppermute | solution.py:329
  42.2 2.4 %collective-permute-done.11 = bf16[1,2,64,128]{3,2,1,0:T(8,128)(2,1)S(1)} collective-permute-done((bf16[1,2,64,128]{3,2,1,0:T(8,128)(2,1)S(1)}, bf16[1,2,64,128]{3,2,1,0:T(8,128)(2,1)S(1)}, u32[]{:S(2)}, u32[]{:S(2)}) %collective-permute-start.11) | collective-permute-done | bytes 32800 | tf_op jit(solution)/shard_map/ppermute | solution.py:329
  44.6 0.9 %collective-permute-start.12 = (bf16[4,2,64,128]{3,2,1,0:T(8,128)(2,1)S(1)}, bf16[4,2,64,128]{3,2,1,0:T(8,128)(2,1)S(1)}, u32[]{:S(2)}, u32[]{:S(2)}) collective-permute-start(bf16[4,2,64,128]{3,2,1,0:T(8,128)(2,1)S(1)} %pad_maximum_fusion.refs_0_), channel_id=1, source_target_pairs={{0,1},{1,0},{2,3},{3,2},{4,5},{5,4},{6,7},{7,6},{8,9},{9,8},{10,11... | collective-permute-start | bytes 393224 | tf_op jit(solution)/shard_map/ppermute | solution.py:332
  45.6 2.5 %collective-permute-start.15 = (bf16[4,2,64,128]{3,2,1,0:T(8,128)(2,1)S(1)}, bf16[4,2,64,128]{3,2,1,0:T(8,128)(2,1)S(1)}, u32[]{:S(2)}, u32[]{:S(2)}) collective-permute-start(bf16[4,2,64,128]{3,2,1,0:T(8,128)(2,1)S(1)} %pad_maximum_fusion.refs_0_), channel_id=1, source_target_pairs={{0,6},{2,4},{4,2},{6,0},{8,14},{10,12},{12,10},{14,8},{16,22},{18,... | collective-permute-start | bytes 393224 | tf_op jit(solution)/shard_map/ppermute | solution.py:329
  48.1 0.5 collective-permute-start.13
  48.6 1.0 %collective-permute-start.14 = (bf16[4,2,64,128]{3,2,1,0:T(8,128)(2,1)S(1)}, bf16[4,2,64,128]{3,2,1,0:T(8,128)(2,1)S(1)}, u32[]{:S(2)}, u32[]{:S(2)}) collective-permute-start(bf16[4,2,64,128]{3,2,1,0:T(8,128)(2,1)S(1)} %pad_maximum_fusion.refs_0_), channel_id=1, source_target_pairs={{0,4},{2,6},{4,0},{6,2},{8,12},{10,14},{12,8},{14,10},{16,20},{18,... | collective-permute-start | bytes 393224 | tf_op jit(solution)/shard_map/ppermute | solution.py:329
  49.6 3.2 %collective-permute-done.15.refs_3_ = bf16[4,2,64,128]{3,2,1,0:T(8,128)(2,1)S(1)} collective-permute-done((bf16[4,2,64,128]{3,2,1,0:T(8,128)(2,1)S(1)}, bf16[4,2,64,128]{3,2,1,0:T(8,128)(2,1)S(1)}, u32[]{:S(2)}, u32[]{:S(2)}) %collective-permute-start.15) | collective-permute-done | bytes 131104 | tf_op jit(solution)/shard_map/ppermute | solution.py:329
  52.8 2.0 %collective-permute-done.13.refs_1_ = bf16[4,2,64,128]{3,2,1,0:T(8,128)(2,1)S(1)} collective-permute-done((bf16[4,2,64,128]{3,2,1,0:T(8,128)(2,1)S(1)}, bf16[4,2,64,128]{3,2,1,0:T(8,128)(2,1)S(1)}, u32[]{:S(2)}, u32[]{:S(2)}) %collective-permute-start.13) | collective-permute-done | bytes 131104 | tf_op jit(solution)/shard_map/ppermute | solution.py:329
  54.9 0.5 collective-permute-start.17
  55.5 0.7 %collective-permute-done.16.refs_5_ = bf16[4,2,64,128]{3,2,1,0:T(8,128)(2,1)S(1)} collective-permute-done((bf16[4,2,64,128]{3,2,1,0:T(8,128)(2,1)S(1)}, bf16[4,2,64,128]{3,2,1,0:T(8,128)(2,1)S(1)}, u32[]{:S(2)}, u32[]{:S(2)}) %collective-permute-start.16) | collective-permute-done | bytes 131104 | tf_op jit(solution)/shard_map/ppermute | solution.py:332
  56.2 0.2 collective-permute-done.17.refs_6_
  56.4 1.5 %decode.1 = bf16[256,512]{1,0:T(8,128)(2,1)} custom-call(bf16[4,2,64,128]{3,2,1,0:T(8,128)(2,1)S(1)} %pad_maximum_fusion.refs_0_, bf16[4,2,64,128]{3,2,1,0:T(8,128)(2,1)S(1)} %collective-permute-done.13.refs_1_, bf16[4,2,64,128]{3,2,1,0:T(8,128)(2,1)S(1)} %collective-permute-done.14.refs_2_, bf16[4,2,64,128]{3,2,1,0:T(8,128)(2,1)S(1)} %collective-permute-done.15.refs_3_, ...), custom_call_target="tpu_custom_call" | custom-call | flops 268435456 | bytes 4194304 | tf_op jit(solution)/shard_map/decode/pallas_call | solution.py:308
  (28 shorter events, 0.4 us)
Async XLA Ops:
  0.0 2.6 %copy-start = (bf16[1,32,4096]{2,1,0:T(8,128)(2,1)S(1)}, bf16[1,32,4096]{2,1,0:T(8,128)(2,1)}, u32[]{:S(2)}) copy-start(bf16[1,32,4096]{2,1,0:T(8,128)(2,1)} %param.7) | copy-start | bytes 786436
  0.0 0.7 %copy-start.1 = (s32[4,16]{1,0:T(4,128)S(1)}, s32[4,16]{1,0:T(4,128)}, u32[]{:S(2)}) copy-start(s32[4,16]{1,0:T(4,128)} %ids_ref.5) | copy-start | bytes 772
  0.7 9.6 %copy-start.2 = (f32[2048]{0:T(1024)S(1)}, f32[2048]{0:T(1024)}, u32[]{:S(2)}) copy-start(f32[2048]{0:T(1024)} %param.9) | copy-start | bytes 24580
  2.7 10.5 %collective-permute-start.3 = (bf16[32,4096]{1,0:T(8,128)(2,1)S(1)}, bf16[32,4096]{1,0:T(8,128)(2,1)S(1)}, u32[]{:S(2)}, u32[]{:S(2)}) collective-permute-start(bf16[32,4096]{1,0:T(8,128)(2,1)S(1)} %get-tuple-element.20), channel_id=1, source_target_pairs={{0,8},{2,10},{4,12},{6,14},{8,24},{10,26},{12,28},{14,30},{16,0},{... | collective-permute-start | bytes 786440 | tf_op jit(solution)/shard_map/ppermute | solution.py:344
  5.8 13.6 %collective-permute-start.4 = (bf16[32,4096]{1,0:T(8,128)(2,1)S(1)}, bf16[32,4096]{1,0:T(8,128)(2,1)S(1)}, u32[]{:S(2)}, u32[]{:S(2)}) collective-permute-start(bf16[32,4096]{1,0:T(8,128)(2,1)S(1)} %get-tuple-element.19), channel_id=1, source_target_pairs={{0,16},{2,18},{4,20},{6,22},{8,0},{10,2},{12,4},{14,6},{16,24},{18... | collective-permute-start | bytes 786440 | tf_op jit(solution)/shard_map/ppermute | solution.py:344
  6.9 14.2 %collective-permute-start = (bf16[32,4096]{1,0:T(8,128)(2,1)S(1)}, bf16[32,4096]{1,0:T(8,128)(2,1)S(1)}, u32[]{:S(2)}, u32[]{:S(2)}) collective-permute-start(bf16[32,4096]{1,0:T(8,128)(2,1)S(1)} %bitcast.9), channel_id=1, source_target_pairs={{0,2},{2,0},{4,6},{6,4},{8,10},{10,8},{12,14},{14,12},{16,18},{18,... | collective-permute-start | bytes 786440 | tf_op jit(solution)/shard_map/ppermute | solution.py:329
  8.6 13.9 %collective-permute-start.1 = (bf16[32,4096]{1,0:T(8,128)(2,1)S(1)}, bf16[32,4096]{1,0:T(8,128)(2,1)S(1)}, u32[]{:S(2)}, u32[]{:S(2)}) collective-permute-start(bf16[32,4096]{1,0:T(8,128)(2,1)S(1)} %bitcast.10), channel_id=1, source_target_pairs={{0,4},{2,6},{4,0},{6,2},{8,12},{10,14},{12,8},{14,10},{16,20},{18,... | collective-permute-start | bytes 786440 | tf_op jit(solution)/shard_map/ppermute | solution.py:329
  10.1 20.8 %collective-permute-start.2 = (bf16[32,4096]{1,0:T(8,128)(2,1)S(1)}, bf16[32,4096]{1,0:T(8,128)(2,1)S(1)}, u32[]{:S(2)}, u32[]{:S(2)}) collective-permute-start(bf16[32,4096]{1,0:T(8,128)(2,1)S(1)} %bitcast.11), channel_id=1, source_target_pairs={{0,6},{2,4},{4,2},{6,0},{8,14},{10,12},{12,10},{14,8},{16,22},{18,... | collective-permute-start | bytes 786440 | tf_op jit(solution)/shard_map/ppermute | solution.py:329
  13.2 22.5 %collective-permute-start.8 = (bf16[3088,128]{1,0:T(8,128)(2,1)S(1)}, bf16[3088,128]{1,0:T(8,128)(2,1)S(1)}, u32[]{:S(2)}, u32[]{:S(2)}) collective-permute-start(bf16[3088,128]{1,0:T(8,128)(2,1)S(1)} %send_columns.2), channel_id=1, source_target_pairs={{0,8},{2,10},{4,12},{6,14},{8,0},{10,2},{12,4},{14,6},{16,24},{18,... | collective-permute-start | bytes 2371592 | tf_op jit(solution)/shard_map/ppermute | solution.py:329
  19.5 16.2 %copy-start.3 = (s32[4,16]{1,0:T(4,128)S(1)}, s32[4,16]{1,0:T(4,128)}, u32[]{:S(2)}) copy-start(s32[4,16]{1,0:T(4,128)} %live_ref.1) | copy-start | bytes 772
  19.5 11.4 %collective-permute-start.5 = (bf16[32,4096]{1,0:T(8,128)(2,1)S(1)}, bf16[32,4096]{1,0:T(8,128)(2,1)S(1)}, u32[]{:S(2)}, u32[]{:S(2)}) collective-permute-start(bf16[32,4096]{1,0:T(8,128)(2,1)S(1)} %get-tuple-element.18.refs_4_), channel_id=1, source_target_pairs={{0,2},{2,0},{4,6},{6,4},{8,10},{10,8},{12,14},{14,12},{16,18},{18,... | collective-permute-start | bytes 786440 | tf_op jit(solution)/shard_map/ppermute | solution.py:329
  21.1 12.9 %collective-permute-start.6 = (bf16[32,4096]{1,0:T(8,128)(2,1)S(1)}, bf16[32,4096]{1,0:T(8,128)(2,1)S(1)}, u32[]{:S(2)}, u32[]{:S(2)}) collective-permute-start(bf16[32,4096]{1,0:T(8,128)(2,1)S(1)} %get-tuple-element.18.refs_4_), channel_id=1, source_target_pairs={{0,4},{2,6},{4,0},{6,2},{8,12},{10,14},{12,8},{14,10},{16,20},{18,... | collective-permute-start | bytes 786440 | tf_op jit(solution)/shard_map/ppermute | solution.py:329
  22.6 11.4 %collective-permute-start.7 = (bf16[32,4096]{1,0:T(8,128)(2,1)S(1)}, bf16[32,4096]{1,0:T(8,128)(2,1)S(1)}, u32[]{:S(2)}, u32[]{:S(2)}) collective-permute-start(bf16[32,4096]{1,0:T(8,128)(2,1)S(1)} %get-tuple-element.18.refs_4_), channel_id=1, source_target_pairs={{0,6},{2,4},{4,2},{6,0},{8,14},{10,12},{12,10},{14,8},{16,22},{18,... | collective-permute-start | bytes 786440 | tf_op jit(solution)/shard_map/ppermute | solution.py:329
  25.3 30.1 %copy-start.4 = (f32[1,256]{1,0:T(1,128)S(1)}, f32[1,256]{1,0:T(1,128)}, u32[]{:S(2)}) copy-start(f32[1,256]{1,0:T(1,128)} %param.11) | copy-start | bytes 3076
  37.2 1.4 %collective-permute-start.9 = (f32[4,64,128]{2,1,0:T(8,128)S(1)}, f32[4,64,128]{2,1,0:T(8,128)S(1)}, u32[]{:S(2)}, u32[]{:S(2)}) collective-permute-start(f32[4,64,128]{2,1,0:T(8,128)S(1)} %encode.1), channel_id=1, source_target_pairs={{0,1},{1,0},{2,3},{3,2},{4,5},{5,4},{6,7},{7,6},{8,9},{9,8},{10,11... | collective-permute-start | bytes 393224 | tf_op jit(solution)/shard_map/ppermute | solution.py:332
  38.6 6.0 %collective-permute-start.10 = (bf16[2,2,64,128]{3,2,1,0:T(8,128)(2,1)S(1)}, bf16[2,2,64,128]{3,2,1,0:T(8,128)(2,1)S(1)}, u32[]{:S(2)}, u32[]{:S(2)}) collective-permute-start(bf16[2,2,64,128]{3,2,1,0:T(8,128)(2,1)S(1)} %bitcast.19), channel_id=1, source_target_pairs={{0,8},{2,10},{4,12},{6,14},{8,0},{10,2},{12,4},{14,6},{16,24},{18,... | collective-permute-start | bytes 196616 | tf_op jit(solution)/shard_map/ppermute | solution.py:362
  39.4 5.2 %collective-permute-start.11 = (bf16[1,2,64,128]{3,2,1,0:T(8,128)(2,1)S(1)}, bf16[1,2,64,128]{3,2,1,0:T(8,128)(2,1)S(1)}, u32[]{:S(2)}, u32[]{:S(2)}) collective-permute-start(bf16[1,2,64,128]{3,2,1,0:T(8,128)(2,1)S(1)} %constant_dynamic-slice_fusion), channel_id=1, source_target_pairs={{0,16},{2,18},{4,20},{6,22},{8,24},{10,26},{12,28},{14,30},{16,0},... | collective-permute-start | bytes 98312 | tf_op jit(solution)/shard_map/ppermute | solution.py:329
  44.6 3.5 %collective-permute-start.12 = (bf16[4,2,64,128]{3,2,1,0:T(8,128)(2,1)S(1)}, bf16[4,2,64,128]{3,2,1,0:T(8,128)(2,1)S(1)}, u32[]{:S(2)}, u32[]{:S(2)}) collective-permute-start(bf16[4,2,64,128]{3,2,1,0:T(8,128)(2,1)S(1)} %pad_maximum_fusion.refs_0_), channel_id=1, source_target_pairs={{0,1},{1,0},{2,3},{3,2},{4,5},{5,4},{6,7},{7,6},{8,9},{9,8},{10,11... | collective-permute-start | bytes 393224 | tf_op jit(solution)/shard_map/ppermute | solution.py:332
  45.6 7.3 %collective-permute-start.15 = (bf16[4,2,64,128]{3,2,1,0:T(8,128)(2,1)S(1)}, bf16[4,2,64,128]{3,2,1,0:T(8,128)(2,1)S(1)}, u32[]{:S(2)}, u32[]{:S(2)}) collective-permute-start(bf16[4,2,64,128]{3,2,1,0:T(8,128)(2,1)S(1)} %pad_maximum_fusion.refs_0_), channel_id=1, source_target_pairs={{0,6},{2,4},{4,2},{6,0},{8,14},{10,12},{12,10},{14,8},{16,22},{18,... | collective-permute-start | bytes 393224 | tf_op jit(solution)/shard_map/ppermute | solution.py:329
  48.1 6.8 %collective-permute-start.13 = (bf16[4,2,64,128]{3,2,1,0:T(8,128)(2,1)S(1)}, bf16[4,2,64,128]{3,2,1,0:T(8,128)(2,1)S(1)}, u32[]{:S(2)}, u32[]{:S(2)}) collective-permute-start(bf16[4,2,64,128]{3,2,1,0:T(8,128)(2,1)S(1)} %pad_maximum_fusion.refs_0_), channel_id=1, source_target_pairs={{0,2},{2,0},{4,6},{6,4},{8,10},{10,8},{12,14},{14,12},{16,18},{18,... | collective-permute-start | bytes 393224 | tf_op jit(solution)/shard_map/ppermute | solution.py:329
  48.6 6.3 %collective-permute-start.14 = (bf16[4,2,64,128]{3,2,1,0:T(8,128)(2,1)S(1)}, bf16[4,2,64,128]{3,2,1,0:T(8,128)(2,1)S(1)}, u32[]{:S(2)}, u32[]{:S(2)}) collective-permute-start(bf16[4,2,64,128]{3,2,1,0:T(8,128)(2,1)S(1)} %pad_maximum_fusion.refs_0_), channel_id=1, source_target_pairs={{0,4},{2,6},{4,0},{6,2},{8,12},{10,14},{12,8},{14,10},{16,20},{18,... | collective-permute-start | bytes 393224 | tf_op jit(solution)/shard_map/ppermute | solution.py:329
  52.8 2.7 %collective-permute-start.18 = (bf16[4,2,64,128]{3,2,1,0:T(8,128)(2,1)S(1)}, bf16[4,2,64,128]{3,2,1,0:T(8,128)(2,1)S(1)}, u32[]{:S(2)}, u32[]{:S(2)}) collective-permute-start(bf16[4,2,64,128]{3,2,1,0:T(8,128)(2,1)S(1)} %collective-permute-done.15.refs_3_), channel_id=1, source_target_pairs={{0,1},{1,0},{2,3},{3,2},{4,5},{5,4},{6,7},{7,6},{8,9},{9,8},{10,11... | collective-permute-start | bytes 393224 | tf_op jit(solution)/shard_map/ppermute | solution.py:332
  54.9 1.3 %collective-permute-start.16 = (bf16[4,2,64,128]{3,2,1,0:T(8,128)(2,1)S(1)}, bf16[4,2,64,128]{3,2,1,0:T(8,128)(2,1)S(1)}, u32[]{:S(2)}, u32[]{:S(2)}) collective-permute-start(bf16[4,2,64,128]{3,2,1,0:T(8,128)(2,1)S(1)} %collective-permute-done.13.refs_1_), channel_id=1, source_target_pairs={{0,1},{1,0},{2,3},{3,2},{4,5},{5,4},{6,7},{7,6},{8,9},{9,8},{10,11... | collective-permute-start | bytes 393224 | tf_op jit(solution)/shard_map/ppermute | solution.py:332
  54.9 1.5 %collective-permute-start.17 = (bf16[4,2,64,128]{3,2,1,0:T(8,128)(2,1)S(1)}, bf16[4,2,64,128]{3,2,1,0:T(8,128)(2,1)S(1)}, u32[]{:S(2)}, u32[]{:S(2)}) collective-permute-start(bf16[4,2,64,128]{3,2,1,0:T(8,128)(2,1)S(1)} %collective-permute-done.14.refs_2_), channel_id=1, source_target_pairs={{0,1},{1,0},{2,3},{3,2},{4,5},{5,4},{6,7},{7,6},{8,9},{9,8},{10,11... | collective-permute-start | bytes 393224 | tf_op jit(solution)/shard_map/ppermute | solution.py:332
